TPU v7x, 256 devices: a whole 4x4x8 slice. The times are simulated.
256 devices in a mesh: band: 8 (over x, z_hi), grid: 32 (over z_lo, y, core).
Axes of the slice: x: 4, y: 4, z: 8 (z_hi: 2, z_lo: 4; z = z_hi * 4 + z_lo), core: 2. Of those that a mesh axis runs over, the one named last changes fastest.
Arguments:
- orbitals: float32 [64, 128, 16384], P('band', 'grid'), may hold values from -6 to 6
- plan: int32 [2, 8, 2], replicated, may hold values from 0 to 1
Outputs:
- exchange: float32 [64, 128, 16384], P('band', 'grid')
All inputs are finite; a program needn't handle non-finite values.
Results may differ from a plain program's by a relative error of at most 0.0003.
Values sent between devices are 32-bit elements; how exact they have to be, the bound alone decides.
No kernel may reach another device: no remote copies, remote signals or barrier semaphores. Data moves between devices by JAX's collectives and lax.ppermute only.
A program may use at most 128 MiB of HBM per device.

v0:
```python
import math

import jax
import jax.numpy as jnp
from jax import lax
from jax.sharding import PartitionSpec as P

GRID = 128
SUB = 4
NSUB = 2
ROUNDS = 2


def from_behind(value, axis, steps):
    count = lax.axis_size(axis)
    pairs = [(source, (source + steps) % count) for source in range(count)]
    return lax.ppermute(value, axis, pairs)


def cas_table(count):
    index = jnp.arange(count, dtype=jnp.int32)
    product = index[:, None] * index[None, :] % count
    angle = product.astype(jnp.float32) * (2.0 * math.pi / count)
    return jnp.cos(angle) + jnp.sin(angle)


def laplace_roots(count):
    freq = jnp.arange(count, dtype=jnp.float32)
    return 2.0 - 2.0 * jnp.cos(freq * (2.0 * math.pi / count))


def pick_index(stack, which):
    return lax.dynamic_index_in_dim(stack, which, 0, False)


def add_index(stack, which, terms):
    current = lax.dynamic_index_in_dim(stack, which, 0, False)
    return lax.dynamic_update_index_in_dim(stack, current + terms, which, 0)


def body(orbitals, plan):
    highest = lax.Precision.HIGHEST
    band_count = lax.axis_size("band")
    band_me = lax.axis_index("band")
    grid_count = lax.axis_size("grid")
    grid_me = lax.axis_index("grid")
    planes = orbitals.shape[1]
    lines = GRID // grid_count
    blocks = orbitals.reshape(NSUB, SUB, planes, GRID, GRID)
    cas = cas_table(GRID)
    roots = laplace_roots(GRID)
    line_start = grid_me * lines
    roots_local = lax.dynamic_slice_in_dim(roots, line_start, lines)
    screen = (4.0 * math.pi / GRID) ** 2
    kern = 1.0 / (screen + roots[:, None, None] + roots_local[None, :, None] + roots[None, None, :])
    whole_index = jnp.arange(GRID, dtype=jnp.int32)
    line_index = line_start + jnp.arange(lines, dtype=jnp.int32)
    anchor = (
        (whole_index[:, None, None] == 0)
        & (line_index[None, :, None] == 0)
        & (whole_index[None, None, :] == 0)
    )
    kern = jnp.where(anchor, jnp.zeros_like(kern), kern)
    norm_factor = 1.0 / float(GRID) ** 3

    def transform_planes(field):
        inner = jnp.einsum("bxyz,zk->bxyk", field, cas, precision=highest)
        return jnp.einsum("bxyk,yj->bxjk", inner, cas, precision=highest)

    pieces = []
    for step in range(ROUNDS):
        offset = (step + 1) % band_count
        first = plan[step, band_me, 0]
        second = plan[step, band_me, 1]
        later = (band_me + step + 1) % band_count
        later_second = plan[step, later, 1]
        own = pick_index(blocks, first)
        received = from_behind(blocks, "band", offset)
        partner = pick_index(received, second)
        pieces.append((offset, first, later_second, own, partner))
    potentials = []
    for offset, first, later_second, own, partner in pieces:
        density = (own[:, None] * partner[None, :]).reshape(SUB * SUB, planes, GRID, GRID)
        solve_spectra = transform_planes(density)
        along = jnp.einsum(
            "bxyk,xi->biyk",
            lax.all_to_all(solve_spectra, "grid", split_axis=2, concat_axis=1, tiled=True),
            cas,
            precision=highest,
        )
        along = along * kern[None]
        screened = lax.all_to_all(
            jnp.einsum("biyk,ix->bxyk", along, cas, precision=highest),
            "grid",
            split_axis=1,
            concat_axis=2,
            tiled=True,
        )
        potentials.append(
            (transform_planes(screened) * norm_factor).reshape(SUB, SUB, planes, GRID, GRID)
        )
    total = jnp.zeros_like(blocks)
    for step in range(ROUNDS):
        offset, first, later_second, own, partner = pieces[step]
        potential = potentials[step]
        own_terms = -jnp.sum(potential * partner[None, :], axis=1)
        partner_terms = -jnp.sum(potential * own[:, None], axis=0)
        returned = from_behind(partner_terms, "band", -offset)
        total = add_index(total, first, own_terms)
        total = add_index(total, later_second, returned)
    return total.reshape(NSUB * SUB, planes, GRID * GRID)


def solution(mesh):
    in_specs = (P("band", "grid", None), P())
    out_specs = P("band", "grid", None)
    return jax.shard_map(body, mesh=mesh, in_specs=in_specs, out_specs=out_specs, check_vma=False)
```

profile of v0, /device:TPU:243, one launch (start us, length us, event | category | flops | bytes accessed | tf_op | source)
XLA Modules:
  0.0 627.8 jit_solution(11185289491770547988)
XLA Ops:
  0.0 2.7 reshape.138
  2.7 1.3 collective-permute-start.2
  4.0 0.6 constant_dynamic-slice_fusion.6
  9.9 1.2 dynamic-slice_bitcast_fusion.1
  11.0 38.4 %collective-permute-done.2 = f32[2,4,4,128,128]{4,3,2,1,0:T(8,128)} collective-permute-done((f32[2,4,4,128,128]{4,3,2,1,0:T(8,128)S(1)}, f32[2,4,4,128,128]{4,3,2,1,0:T(8,128)}, u32[]{:S(2)}, u32[]{:S(2)}) %collective-permute-start.2) | collective-permute-done | bytes 2097184 | tf_op jit(solution)/shard_map/ppermute | solution.py:17
  49.4 1.3 dynamic-slice_bitcast_fusion
  50.7 0.5 broadcast_multiply_fusion
  51.2 3.8 fusion.27
  55.1 4.3 convolution_bitcast_fusion
  59.4 4.7 copy.30
  64.1 9.0 %all-to-all-start.2 = ((f32[16,4,128,128]{3,1,0,2:T(4,128)}), f32[16,4,128,128]{3,1,0,2:T(4,128)}, u32[]{:S(2)}, u32[]{:S(2)}) async-start(f32[16,4,128,128]{3,1,0,2:T(4,128)} %copy.30), calls=%async_computation.2 | async-start | bytes 8388608 | tf_op jit(solution)/shard_map/all_to_all | solution.py:87
  73.0 2.5 collective-permute-start
  77.4 156.2 %collective-permute-done = f32[2,4,4,128,128]{4,3,2,1,0:T(8,128)} collective-permute-done((f32[2,4,4,128,128]{4,3,2,1,0:T(8,128)}, f32[2,4,4,128,128]{4,3,2,1,0:T(8,128)}, u32[]{:S(2)}, u32[]{:S(2)}) %collective-permute-start) | collective-permute-done | bytes 2097184 | tf_op jit(solution)/shard_map/ppermute | solution.py:17
  233.6 1.3 dynamic-slice_bitcast_fusion.2
  234.9 1.7 broadcast_multiply_fusion.1
  236.6 3.8 fusion.30
  240.5 4.3 convolution_bitcast_fusion.1
  244.8 4.7 copy.20
  249.4 5.5 all-to-all-done.2
  254.9 8.0 %all-to-all-start = ((f32[16,4,128,128]{3,1,0,2:T(4,128)}), f32[16,4,128,128]{3,1,0,2:T(4,128)}, u32[]{:S(2)}, u32[]{:S(2)}) async-start(f32[16,4,128,128]{3,1,0,2:T(4,128)} %copy.20), calls=%async_computation | async-start | bytes 8388608 | tf_op jit(solution)/shard_map/all_to_all | solution.py:87
  263.0 0.1 dynamic_slice.48
  263.2 0.1 broadcast_and_fusion
  263.2 0.1 broadcast_add_fusion
  263.3 0.2 divide_select_fusion
  263.5 2.5 copy.31
  266.1 0.6 copy.32
  266.7 6.7 %fusion.6 = f32[128,16,4,128]{3,0,2,1:T(8,128)S(1)} fusion(f32[16,128,4,128]{3,0,2,1:T(8,128)S(1)} %bitcast.123), kind=kOutput, calls=%fused_computation.6 | convolution fusion | flops 1610858496 | bytes 8388608 | tf_op jit(solution)/shard_map/bxyk,xi->biyk/dot_general | solution.py:85
  273.4 4.4 fusion.17
  277.8 5.0 copy.34
  282.9 71.9 %all-to-all-done = f32[16,4,128,128]{3,1,0,2:T(4,128)} async-done(((f32[16,4,128,128]{3,1,0,2:T(4,128)}), f32[16,4,128,128]{3,1,0,2:T(4,128)}, u32[]{:S(2)}, u32[]{:S(2)}) %all-to-all-start) | async-done | bytes 4194336 | tf_op jit(solution)/shard_map/all_to_all | solution.py:87
  354.8 7.9 %all-to-all-start.3 = ((f32[16,128,4,128]{3,2,0,1:T(4,128)}), f32[16,128,4,128]{3,2,0,1:T(4,128)}, u32[]{:S(2)}, u32[]{:S(2)}) async-start(f32[16,128,4,128]{3,2,0,1:T(4,128)} %copy.34), calls=%async_computation.3 | async-start | bytes 8388608 | tf_op jit(solution)/shard_map/all_to_all | solution.py:92
  362.6 2.5 copy.21
  365.2 0.6 copy.22
  365.8 6.7 %fusion.10 = f32[128,16,4,128]{3,0,2,1:T(8,128)S(1)} fusion(f32[16,128,4,128]{3,0,2,1:T(8,128)S(1)} %bitcast.125), kind=kOutput, calls=%fused_computation.10 | convolution fusion | flops 1610858496 | bytes 8388608 | tf_op jit(solution)/shard_map/bxyk,xi->biyk/dot_general | solution.py:85
  372.5 4.4 fusion.14
  377.0 4.9 copy.24
  381.8 72.8 %all-to-all-done.3 = f32[16,128,4,128]{3,2,0,1:T(4,128)} async-done(((f32[16,128,4,128]{3,2,0,1:T(4,128)}), f32[16,128,4,128]{3,2,0,1:T(4,128)}, u32[]{:S(2)}, u32[]{:S(2)}) %all-to-all-start.3) | async-done | bytes 4194336 | tf_op jit(solution)/shard_map/all_to_all | solution.py:92
  454.6 7.9 %all-to-all-start.1 = ((f32[16,128,4,128]{3,2,0,1:T(4,128)}), f32[16,128,4,128]{3,2,0,1:T(4,128)}, u32[]{:S(2)}, u32[]{:S(2)}) async-start(f32[16,128,4,128]{3,2,0,1:T(4,128)} %copy.24), calls=%async_computation.1 | async-start | bytes 8388608 | tf_op jit(solution)/shard_map/all_to_all | solution.py:92
  466.2 2.7 copy.35
  468.9 2.3 copy.36
  471.1 83.3 %all-to-all-done.1 = f32[16,128,4,128]{3,2,0,1:T(4,128)} async-done(((f32[16,128,4,128]{3,2,0,1:T(4,128)}), f32[16,128,4,128]{3,2,0,1:T(4,128)}, u32[]{:S(2)}, u32[]{:S(2)}) %all-to-all-start.1) | async-done | bytes 4194336 | tf_op jit(solution)/shard_map/all_to_all | solution.py:92
  554.5 2.7 copy.25
  557.1 0.6 copy.26
  557.7 4.7 fusion.8
  562.4 4.5 multiply_reduce_fusion.3
  567.0 0.6 multiply_reduce_fusion.2
  567.6 0.1 neg.34
  567.7 1.5 collective-permute-start.1
  569.1 0.0 copy-done
  569.2 4.7 fusion.4
  573.9 4.5 multiply_reduce_fusion.1
  578.4 0.6 multiply_reduce_fusion
  579.0 0.1 neg.37
  579.1 1.5 collective-permute-start.3
  580.7 0.2 broadcast_in_dim.12
  580.9 0.1 bitcast_dynamic-update-slice_fusion.2
  581.0 0.1 constant_dynamic-slice_fusion.2
  581.1 37.4 %collective-permute-done.1 = f32[4,4,128,128]{3,2,1,0:T(8,128)S(1)} collective-permute-done((f32[4,4,128,128]{3,2,1,0:T(8,128)S(1)}, f32[4,4,128,128]{3,2,1,0:T(8,128)S(1)}, u32[]{:S(2)}, u32[]{:S(2)}) %collective-permute-start.1) | collective-permute-done | bytes 1048608 | tf_op jit(solution)/shard_map/ppermute | solution.py:17
  618.5 0.1 bitcast_dynamic-update-slice_fusion.1
  618.6 0.2 fusion.22
  618.9 0.1 constant_dynamic-slice_fusion
  619.0 6.4 %collective-permute-done.3 = f32[4,4,128,128]{3,2,1,0:T(8,128)S(1)} collective-permute-done((f32[4,4,128,128]{3,2,1,0:T(8,128)S(1)}, f32[4,4,128,128]{3,2,1,0:T(8,128)S(1)}, u32[]{:S(2)}, u32[]{:S(2)}) %collective-permute-start.3) | collective-permute-done | bytes 1048608 | tf_op jit(solution)/shard_map/ppermute | solution.py:17
  625.4 0.1 bitcast_dynamic-update-slice_fusion
  625.5 1.9 reshape.141
  (11 shorter events, 0.1 us)
Async XLA Ops:
  0.0 4.0 copy-start.3
  2.7 8.3 %copy-start.2 = (f32[2,4,4,128,128]{4,3,2,1,0:T(8,128)}, f32[2,4,4,128,128]{4,3,2,1,0:T(8,128)S(1)}, u32[]{:S(2)}) copy-start(f32[2,4,4,128,128]{4,3,2,1,0:T(8,128)S(1)} %reshape.138) | copy-start | bytes 6291460
  2.7 46.7 %collective-permute-start.2 = (f32[2,4,4,128,128]{4,3,2,1,0:T(8,128)S(1)}, f32[2,4,4,128,128]{4,3,2,1,0:T(8,128)}, u32[]{:S(2)}, u32[]{:S(2)}) collective-permute-start(f32[2,4,4,128,128]{4,3,2,1,0:T(8,128)S(1)} %reshape.138), channel_id=1, source_target_pairs={{0,64},{32,96},{64,128},{96,160},{128,192},{160,224},{192,0},{224,... | collective-permute-start | bytes 6291464 | tf_op jit(solution)/shard_map/ppermute | solution.py:17
  64.1 190.8 %all-to-all-start.2 = ((f32[16,4,128,128]{3,1,0,2:T(4,128)}), f32[16,4,128,128]{3,1,0,2:T(4,128)}, u32[]{:S(2)}, u32[]{:S(2)}) async-start(f32[16,4,128,128]{3,1,0,2:T(4,128)} %copy.30), calls=%async_computation.2 | async-start | bytes 8388608 | tf_op jit(solution)/shard_map/all_to_all | solution.py:87
  73.0 160.5 %collective-permute-start = (f32[2,4,4,128,128]{4,3,2,1,0:T(8,128)}, f32[2,4,4,128,128]{4,3,2,1,0:T(8,128)}, u32[]{:S(2)}, u32[]{:S(2)}) collective-permute-start(f32[2,4,4,128,128]{4,3,2,1,0:T(8,128)} %copy-done.2), channel_id=1, source_target_pairs={{0,32},{32,64},{64,96},{96,128},{128,160},{160,192},{192,224},{224... | collective-permute-start | bytes 6291464 | tf_op jit(solution)/shard_map/ppermute | solution.py:17
  254.9 99.9 %all-to-all-start = ((f32[16,4,128,128]{3,1,0,2:T(4,128)}), f32[16,4,128,128]{3,1,0,2:T(4,128)}, u32[]{:S(2)}, u32[]{:S(2)}) async-start(f32[16,4,128,128]{3,1,0,2:T(4,128)} %copy.20), calls=%async_computation | async-start | bytes 8388608 | tf_op jit(solution)/shard_map/all_to_all | solution.py:87
  354.8 99.9 %all-to-all-start.3 = ((f32[16,128,4,128]{3,2,0,1:T(4,128)}), f32[16,128,4,128]{3,2,0,1:T(4,128)}, u32[]{:S(2)}, u32[]{:S(2)}) async-start(f32[16,128,4,128]{3,2,0,1:T(4,128)} %copy.34), calls=%async_computation.3 | async-start | bytes 8388608 | tf_op jit(solution)/shard_map/all_to_all | solution.py:92
  454.6 99.9 %all-to-all-start.1 = ((f32[16,128,4,128]{3,2,0,1:T(4,128)}), f32[16,128,4,128]{3,2,0,1:T(4,128)}, u32[]{:S(2)}, u32[]{:S(2)}) async-start(f32[16,128,4,128]{3,2,0,1:T(4,128)} %copy.24), calls=%async_computation.1 | async-start | bytes 8388608 | tf_op jit(solution)/shard_map/all_to_all | solution.py:92
  562.4 4.5 copy-start.1
  567.0 2.2 copy-start
  567.7 50.8 %collective-permute-start.1 = (f32[4,4,128,128]{3,2,1,0:T(8,128)S(1)}, f32[4,4,128,128]{3,2,1,0:T(8,128)S(1)}, u32[]{:S(2)}, u32[]{:S(2)}) collective-permute-start(f32[4,4,128,128]{3,2,1,0:T(8,128)S(1)} %neg.34), channel_id=1, source_target_pairs={{0,224},{32,0},{64,32},{96,64},{128,96},{160,128},{192,160},{224,1... | collective-permute-start | bytes 3145736 | tf_op jit(solution)/shard_map/ppermute | solution.py:17
  579.1 46.3 %collective-permute-start.3 = (f32[4,4,128,128]{3,2,1,0:T(8,128)S(1)}, f32[4,4,128,128]{3,2,1,0:T(8,128)S(1)}, u32[]{:S(2)}, u32[]{:S(2)}) collective-permute-start(f32[4,4,128,128]{3,2,1,0:T(8,128)S(1)} %neg.37), channel_id=1, source_target_pairs={{0,192},{32,224},{64,0},{96,32},{128,64},{160,96},{192,128},{224,1... | collective-permute-start | bytes 3145736 | tf_op jit(solution)/shard_map/ppermute | solution.py:17
where the time goes:
time: 638 us; the launch traced here: 628 us
  waiting for transfers between devices  472 us (74%)
  matrix products  57.1 us (9%)
  local copies, waits for them, and re-layouts  43.1 us (7%)
  starting transfers between devices  39.5 us (6%)
  between operations  11.5 us (2%)
    ppermute x4, waiting for transfers between devices, from_behind(): return lax.ppermute(value, axis, pairs)  238 us
    all_to_all x2, waiting for transfers between devices, body(): lax.all_to_all(jnp.einsum('biyk,ix->bxyk', along, cas, precision=highest)...  156 us
    all_to_all x2, waiting for transfers between devices, body(): lax.all_to_all(solve_spectra, 'grid', split_axis=2, concat_axis=1, tiled=...  77.4 us
    dot_general x4, matrix products, transform_planes(): return jnp.einsum('bxyk,yj->bxjk', inner, cas, precision=highest)  17.6 us
    dot_general x4, matrix products, transform_planes(): inner = jnp.einsum('bxyz,zk->bxyk', field, cas, precision=highest)  17.1 us
    all_to_all x2, starting transfers between devices, body(): lax.all_to_all(solve_spectra, 'grid', split_axis=2, concat_axis=1, tiled=...  17 us
    all_to_all x2, starting transfers between devices, body(): lax.all_to_all(jnp.einsum('biyk,ix->bxyk', along, cas, precision=highest)...  15.7 us
    dot_general x2, matrix products, body(): jnp.einsum('bxyk,xi->biyk', lax.all_to_all(solve_spectra, 'grid', split_a...  13.5 us
  transfers between devices with their start and end apart: 8, of which 8 were waited for; matrix products, arithmetic and copies ran while one was open for 12% of the time, Pallas kernels for 0%

commit v1 on v0

v1 whole, which is shorter than its diff:
```python
import functools
import math

import jax
import jax.numpy as jnp
import ml_dtypes
import numpy as np
from jax import lax
from jax.experimental import pallas as pl
from jax.experimental.pallas import tpu as pltpu
from jax.sharding import PartitionSpec as P

GRID = 128
SUB = 4
NSUB = 2
ROUNDS = 2
CORES = 2
YS = 4
ZS = 4
PLANES = 4
ROWS = GRID * PLANES
HALF = SUB // CORES
QUARTER = GRID // YS
CHUNKS = ((0, (0,)), (1, (0, 1)), (0, (1,)))
F32 = jnp.float32
BF16 = jnp.bfloat16


@functools.cache
def tables():
    index = np.arange(GRID, dtype=np.int64)
    angle = (index[:, None] * index[None, :] % GRID) * (2.0 * math.pi / GRID)
    cas = (np.cos(angle) + np.sin(angle)).astype(np.float32)
    high = cas.astype(ml_dtypes.bfloat16)
    low = (cas - high.astype(np.float32)).astype(ml_dtypes.bfloat16)
    zero = np.zeros_like(high)
    right = np.block([[high, low], [high, zero]])
    left = np.block([[high, high], [low, zero]])
    roots = 2.0 - 2.0 * np.cos(index * (2.0 * math.pi / GRID))
    screen = (4.0 * math.pi / GRID) ** 2
    shift = screen + roots[:, None] + roots[None, :]
    spread = np.sqrt(shift + shift * shift / 4.0)
    decay = 1.0 / (1.0 + shift / 2.0 + spread)
    scale = 1.0 / (2.0 * spread * GRID**2)
    mean = np.zeros((1, GRID))
    mean[0, 0] = 2.0 * spread[0, 0] / (GRID * screen)
    chips = np.stack([decay ** (8 * k) for k in range(YS)])
    runs = np.stack([decay**32, decay**64, 1.0 / (1.0 - decay**GRID)])
    as32 = lambda value: np.asarray(value, dtype=np.float32)
    return right, left, as32(decay), as32(scale), as32(mean), as32(chips), as32(runs)


def split(value):
    high = value.astype(BF16)
    low = (value - high.astype(F32)).astype(BF16)
    return high, low


def times_right(value, table):
    full = jnp.dot(jnp.concatenate(split(value), axis=1), table, preferred_element_type=F32)
    return full[:, :GRID] + full[:, GRID:]


def times_left(value, table):
    full = jnp.dot(table, jnp.concatenate(split(value), axis=0), preferred_element_type=F32)
    return full[:GRID] + full[GRID:]


def place():
    spot = lax.axis_index("grid")
    return spot // (YS * CORES), (spot // CORES) % YS, spot % CORES


def quarter_of(which):
    return pl.ds(pl.multiple_of(which * QUARTER, QUARTER), QUARTER)


def pick_kernel(plan, orbitals, index, *rest):
    outs, sems = rest[:-1], rest[-1]
    band_count = lax.axis_size("band")
    band_me = lax.axis_index("band")
    core = place()[2]
    copies = []
    for step in range(ROUNDS):
        later = plan[step, (band_me + step + 1) % band_count, 1] * SUB
        index[step] = plan[step, band_me, 0] * SUB
        index[ROUNDS + step] = later
        for cross in range(2):
            target = core if cross == 0 else 1 - core
            for j in range(HALF):
                number = len(copies)
                copy = pltpu.make_async_copy(
                    orbitals.at[pl.ds(later + target * HALF + j, 1)], outs[number], sems.at[number]
                )
                copy.start()
                copies.append(copy)
    for copy in copies:
        copy.wait()


def pick(plan, orbitals):
    count = ROUNDS * 2 * HALF
    hbm = pl.BlockSpec(memory_space=pl.ANY)
    smem = pl.BlockSpec(memory_space=pltpu.SMEM)
    outs = pl.pallas_call(
        pick_kernel,
        in_specs=[smem, hbm],
        out_specs=[smem] + [hbm] * count,
        out_shape=[jax.ShapeDtypeStruct((2 * ROUNDS,), jnp.int32)]
        + [jax.ShapeDtypeStruct((1, ROWS, GRID), F32)] * count,
        scratch_shapes=[pltpu.SemaphoreType.DMA((count,))],
        compiler_params=pltpu.CompilerParams(vmem_limit_bytes=2 << 20),
        name="pick",
    )(plan, orbitals)
    index, blocks = outs[0], outs[1:]
    sends = {}
    for step in range(ROUNDS):
        for cross in range(2):
            for j in range(HALF):
                sends[step, cross, j] = blocks[(step * 2 + cross) * HALF + j]
    return index, sends


def forward_kernel(pairs, index, own_a, own_b, part_a, part_b, right, left, decay, scale, spec, *rest):
    outs, lines = rest[:YS], rest[YS]
    _, y, core = place()
    pair = pl.program_id(0) * SUB + pl.program_id(1)
    for source, (own, part) in enumerate(((own_a, part_a), (own_b, part_b))):
        lines[...] = times_right(own[0] * part[0], right[...])
        half = (core if source == 0 else 1 - core) * PLANES
        for x in range(0, PLANES, 2):
            two = jnp.concatenate(
                [lines[pl.ds(x + k, GRID, stride=PLANES), :] for k in range(2)], axis=1
            )
            two = times_left(two, left[...])
            for k in range(2):
                spec[0, half + x + k] = two[:, k * GRID : (k + 1) * GRID] * scale[...]
    total = spec[0, 0, 0:1, :]
    for x in range(1, 2 * PLANES):
        total = total + spec[0, x, 0:1, :]
    base = pl.multiple_of(pair * (2 * QUARTER), 2 * QUARTER)
    for d in range(YS):
        rows = quarter_of((y + d) % YS)
        ratio = decay[rows, :]
        planes = [spec[0, x, rows, :] for x in range(2 * PLANES)]
        ahead, behind = planes[0], planes[-1]
        for x in range(1, 2 * PLANES):
            ahead = planes[x] + ratio * ahead
            behind = planes[-1 - x] + ratio * behind
        outs[d][pl.ds(base, QUARTER), :] = ahead
        outs[d][pl.ds(base + QUARTER, QUARTER), :] = behind

        @pl.when(pair == 0)
        def _():
            outs[d][pl.ds(pairs * 2 * QUARTER, 8), :] = jnp.zeros((8, GRID), F32)

        outs[d][pl.ds(pairs * 2 * QUARTER + pair, 1), :] = total


def own_spec(step):
    return pl.BlockSpec((1, ROWS, GRID), lambda j, i, index: (index[step] + i, 0, 0))


def whole(shape):
    return pl.BlockSpec(shape, lambda *_: (0,) * len(shape))


def forward(step, count, index, own, part):
    right, left, decay, scale = tables()[:4]
    pairs = count * SUB
    message = (pairs * 2 * QUARTER + 8, GRID)
    band = pl.BlockSpec((1, ROWS, GRID), lambda j, i, index: (j, 0, 0))
    outs = pl.pallas_call(
        functools.partial(forward_kernel, pairs),
        grid_spec=pltpu.PrefetchScalarGridSpec(
            num_scalar_prefetch=1,
            grid=(count, SUB),
            in_specs=[own_spec(step)] * 2
            + [band] * 2
            + [whole((2 * GRID, 2 * GRID))] * 2
            + [whole((GRID, GRID))] * 2,
            out_specs=[
                pl.BlockSpec((1, 2 * PLANES, GRID, GRID), lambda j, i, index: (j * SUB + i, 0, 0, 0))
            ]
            + [whole(message)] * YS,
            scratch_shapes=[pltpu.VMEM((ROWS, GRID), F32)],
        ),
        out_shape=[jax.ShapeDtypeStruct((pairs, 2 * PLANES, GRID, GRID), F32)]
        + [jax.ShapeDtypeStruct(message, F32)] * YS,
        compiler_params=pltpu.CompilerParams(vmem_limit_bytes=16 << 20),
        cost_estimate=pl.CostEstimate(
            flops=pairs * 2048 * 2 * 65536, bytes_accessed=pairs << 20, transcendentals=0
        ),
        name="forward",
    )(index, own[0], own[1], part[0], part[1], right, left, decay, scale)
    return outs[0], outs[1:]


def run_kernel(pairs, a, b, c, d, chips, out):
    _, y, _ = place()
    rows = quarter_of(y)
    got = (a, b, c, d)
    from_chip = [(y - k + YS) % YS for k in range(YS)]
    ahead = [chips[YS - 1 - chip, rows, :] for chip in from_chip]
    behind = [chips[chip, rows, :] for chip in from_chip]
    for pair in range(pairs):
        base = pair * 2 * QUARTER
        for weights, start in ((ahead, base), (behind, base + QUARTER)):
            at = slice(start, start + QUARTER)
            out[at, :] = sum(got[k][at, :] * weights[k] for k in range(YS))
    at = slice(pairs * 2 * QUARTER, pairs * 2 * QUARTER + 8)
    out[at, :] = sum(got[k][at, :] for k in range(YS))


def two_kernel(pairs, mine, other, runs, out):
    z, y, _ = place()
    power = runs[0, quarter_of(y), :]
    odd = (jnp.zeros(power.shape, jnp.int32) + z % 2) == 1
    ones = jnp.ones_like(power)
    first = jnp.where(odd, ones, power)
    second = jnp.where(odd, power, ones)
    for pair in range(pairs):
        base = pair * 2 * QUARTER
        at = slice(base, base + QUARTER)
        out[at, :] = mine[at, :] * first + other[at, :] * second
        at = slice(base + QUARTER, base + 2 * QUARTER)
        out[at, :] = mine[at, :] * second + other[at, :] * first
    at = slice(pairs * 2 * QUARTER, pairs * 2 * QUARTER + 8)
    out[at, :] = mine[at, :] + other[at, :]


def edges_kernel(pairs, a, b, c, d, near, mine, other, chips, runs, *rest):
    outs, held = rest[:YS], rest[YS]
    z, y, _ = place()
    rows = quarter_of(y)
    got = (a, b, c, d)
    step, run, two, wrap = chips[1, rows, :], runs[0, rows, :], runs[1, rows, :], runs[2, rows, :]
    odd = (jnp.zeros(step.shape, jnp.int32) + z % 2) == 1
    for k in range(YS):
        held[(y - k + YS) % YS] = got[k][...]
    for pair in range(pairs):
        base = pair * 2 * QUARTER
        ahead = slice(base, base + QUARTER)
        behind = slice(base + QUARTER, base + 2 * QUARTER)
        from_left = (other[ahead, :] + two * mine[ahead, :]) * wrap
        from_right = (other[behind, :] + two * mine[behind, :]) * wrap
        from_left = jnp.where(odd, near[ahead, :] + run * from_left, from_left)
        from_right = jnp.where(odd, from_right, near[behind, :] + run * from_right)
        for chip in range(YS):
            chip_ahead = held[chip, ahead, :]
            held[chip, ahead, :] = from_left
            from_left = chip_ahead + step * from_left
        for chip in reversed(range(YS)):
            chip_behind = held[chip, behind, :]
            held[chip, behind, :] = from_right
            from_right = chip_behind + step * from_right
    at = slice(pairs * 2 * QUARTER, pairs * 2 * QUARTER + 8)
    total = mine[at, :] + other[at, :]
    for k in range(YS):
        outs[k][...] = held[(y - k + YS) % YS]
        outs[k][at, :] = total


def small_call(kernel, pairs, args, count, name, scratch=()):
    shape = args[0].shape
    outs = pl.pallas_call(
        functools.partial(kernel, pairs),
        in_specs=[pl.BlockSpec(memory_space=pltpu.VMEM)] * len(args),
        out_specs=[pl.BlockSpec(memory_space=pltpu.VMEM)] * count,
        out_shape=[jax.ShapeDtypeStruct(shape, F32)] * count,
        scratch_shapes=scratch,
        compiler_params=pltpu.CompilerParams(vmem_limit_bytes=8 << 20),
        cost_estimate=pl.CostEstimate(
            flops=8 * args[0].size, bytes_accessed=4 * args[0].size * (len(args) + count), transcendentals=0
        ),
        name=name,
    )(*args)
    return outs


def backward_kernel(
    pairs, index, spec, a, b, c, d, own_a, own_b, part_a, part_b, right, left, decay, mean,
    part_out_a, part_out_b, own_out_a, own_out_b, field, lines
):
    edges = (a, b, c, d)
    _, y, core = place()
    j, i = pl.program_id(0), pl.program_id(1)
    pair = j * SUB + i
    base = pl.multiple_of(pair * (2 * QUARTER), 2 * QUARTER)
    for k in range(YS):
        rows = quarter_of((y + k) % YS)
        ratio = decay[rows, :]
        planes = [spec[0, x, rows, :] for x in range(2 * PLANES)]
        ahead = edges[k][pl.ds(base, QUARTER), :]
        behind = edges[k][pl.ds(base + QUARTER, QUARTER), :]
        sums = []
        for x in range(2 * PLANES):
            ahead = planes[x] + ratio * ahead
            sums.append(ahead)
        for x in reversed(range(2 * PLANES)):
            behind = ratio * behind
            field[x, rows, :] = sums[x] + behind
            behind = planes[x] + behind
    average = a[pl.ds(pairs * 2 * QUARTER + pair, 1), :] * mean[...]
    for x in range(2 * PLANES):
        field[x, 0:1, :] = field[x, 0:1, :] - average
    for source, (own, part, part_out, own_out) in enumerate(
        ((own_a, part_a, part_out_a, own_out_a), (own_b, part_b, part_out_b, own_out_b))
    ):
        half = (core if source == 0 else 1 - core) * PLANES
        for x in range(0, PLANES, 2):
            two = jnp.concatenate([field[half + x + k] for k in range(2)], axis=1)
            two = times_left(two, left[...])
            for k in range(2):
                lines[pl.ds(x + k, GRID, stride=PLANES), :] = two[:, k * GRID : (k + 1) * GRID]
        potential = times_right(lines[...], right[...])
        to_part = potential * own[0]
        to_own = potential * part[0]

        @pl.when(i == 0)
        def _():
            part_out[0] = -to_part

        @pl.when(i != 0)
        def _():
            part_out[0] = part_out[0] - to_part

        @pl.when(j == 0)
        def _():
            own_out[i] = -to_own

        @pl.when(j != 0)
        def _():
            own_out[i] = own_out[i] - to_own


def backward(step, count, index, spec, edges, own, part):
    right, left, decay, _, mean = tables()[:5]
    pairs = count * SUB
    message = edges[0].shape
    band = pl.BlockSpec((1, ROWS, GRID), lambda j, i, index: (j, 0, 0))
    outs = pl.pallas_call(
        functools.partial(backward_kernel, pairs),
        grid_spec=pltpu.PrefetchScalarGridSpec(
            num_scalar_prefetch=1,
            grid=(count, SUB),
            in_specs=[
                pl.BlockSpec((1, 2 * PLANES, GRID, GRID), lambda j, i, index: (j * SUB + i, 0, 0, 0))
            ]
            + [whole(message)] * YS
            + [own_spec(step)] * 2
            + [band] * 2
            + [whole((2 * GRID, 2 * GRID))] * 2
            + [whole((GRID, GRID)), whole((1, GRID))],
            out_specs=[band] * 2 + [whole((SUB, ROWS, GRID))] * 2,
            scratch_shapes=[pltpu.VMEM((2 * PLANES, GRID, GRID), F32), pltpu.VMEM((ROWS, GRID), F32)],
        ),
        out_shape=[jax.ShapeDtypeStruct((count, ROWS, GRID), F32)] * 2
        + [jax.ShapeDtypeStruct((SUB, ROWS, GRID), F32)] * 2,
        compiler_params=pltpu.CompilerParams(vmem_limit_bytes=20 << 20),
        cost_estimate=pl.CostEstimate(
            flops=pairs * 2048 * 2 * 65536, bytes_accessed=pairs << 20, transcendentals=0
        ),
        name="backward",
    )(index, spec, *edges, own[0], own[1], part[0], part[1], right, left, decay, mean)
    return outs


def total_kernel(kinds, index, *refs):
    terms, out = refs[:-1], refs[-1]
    core = place()[2]
    i = pl.program_id(0)
    sums = [jnp.zeros((ROWS, GRID), F32) for _ in range(NSUB)]
    for (slot, cross, j), ref in zip(kinds, terms):
        base = index[slot]
        for sub in range(NSUB):
            use = base == sub * SUB
            if cross is not None:
                target = core if cross == 0 else 1 - core
                use = use & (i == target * HALF + j)
            sums[sub] = sums[sub] + jnp.where(use, ref[0], 0.0)
    for sub in range(NSUB):
        out[sub, 0] = sums[sub]


def add_up(index, own_terms, part_terms):
    kinds, args, specs = [], [], []
    for step, value in own_terms:
        kinds.append((step, None, None))
        args.append(value)
        specs.append(pl.BlockSpec((1, ROWS, GRID), lambda i, index: (i, 0, 0)))
    for step, cross, j, at, value in part_terms:
        kinds.append((ROUNDS + step, cross, j))
        args.append(value)
        specs.append(pl.BlockSpec((1, ROWS, GRID), lambda i, index, at=at: (at, 0, 0)))
    return pl.pallas_call(
        functools.partial(total_kernel, tuple(kinds)),
        grid_spec=pltpu.PrefetchScalarGridSpec(
            num_scalar_prefetch=1,
            grid=(SUB,),
            in_specs=specs,
            out_specs=pl.BlockSpec((NSUB, 1, ROWS, GRID), lambda i, index: (0, i, 0, 0)),
        ),
        out_shape=jax.ShapeDtypeStruct((NSUB, SUB, ROWS, GRID), F32),
        compiler_params=pltpu.CompilerParams(vmem_limit_bytes=24 << 20),
        name="add_up",
    )(index, *args)


def body(orbitals, plan):
    bands = lax.axis_size("band")
    spots = lax.axis_size("grid")

    def move(value, target):
        pairs = []
        for band in range(bands):
            for spot in range(spots):
                z, y, core = spot // (YS * CORES), (spot // CORES) % YS, spot % CORES
                b2, z2, y2, c2 = target(band, z, y, core)
                pairs.append((band * spots + spot, (b2 % bands) * spots + (z2 * YS + y2 % YS) * CORES + c2))
        return lax.ppermute(value, ("band", "grid"), pairs)

    def swap_cores(value):
        return move(value, lambda b, z, y, c: (b, z, y, 1 - c))

    chips, runs = tables()[5:7]
    blocks = orbitals.reshape(NSUB * SUB, PLANES, GRID, GRID).transpose(0, 2, 1, 3)
    blocks = blocks.reshape(NSUB * SUB, ROWS, GRID)
    index, sends = pick(plan, blocks)
    own = (blocks, swap_cores(blocks))
    got = {}
    for step, members in CHUNKS:
        for j in members:
            for cross in range(2):
                got[step, cross, j] = move(
                    sends[step, cross, j],
                    lambda b, z, y, c, s=step + 1, f=cross: (b + s, z, y, 1 - c if f else c),
                )
    own_terms, part_terms = [], []
    for step, members in CHUNKS:
        count = len(members)
        pairs = count * SUB
        part = [
            jnp.concatenate([got[step, cross, j] for j in members], axis=0) if count > 1 else got[step, cross, members[0]]
            for cross in range(2)
        ]
        spec, sums = forward(step, count, index, own, part)
        sums = [sums[0]] + [
            move(sums[d], lambda b, z, y, c, d=d: (b, z, y + d, c)) for d in range(1, YS)
        ]
        run = small_call(run_kernel, pairs, [*sums, chips], 1, "run")[0]
        near = move(run, lambda b, z, y, c: (b, z ^ 1, y, c))
        two = small_call(two_kernel, pairs, [run, near, runs], 1, "two")[0]
        far = move(two, lambda b, z, y, c: (b, z ^ 2, y, c))
        edges = small_call(
            edges_kernel, pairs, [*sums, near, two, far, chips, runs], YS, "edges",
            [pltpu.VMEM((YS, *run.shape), F32)],
        )
        edges = [edges[0]] + [
            move(edges[d], lambda b, z, y, c, d=d: (b, z, y + YS - d, c)) for d in range(1, YS)
        ]
        part_same, part_cross, own_same, own_cross = backward(step, count, index, spec, edges, own, part)
        for cross, value in ((0, part_same), (1, part_cross)):
            value = move(value, lambda b, z, y, c, s=step + 1, f=cross: (b - s, z, y, 1 - c if f else c))
            for at, j in enumerate(members):
                part_terms.append((step, cross, j, at, value))
        own_terms.append((step, own_same))
        own_terms.append((step, swap_cores(own_cross)))
    total = add_up(index, own_terms, part_terms)
    total = total.reshape(NSUB * SUB, GRID, PLANES, GRID).transpose(0, 2, 1, 3)
    return total.reshape(NSUB * SUB, PLANES, GRID * GRID)


def solution(mesh):
    in_specs = (P("band", "grid", None), P())
    out_specs = P("band", "grid", None)
    return jax.shard_map(body, mesh=mesh, in_specs=in_specs, out_specs=out_specs, check_vma=False)
```

time: 638 us -> 222 us (0.35)
  the two profiles are of different devices: /device:TPU:243 before, /device:TPU:1 now
where the time goes in v1:
time: 222 us; the launch traced here: 221 us
  starting transfers between devices  102 us (46%)
  waiting for transfers between devices  72 us (32%)
  Pallas kernels  43.8 us (20%)
  local copies, waits for them, and re-layouts  2.46 us (1%)
    ppermute x42, starting transfers between devices, move(): return lax.ppermute(value, ('band', 'grid'), pairs)  102 us
    ppermute x42, waiting for transfers between devices, move(): return lax.ppermute(value, ('band', 'grid'), pairs)  72 us
    pallas_call x3, Pallas kernels, backward(): pl.pallas_call(functools.partial(backward_kernel, pairs), grid_spec=pltpu...  22.2 us
    pallas_call x3, Pallas kernels, forward(): pl.pallas_call(functools.partial(forward_kernel, pairs), grid_spec=pltpu....  15.3 us
  transfers between devices with their start and end apart: 42, of which 15 were waited for; matrix products, arithmetic and copies ran while one was open for 0% of the time, Pallas kernels for 18%

profile of v1, /device:TPU:1, one launch (start us, length us, event | category | flops | bytes accessed | tf_op | source)
XLA Modules:
  0.0 220.6 jit_solution(1539282827941629368)
XLA Ops:
  0.0 3.2 %collective-permute-start = (f32[8,512,128]{2,1,0:T(8,128)}, f32[8,512,128]{2,1,0:T(8,128)S(1)}, u32[]{:S(2)}, u32[]{:S(2)}) collective-permute-start(f32[8,512,128]{2,1,0:T(8,128)} %bitcast.10), channel_id=1, source_target_pairs={{0,1},{1,0},{2,3},{3,2},{4,5},{5,4},{6,7},{7,6},{8,9},{9,8},{10,11... | collective-permute-start | bytes 6291464 | tf_op jit(solution)/shard_map/ppermute | solution.py:421
  3.2 0.8 copy.11.plan
  4.0 1.6 copy-done
  5.6 1.5 pick.1
  7.2 0.8 collective-permute-start.14
  8.1 0.9 collective-permute-start.13
  9.0 6.9 %collective-permute-start.25 = (f32[1,512,128]{2,1,0:T(8,128)S(1)}, f32[1,512,128]{2,1,0:T(8,128)S(1)}, u32[]{:S(2)}, u32[]{:S(2)}) collective-permute-start(f32[1,512,128]{2,1,0:T(8,128)S(1)} %get-tuple-element.82), channel_id=1, source_target_pairs={{0,32},{1,33},{2,34},{3,35},{4,36},{5,37},{6,38},{7,39},{8,40},{9,... | collective-permute-start | bytes 786440 | tf_op jit(solution)/shard_map/ppermute | solution.py:421
  15.9 0.5 collective-permute-done.12
  16.4 0.4 collective-permute-start.15
  16.8 11.3 %collective-permute-done.14 = f32[1,512,128]{2,1,0:T(8,128)S(1)} collective-permute-done((f32[1,512,128]{2,1,0:T(8,128)S(1)}, f32[1,512,128]{2,1,0:T(8,128)S(1)}, u32[]{:S(2)}, u32[]{:S(2)}) %collective-permute-start.14) | collective-permute-done | bytes 262176 | tf_op jit(solution)/shard_map/ppermute | solution.py:421
  28.1 5.1 %collective-permute-done.13 = f32[1,512,128]{2,1,0:T(8,128)S(1)} collective-permute-done((f32[1,512,128]{2,1,0:T(8,128)S(1)}, f32[1,512,128]{2,1,0:T(8,128)S(1)}, u32[]{:S(2)}, u32[]{:S(2)}) %collective-permute-start.13) | collective-permute-done | bytes 262176 | tf_op jit(solution)/shard_map/ppermute | solution.py:421
  33.3 6.1 %collective-permute-done.15 = f32[1,512,128]{2,1,0:T(8,128)S(1)} collective-permute-done((f32[1,512,128]{2,1,0:T(8,128)S(1)}, f32[1,512,128]{2,1,0:T(8,128)S(1)}, u32[]{:S(2)}, u32[]{:S(2)}) %collective-permute-start.15) | collective-permute-done | bytes 262176 | tf_op jit(solution)/shard_map/ppermute | solution.py:421
  39.4 7.4 %forward.4 = (f32[8,8,128,128]{3,2,1,0:T(8,128)S(1)}, f32[520,128]{1,0:T(8,128)S(1)}, f32[520,128]{1,0:T(8,128)S(1)}, f32[520,128]{1,0:T(8,128)S(1)}, f32[520,128]{1,0:T(8,128)S(1)}) custom-call(s32[4]{0:T(128)S(1)} %get-tuple-element.53.index, f32[8,512,128]{2,1,0:T(8,128)S(1)} %bitcast.12, f32[8,512,128]{2,1,0:T(8,128)S(1)} %collective-permute-done.own_b, ...), custom_call_target="tpu_custom_call" | custom-call | flops 2147483648 | bytes 8388608 | tf_op jit(solution)/shard_map/forward/pallas_call | solution.py:173
  46.9 2.4 %collective-permute-start.17 = (f32[520,128]{1,0:T(8,128)S(1)}, f32[520,128]{1,0:T(8,128)S(1)}, u32[]{:S(2)}, u32[]{:S(2)}) collective-permute-start(f32[520,128]{1,0:T(8,128)S(1)} %get-tuple-element.74), channel_id=1, source_target_pairs={{0,4},{1,5},{2,6},{3,7},{4,0},{5,1},{6,2},{7,3},{8,12},{9,13},{10,... | collective-permute-start | bytes 798728 | tf_op jit(solution)/shard_map/ppermute | solution.py:421
  49.3 1.1 collective-permute-start.18
  50.3 1.0 collective-permute-start.1
  51.3 5.3 %collective-permute-start.2 = (f32[1,512,128]{2,1,0:T(8,128)S(1)}, f32[1,512,128]{2,1,0:T(8,128)S(1)}, u32[]{:S(2)}, u32[]{:S(2)}) collective-permute-start(f32[1,512,128]{2,1,0:T(8,128)S(1)} %get-tuple-element.55), channel_id=1, source_target_pairs={{0,33},{1,32},{2,35},{3,34},{4,37},{5,36},{6,39},{7,38},{8,41},{9,... | collective-permute-start | bytes 786440 | tf_op jit(solution)/shard_map/ppermute | solution.py:421
  56.6 4.0 %forward.5 = (f32[4,8,128,128]{3,2,1,0:T(8,128)S(1)}, f32[264,128]{1,0:T(8,128)S(1)}, f32[264,128]{1,0:T(8,128)S(1)}, f32[264,128]{1,0:T(8,128)S(1)}, f32[264,128]{1,0:T(8,128)S(1)}) custom-call(s32[4]{0:T(128)S(1)} %get-tuple-element.53.index, f32[8,512,128]{2,1,0:T(8,128)S(1)} %bitcast.13, f32[8,512,128]{2,1,0:T(8,128)S(1)} %collective-permute-done.own_b, ...), custom_call_target="tpu_custom_call" | custom-call | flops 1073741824 | bytes 4194304 | tf_op jit(solution)/shard_map/forward/pallas_call | solution.py:173
  60.6 0.5 collective-permute-start.27
  61.1 0.5 collective-permute-done.17.c
  61.6 0.7 collective-permute-start.28
  62.3 2.8 %collective-permute-start.29 = (f32[264,128]{1,0:T(8,128)S(1)}, f32[264,128]{1,0:T(8,128)S(1)}, u32[]{:S(2)}, u32[]{:S(2)}) collective-permute-start(f32[264,128]{1,0:T(8,128)S(1)} %get-tuple-element.88), channel_id=1, source_target_pairs={{0,6},{1,7},{2,0},{3,1},{4,2},{5,3},{6,4},{7,5},{8,14},{9,15},{10,... | collective-permute-start | bytes 405512 | tf_op jit(solution)/shard_map/ppermute | solution.py:421
  65.1 0.1 run.4.mine
  65.2 11.8 %collective-permute-start.19 = (f32[520,128]{1,0:T(8,128)S(1)}, f32[520,128]{1,0:T(8,128)S(1)}, u32[]{:S(2)}, u32[]{:S(2)}) collective-permute-start(f32[520,128]{1,0:T(8,128)S(1)} %run.4.mine), channel_id=1, source_target_pairs={{0,8},{1,9},{2,10},{3,11},{4,12},{5,13},{6,14},{7,15},{8,0},{9,1},... | collective-permute-start | bytes 798728 | tf_op jit(solution)/shard_map/ppermute | solution.py:421
  77.0 4.5 %collective-permute-done.2.part_b = f32[1,512,128]{2,1,0:T(8,128)S(1)} collective-permute-done((f32[1,512,128]{2,1,0:T(8,128)S(1)}, f32[1,512,128]{2,1,0:T(8,128)S(1)}, u32[]{:S(2)}, u32[]{:S(2)}) %collective-permute-start.2) | collective-permute-done | bytes 262176 | tf_op jit(solution)/shard_map/ppermute | solution.py:421
  81.5 4.0 %forward.3 = (f32[4,8,128,128]{3,2,1,0:T(8,128)S(1)}, f32[264,128]{1,0:T(8,128)S(1)}, f32[264,128]{1,0:T(8,128)S(1)}, f32[264,128]{1,0:T(8,128)S(1)}, f32[264,128]{1,0:T(8,128)S(1)}) custom-call(s32[4]{0:T(128)S(1)} %get-tuple-element.53.index, f32[8,512,128]{2,1,0:T(8,128)S(1)} %bitcast.14, f32[8,512,128]{2,1,0:T(8,128)S(1)} %collective-permute-done.own_b, ...), custom_call_target="tpu_custom_call" | custom-call | flops 1073741824 | bytes 4194304 | tf_op jit(solution)/shard_map/forward/pallas_call | solution.py:173
  85.5 0.5 collective-permute-start.3
  86.0 2.4 %collective-permute-start.4 = (f32[264,128]{1,0:T(8,128)S(1)}, f32[264,128]{1,0:T(8,128)S(1)}, u32[]{:S(2)}, u32[]{:S(2)}) collective-permute-start(f32[264,128]{1,0:T(8,128)S(1)} %get-tuple-element.59), channel_id=1, source_target_pairs={{0,4},{1,5},{2,6},{3,7},{4,0},{5,1},{6,2},{7,3},{8,12},{9,13},{10,... | collective-permute-start | bytes 405512 | tf_op jit(solution)/shard_map/ppermute | solution.py:421
  88.4 2.0 collective-permute-start.5
  90.4 6.2 %collective-permute-start.30 = (f32[264,128]{1,0:T(8,128)S(1)}, f32[264,128]{1,0:T(8,128)S(1)}, u32[]{:S(2)}, u32[]{:S(2)}) collective-permute-start(f32[264,128]{1,0:T(8,128)S(1)} %run.5.mine), channel_id=1, source_target_pairs={{0,8},{1,9},{2,10},{3,11},{4,12},{5,13},{6,14},{7,15},{8,0},{9,1},... | collective-permute-start | bytes 405512 | tf_op jit(solution)/shard_map/ppermute | solution.py:421
  96.6 5.4 %collective-permute-start.6 = (f32[264,128]{1,0:T(8,128)S(1)}, f32[264,128]{1,0:T(8,128)S(1)}, u32[]{:S(2)}, u32[]{:S(2)}) collective-permute-start(f32[264,128]{1,0:T(8,128)S(1)} %run.3.mine), channel_id=1, source_target_pairs={{0,8},{1,9},{2,10},{3,11},{4,12},{5,13},{6,14},{7,15},{8,0},{9,1},... | collective-permute-start | bytes 405512 | tf_op jit(solution)/shard_map/ppermute | solution.py:421
  102.1 0.1 collective-permute-start.31
  102.3 2.4 %collective-permute-start.20 = (f32[520,128]{1,0:T(8,128)S(1)}, f32[520,128]{1,0:T(8,128)S(1)}, u32[]{:S(2)}, u32[]{:S(2)}) collective-permute-start(f32[520,128]{1,0:T(8,128)S(1)} %two.4.mine), channel_id=1, source_target_pairs={{0,16},{1,17},{2,18},{3,19},{4,20},{5,21},{6,22},{7,23},{8,24},{9,... | collective-permute-start | bytes 798728 | tf_op jit(solution)/shard_map/ppermute | solution.py:421
  104.7 0.8 collective-permute-done.6.other.near
  105.6 14.1 %collective-permute-done.31.other = f32[264,128]{1,0:T(8,128)S(1)} collective-permute-done((f32[264,128]{1,0:T(8,128)S(1)}, f32[264,128]{1,0:T(8,128)S(1)}, u32[]{:S(2)}, u32[]{:S(2)}) %collective-permute-start.31) | collective-permute-done | bytes 135200 | tf_op jit(solution)/shard_map/ppermute | solution.py:421
  119.6 0.2 edges.5
  119.8 2.7 %collective-permute-start.32 = (f32[264,128]{1,0:T(8,128)S(1)}, f32[264,128]{1,0:T(8,128)S(1)}, u32[]{:S(2)}, u32[]{:S(2)}) collective-permute-start(f32[264,128]{1,0:T(8,128)S(1)} %get-tuple-element.90), channel_id=1, source_target_pairs={{0,6},{1,7},{2,0},{3,1},{4,2},{5,3},{6,4},{7,5},{8,14},{9,15},{10,... | collective-permute-start | bytes 405512 | tf_op jit(solution)/shard_map/ppermute | solution.py:421
  122.5 0.7 collective-permute-start.34
  123.2 5.1 %collective-permute-done.7.other = f32[264,128]{1,0:T(8,128)S(1)} collective-permute-done((f32[264,128]{1,0:T(8,128)S(1)}, f32[264,128]{1,0:T(8,128)S(1)}, u32[]{:S(2)}, u32[]{:S(2)}) %collective-permute-start.7) | collective-permute-done | bytes 135200 | tf_op jit(solution)/shard_map/ppermute | solution.py:421
  128.2 0.2 edges.3
  128.4 0.6 collective-permute-start.10
  129.0 0.3 edges.4
  129.3 2.3 %collective-permute-start.21 = (f32[520,128]{1,0:T(8,128)S(1)}, f32[520,128]{1,0:T(8,128)S(1)}, u32[]{:S(2)}, u32[]{:S(2)}) collective-permute-start(f32[520,128]{1,0:T(8,128)S(1)} %get-tuple-element.77), channel_id=1, source_target_pairs={{0,6},{1,7},{2,0},{3,1},{4,2},{5,3},{6,4},{7,5},{8,14},{9,15},{10,... | collective-permute-start | bytes 798728 | tf_op jit(solution)/shard_map/ppermute | solution.py:421
  131.5 1.2 collective-permute-start.22
  132.8 0.8 collective-permute-start.23
  133.5 1.9 collective-permute-start.8
  135.5 0.5 collective-permute-start.9
  136.0 5.6 %backward.5 = (f32[1,512,128]{2,1,0:T(8,128)S(1)}, f32[1,512,128]{2,1,0:T(8,128)S(1)}, f32[4,512,128]{2,1,0:T(8,128)S(1)}, f32[4,512,128]{2,1,0:T(8,128)S(1)}) custom-call(s32[4]{0:T(128)S(1)} %get-tuple-element.53.index, f32[4,8,128,128]{3,2,1,0:T(8,128)S(1)} %get-tuple-element.84.spec, f32[264,128]{1,0:T(8,128)S(1)} %get-tuple-element.89.a, ...), custom_call_target="tpu_custom_call" | custom-call | flops 1073741824 | bytes 4194304 | tf_op jit(solution)/shard_map/backward/pallas_call | solution.py:342
  141.6 4.1 %collective-permute-done.8.b = f32[264,128]{1,0:T(8,128)S(1)} collective-permute-done((f32[264,128]{1,0:T(8,128)S(1)}, f32[264,128]{1,0:T(8,128)S(1)}, u32[]{:S(2)}, u32[]{:S(2)}) %collective-permute-start.8) | collective-permute-done | bytes 135200 | tf_op jit(solution)/shard_map/ppermute | solution.py:421
  145.8 3.9 %collective-permute-start.35 = (f32[4,512,128]{2,1,0:T(8,128)S(1)}, f32[4,512,128]{2,1,0:T(8,128)S(1)}, u32[]{:S(2)}, u32[]{:S(2)}) collective-permute-start(f32[4,512,128]{2,1,0:T(8,128)S(1)} %get-tuple-element.94), channel_id=1, source_target_pairs={{0,1},{1,0},{2,3},{3,2},{4,5},{5,4},{6,7},{7,6},{8,9},{9,8},{10,11... | collective-permute-start | bytes 3145736 | tf_op jit(solution)/shard_map/ppermute | solution.py:421
  149.7 0.3 collective-permute-done.9.c
  149.9 5.6 %backward.3 = (f32[1,512,128]{2,1,0:T(8,128)S(1)}, f32[1,512,128]{2,1,0:T(8,128)S(1)}, f32[4,512,128]{2,1,0:T(8,128)S(1)}, f32[4,512,128]{2,1,0:T(8,128)S(1)}) custom-call(s32[4]{0:T(128)S(1)} %get-tuple-element.53.index, f32[4,8,128,128]{3,2,1,0:T(8,128)S(1)} %get-tuple-element.56.spec, f32[264,128]{1,0:T(8,128)S(1)} %get-tuple-element.61.a, ...), custom_call_target="tpu_custom_call" | custom-call | flops 1073741824 | bytes 4194304 | tf_op jit(solution)/shard_map/backward/pallas_call | solution.py:342
  155.6 3.5 %collective-permute-start.41 = (f32[1,512,128]{2,1,0:T(8,128)S(1)}, f32[1,512,128]{2,1,0:T(8,128)S(1)}, u32[]{:S(2)}, u32[]{:S(2)}) collective-permute-start(f32[1,512,128]{2,1,0:T(8,128)S(1)} %get-tuple-element.100), channel_id=1, source_target_pairs={{0,225},{1,224},{2,227},{3,226},{4,229},{5,228},{6,231},{7,230},{8... | collective-permute-start | bytes 786440 | tf_op jit(solution)/shard_map/ppermute | solution.py:421
  159.1 10.9 %backward.4 = (f32[2,512,128]{2,1,0:T(8,128)S(1)}, f32[2,512,128]{2,1,0:T(8,128)S(1)}, f32[4,512,128]{2,1,0:T(8,128)S(1)}, f32[4,512,128]{2,1,0:T(8,128)S(1)}) custom-call(s32[4]{0:T(128)S(1)} %get-tuple-element.53.index, f32[8,8,128,128]{3,2,1,0:T(8,128)S(1)} %get-tuple-element.71.spec, f32[520,128]{1,0:T(8,128)S(1)} %get-tuple-element.76.a, ...), custom_call_target="tpu_custom_call" | custom-call | flops 2147483648 | bytes 8388608 | tf_op jit(solution)/shard_map/backward/pallas_call | solution.py:342
  170.0 0.6 collective-permute-start.24
  170.6 2.6 %collective-permute-start.36 = (f32[1,512,128]{2,1,0:T(8,128)S(1)}, f32[1,512,128]{2,1,0:T(8,128)S(1)}, u32[]{:S(2)}, u32[]{:S(2)}) collective-permute-start(f32[1,512,128]{2,1,0:T(8,128)S(1)} %get-tuple-element.95), channel_id=1, source_target_pairs={{0,224},{1,225},{2,226},{3,227},{4,228},{5,229},{6,230},{7,231},{8... | collective-permute-start | bytes 786440 | tf_op jit(solution)/shard_map/ppermute | solution.py:421
  173.2 3.0 %collective-permute-done.41.refs_13_ = f32[1,512,128]{2,1,0:T(8,128)S(1)} collective-permute-done((f32[1,512,128]{2,1,0:T(8,128)S(1)}, f32[1,512,128]{2,1,0:T(8,128)S(1)}, u32[]{:S(2)}, u32[]{:S(2)}) %collective-permute-start.41) | collective-permute-done | bytes 262176 | tf_op jit(solution)/shard_map/ppermute | solution.py:421
  176.2 4.6 %collective-permute-start.37 = (f32[1,512,128]{2,1,0:T(8,128)S(1)}, f32[1,512,128]{2,1,0:T(8,128)S(1)}, u32[]{:S(2)}, u32[]{:S(2)}) collective-permute-start(f32[1,512,128]{2,1,0:T(8,128)S(1)} %get-tuple-element.96), channel_id=1, source_target_pairs={{0,225},{1,224},{2,227},{3,226},{4,229},{5,228},{6,231},{7,230},{8... | collective-permute-start | bytes 786440 | tf_op jit(solution)/shard_map/ppermute | solution.py:421
  180.8 0.7 collective-permute-done.36.refs_6_
  181.5 13.4 %collective-permute-start.38 = (f32[2,512,128]{2,1,0:T(8,128)S(1)}, f32[2,512,128]{2,1,0:T(8,128)S(1)}, u32[]{:S(2)}, u32[]{:S(2)}) collective-permute-start(f32[2,512,128]{2,1,0:T(8,128)S(1)} %get-tuple-element.97), channel_id=1, source_target_pairs={{0,192},{1,193},{2,194},{3,195},{4,196},{5,197},{6,198},{7,199},{8... | collective-permute-start | bytes 1572872 | tf_op jit(solution)/shard_map/ppermute | solution.py:421
  194.9 5.9 %collective-permute-start.39 = (f32[2,512,128]{2,1,0:T(8,128)S(1)}, f32[2,512,128]{2,1,0:T(8,128)S(1)}, u32[]{:S(2)}, u32[]{:S(2)}) collective-permute-start(f32[2,512,128]{2,1,0:T(8,128)S(1)} %get-tuple-element.98), channel_id=1, source_target_pairs={{0,193},{1,192},{2,195},{3,194},{4,197},{5,196},{6,199},{7,198},{8... | collective-permute-start | bytes 1572872 | tf_op jit(solution)/shard_map/ppermute | solution.py:421
  200.8 4.8 %collective-permute-done.38.refs_8_.refs_9_ = f32[2,512,128]{2,1,0:T(8,128)S(1)} collective-permute-done((f32[2,512,128]{2,1,0:T(8,128)S(1)}, f32[2,512,128]{2,1,0:T(8,128)S(1)}, u32[]{:S(2)}, u32[]{:S(2)}) %collective-permute-start.38) | collective-permute-done | bytes 524320 | tf_op jit(solution)/shard_map/ppermute | solution.py:421
  205.6 11.2 %collective-permute-done.39.refs_10_.refs_11_ = f32[2,512,128]{2,1,0:T(8,128)S(1)} collective-permute-done((f32[2,512,128]{2,1,0:T(8,128)S(1)}, f32[2,512,128]{2,1,0:T(8,128)S(1)}, u32[]{:S(2)}, u32[]{:S(2)}) %collective-permute-start.39) | collective-permute-done | bytes 524320 | tf_op jit(solution)/shard_map/ppermute | solution.py:421
  216.9 3.8 %add_up.1 = f32[2,4,512,128]{3,2,1,0:T(8,128)} custom-call(s32[4]{0:T(128)S(1)} %get-tuple-element.53.index, f32[4,512,128]{2,1,0:T(8,128)S(1)} %get-tuple-element.65.refs_0_, f32[4,512,128]{2,1,0:T(8,128)S(1)} %collective-permute-done.11.refs_1_, f32[4,512,128]{2,1,0:T(8,128)S(1)} %get-tuple-element.80.refs_2_, ...), custom_call_target="tpu_custom_call" | custom-call | tf_op jit(solution)/shard_map/add_up/pallas_call | solution.py:396
  (60 shorter events, 0.7 us)
Async XLA Ops:
  0.0 39.4 %collective-permute-start = (f32[8,512,128]{2,1,0:T(8,128)}, f32[8,512,128]{2,1,0:T(8,128)S(1)}, u32[]{:S(2)}, u32[]{:S(2)}) collective-permute-start(f32[8,512,128]{2,1,0:T(8,128)} %bitcast.10), channel_id=1, source_target_pairs={{0,1},{1,0},{2,3},{3,2},{4,5},{5,4},{6,7},{7,6},{8,9},{9,8},{10,11... | collective-permute-start | bytes 6291464 | tf_op jit(solution)/shard_map/ppermute | solution.py:421
  4.0 1.6 copy-start
  5.6 33.8 %copy-start.1 = (f32[8,4,16384]{2,1,0:T(4,128)S(1)}, f32[8,4,16384]{2,1,0:T(4,128)}, u32[]{:S(2)}) copy-start(f32[8,4,16384]{2,1,0:T(4,128)} %param.9) | copy-start | bytes 6291460
  5.6 33.8 %copy-start.4 = (bf16[256,256]{1,0:T(8,128)(2,1)S(1)}, bf16[256,256]{1,0:T(8,128)(2,1)}, u32[]{:S(2)}) copy-start(bf16[256,256]{1,0:T(8,128)(2,1)} %constant.14.clone.right) | copy-start | bytes 393220
  5.6 33.8 %copy-start.5 = (bf16[256,256]{1,0:T(8,128)(2,1)S(1)}, bf16[256,256]{1,0:T(8,128)(2,1)}, u32[]{:S(2)}) copy-start(bf16[256,256]{1,0:T(8,128)(2,1)} %constant.15.clone.left) | copy-start | bytes 393220
  5.6 33.8 %copy-start.6 = (f32[128,128]{1,0:T(8,128)S(1)}, f32[128,128]{1,0:T(8,128)}, u32[]{:S(2)}) copy-start(f32[128,128]{1,0:T(8,128)} %constant.16.clone.decay) | copy-start | bytes 196612
  5.6 33.8 %copy-start.7 = (f32[128,128]{1,0:T(8,128)S(1)}, f32[128,128]{1,0:T(8,128)}, u32[]{:S(2)}) copy-start(f32[128,128]{1,0:T(8,128)} %constant.17.clone.scale) | copy-start | bytes 196612
  7.2 9.3 %collective-permute-start.12 = (f32[1,512,128]{2,1,0:T(8,128)S(1)}, f32[1,512,128]{2,1,0:T(8,128)S(1)}, u32[]{:S(2)}, u32[]{:S(2)}) collective-permute-start(f32[1,512,128]{2,1,0:T(8,128)S(1)} %get-tuple-element.67), channel_id=1, source_target_pairs={{0,64},{1,65},{2,66},{3,67},{4,68},{5,69},{6,70},{7,71},{8,72},{9,... | collective-permute-start | bytes 786440 | tf_op jit(solution)/shard_map/ppermute | solution.py:421
  7.2 20.8 %collective-permute-start.14 = (f32[1,512,128]{2,1,0:T(8,128)S(1)}, f32[1,512,128]{2,1,0:T(8,128)S(1)}, u32[]{:S(2)}, u32[]{:S(2)}) collective-permute-start(f32[1,512,128]{2,1,0:T(8,128)S(1)} %get-tuple-element.69), channel_id=1, source_target_pairs={{0,65},{1,64},{2,67},{3,66},{4,69},{5,68},{6,71},{7,70},{8,73},{9,... | collective-permute-start | bytes 786440 | tf_op jit(solution)/shard_map/ppermute | solution.py:421
  8.1 25.2 %collective-permute-start.13 = (f32[1,512,128]{2,1,0:T(8,128)S(1)}, f32[1,512,128]{2,1,0:T(8,128)S(1)}, u32[]{:S(2)}, u32[]{:S(2)}) collective-permute-start(f32[1,512,128]{2,1,0:T(8,128)S(1)} %get-tuple-element.68), channel_id=1, source_target_pairs={{0,64},{1,65},{2,66},{3,67},{4,68},{5,69},{6,70},{7,71},{8,72},{9,... | collective-permute-start | bytes 786440 | tf_op jit(solution)/shard_map/ppermute | solution.py:421
  9.0 41.3 %collective-permute-start.25 = (f32[1,512,128]{2,1,0:T(8,128)S(1)}, f32[1,512,128]{2,1,0:T(8,128)S(1)}, u32[]{:S(2)}, u32[]{:S(2)}) collective-permute-start(f32[1,512,128]{2,1,0:T(8,128)S(1)} %get-tuple-element.82), channel_id=1, source_target_pairs={{0,32},{1,33},{2,34},{3,35},{4,36},{5,37},{6,38},{7,39},{8,40},{9,... | collective-permute-start | bytes 786440 | tf_op jit(solution)/shard_map/ppermute | solution.py:421
  16.4 22.9 %collective-permute-start.15 = (f32[1,512,128]{2,1,0:T(8,128)S(1)}, f32[1,512,128]{2,1,0:T(8,128)S(1)}, u32[]{:S(2)}, u32[]{:S(2)}) collective-permute-start(f32[1,512,128]{2,1,0:T(8,128)S(1)} %get-tuple-element.70), channel_id=1, source_target_pairs={{0,65},{1,64},{2,67},{3,66},{4,69},{5,68},{6,71},{7,70},{8,73},{9,... | collective-permute-start | bytes 786440 | tf_op jit(solution)/shard_map/ppermute | solution.py:421
  28.1 23.2 %collective-permute-start.26 = (f32[1,512,128]{2,1,0:T(8,128)S(1)}, f32[1,512,128]{2,1,0:T(8,128)S(1)}, u32[]{:S(2)}, u32[]{:S(2)}) collective-permute-start(f32[1,512,128]{2,1,0:T(8,128)S(1)} %get-tuple-element.83), channel_id=1, source_target_pairs={{0,33},{1,32},{2,35},{3,34},{4,37},{5,36},{6,39},{7,38},{8,41},{9,... | collective-permute-start | bytes 786440 | tf_op jit(solution)/shard_map/ppermute | solution.py:421
  46.8 13.8 %collective-permute-start.16 = (f32[520,128]{1,0:T(8,128)S(1)}, f32[520,128]{1,0:T(8,128)S(1)}, u32[]{:S(2)}, u32[]{:S(2)}) collective-permute-start(f32[520,128]{1,0:T(8,128)S(1)} %get-tuple-element.73), channel_id=1, source_target_pairs={{0,2},{1,3},{2,4},{3,5},{4,6},{5,7},{6,0},{7,1},{8,10},{9,11},{10,... | collective-permute-start | bytes 798728 | tf_op jit(solution)/shard_map/ppermute | solution.py:421
  46.9 14.7 %collective-permute-start.17 = (f32[520,128]{1,0:T(8,128)S(1)}, f32[520,128]{1,0:T(8,128)S(1)}, u32[]{:S(2)}, u32[]{:S(2)}) collective-permute-start(f32[520,128]{1,0:T(8,128)S(1)} %get-tuple-element.74), channel_id=1, source_target_pairs={{0,4},{1,5},{2,6},{3,7},{4,0},{5,1},{6,2},{7,3},{8,12},{9,13},{10,... | collective-permute-start | bytes 798728 | tf_op jit(solution)/shard_map/ppermute | solution.py:421
  49.3 13.0 %collective-permute-start.18 = (f32[520,128]{1,0:T(8,128)S(1)}, f32[520,128]{1,0:T(8,128)S(1)}, u32[]{:S(2)}, u32[]{:S(2)}) collective-permute-start(f32[520,128]{1,0:T(8,128)S(1)} %get-tuple-element.75), channel_id=1, source_target_pairs={{0,6},{1,7},{2,0},{3,1},{4,2},{5,3},{6,4},{7,5},{8,14},{9,15},{10,... | collective-permute-start | bytes 798728 | tf_op jit(solution)/shard_map/ppermute | solution.py:421
  50.3 14.9 %collective-permute-start.1 = (f32[1,512,128]{2,1,0:T(8,128)S(1)}, f32[1,512,128]{2,1,0:T(8,128)S(1)}, u32[]{:S(2)}, u32[]{:S(2)}) collective-permute-start(f32[1,512,128]{2,1,0:T(8,128)S(1)} %get-tuple-element.54), channel_id=1, source_target_pairs={{0,32},{1,33},{2,34},{3,35},{4,36},{5,37},{6,38},{7,39},{8,40},{9,... | collective-permute-start | bytes 786440 | tf_op jit(solution)/shard_map/ppermute | solution.py:421
  51.3 13.8 %copy-start.2 = (f32[4,128,128]{2,1,0:T(8,128)S(1)}, f32[4,128,128]{2,1,0:T(8,128)}, u32[]{:S(2)}) copy-start(f32[4,128,128]{2,1,0:T(8,128)} %constant.18.clone.chips) | copy-start | bytes 786436
  51.3 30.2 %collective-permute-start.2 = (f32[1,512,128]{2,1,0:T(8,128)S(1)}, f32[1,512,128]{2,1,0:T(8,128)S(1)}, u32[]{:S(2)}, u32[]{:S(2)}) collective-permute-start(f32[1,512,128]{2,1,0:T(8,128)S(1)} %get-tuple-element.55), channel_id=1, source_target_pairs={{0,33},{1,32},{2,35},{3,34},{4,37},{5,36},{6,39},{7,38},{8,41},{9,... | collective-permute-start | bytes 786440 | tf_op jit(solution)/shard_map/ppermute | solution.py:421
  60.6 25.4 %collective-permute-start.27 = (f32[264,128]{1,0:T(8,128)S(1)}, f32[264,128]{1,0:T(8,128)S(1)}, u32[]{:S(2)}, u32[]{:S(2)}) collective-permute-start(f32[264,128]{1,0:T(8,128)S(1)} %get-tuple-element.86), channel_id=1, source_target_pairs={{0,2},{1,3},{2,4},{3,5},{4,6},{5,7},{6,0},{7,1},{8,10},{9,11},{10,... | collective-permute-start | bytes 405512 | tf_op jit(solution)/shard_map/ppermute | solution.py:421
  61.6 26.8 %collective-permute-start.28 = (f32[264,128]{1,0:T(8,128)S(1)}, f32[264,128]{1,0:T(8,128)S(1)}, u32[]{:S(2)}, u32[]{:S(2)}) collective-permute-start(f32[264,128]{1,0:T(8,128)S(1)} %get-tuple-element.87), channel_id=1, source_target_pairs={{0,4},{1,5},{2,6},{3,7},{4,0},{5,1},{6,2},{7,3},{8,12},{9,13},{10,... | collective-permute-start | bytes 405512 | tf_op jit(solution)/shard_map/ppermute | solution.py:421
  62.3 28.0 %collective-permute-start.29 = (f32[264,128]{1,0:T(8,128)S(1)}, f32[264,128]{1,0:T(8,128)S(1)}, u32[]{:S(2)}, u32[]{:S(2)}) collective-permute-start(f32[264,128]{1,0:T(8,128)S(1)} %get-tuple-element.88), channel_id=1, source_target_pairs={{0,6},{1,7},{2,0},{3,1},{4,2},{5,3},{6,4},{7,5},{8,14},{9,15},{10,... | collective-permute-start | bytes 405512 | tf_op jit(solution)/shard_map/ppermute | solution.py:421
  65.2 36.8 %copy-start.3 = (f32[3,128,128]{2,1,0:T(8,128)S(1)}, f32[3,128,128]{2,1,0:T(8,128)}, u32[]{:S(2)}) copy-start(f32[3,128,128]{2,1,0:T(8,128)} %constant.19.clone.runs) | copy-start | bytes 589828
  65.2 37.0 %collective-permute-start.19 = (f32[520,128]{1,0:T(8,128)S(1)}, f32[520,128]{1,0:T(8,128)S(1)}, u32[]{:S(2)}, u32[]{:S(2)}) collective-permute-start(f32[520,128]{1,0:T(8,128)S(1)} %run.4.mine), channel_id=1, source_target_pairs={{0,8},{1,9},{2,10},{3,11},{4,12},{5,13},{6,14},{7,15},{8,0},{9,1},... | collective-permute-start | bytes 798728 | tf_op jit(solution)/shard_map/ppermute | solution.py:421
  85.5 11.1 %collective-permute-start.3 = (f32[264,128]{1,0:T(8,128)S(1)}, f32[264,128]{1,0:T(8,128)S(1)}, u32[]{:S(2)}, u32[]{:S(2)}) collective-permute-start(f32[264,128]{1,0:T(8,128)S(1)} %get-tuple-element.58), channel_id=1, source_target_pairs={{0,2},{1,3},{2,4},{3,5},{4,6},{5,7},{6,0},{7,1},{8,10},{9,11},{10,... | collective-permute-start | bytes 405512 | tf_op jit(solution)/shard_map/ppermute | solution.py:421
  86.0 10.6 %collective-permute-start.4 = (f32[264,128]{1,0:T(8,128)S(1)}, f32[264,128]{1,0:T(8,128)S(1)}, u32[]{:S(2)}, u32[]{:S(2)}) collective-permute-start(f32[264,128]{1,0:T(8,128)S(1)} %get-tuple-element.59), channel_id=1, source_target_pairs={{0,4},{1,5},{2,6},{3,7},{4,0},{5,1},{6,2},{7,3},{8,12},{9,13},{10,... | collective-permute-start | bytes 405512 | tf_op jit(solution)/shard_map/ppermute | solution.py:421
  88.4 8.2 %collective-permute-start.5 = (f32[264,128]{1,0:T(8,128)S(1)}, f32[264,128]{1,0:T(8,128)S(1)}, u32[]{:S(2)}, u32[]{:S(2)}) collective-permute-start(f32[264,128]{1,0:T(8,128)S(1)} %get-tuple-element.60), channel_id=1, source_target_pairs={{0,6},{1,7},{2,0},{3,1},{4,2},{5,3},{6,4},{7,5},{8,14},{9,15},{10,... | collective-permute-start | bytes 405512 | tf_op jit(solution)/shard_map/ppermute | solution.py:421
  90.4 11.7 %collective-permute-start.30 = (f32[264,128]{1,0:T(8,128)S(1)}, f32[264,128]{1,0:T(8,128)S(1)}, u32[]{:S(2)}, u32[]{:S(2)}) collective-permute-start(f32[264,128]{1,0:T(8,128)S(1)} %run.5.mine), channel_id=1, source_target_pairs={{0,8},{1,9},{2,10},{3,11},{4,12},{5,13},{6,14},{7,15},{8,0},{9,1},... | collective-permute-start | bytes 405512 | tf_op jit(solution)/shard_map/ppermute | solution.py:421
  96.6 8.8 %collective-permute-start.6 = (f32[264,128]{1,0:T(8,128)S(1)}, f32[264,128]{1,0:T(8,128)S(1)}, u32[]{:S(2)}, u32[]{:S(2)}) collective-permute-start(f32[264,128]{1,0:T(8,128)S(1)} %run.3.mine), channel_id=1, source_target_pairs={{0,8},{1,9},{2,10},{3,11},{4,12},{5,13},{6,14},{7,15},{8,0},{9,1},... | collective-permute-start | bytes 405512 | tf_op jit(solution)/shard_map/ppermute | solution.py:421
  102.1 17.5 %collective-permute-start.31 = (f32[264,128]{1,0:T(8,128)S(1)}, f32[264,128]{1,0:T(8,128)S(1)}, u32[]{:S(2)}, u32[]{:S(2)}) collective-permute-start(f32[264,128]{1,0:T(8,128)S(1)} %two.5.mine), channel_id=1, source_target_pairs={{0,16},{1,17},{2,18},{3,19},{4,20},{5,21},{6,22},{7,23},{8,24},{9,... | collective-permute-start | bytes 405512 | tf_op jit(solution)/shard_map/ppermute | solution.py:421
  102.3 26.7 %collective-permute-start.20 = (f32[520,128]{1,0:T(8,128)S(1)}, f32[520,128]{1,0:T(8,128)S(1)}, u32[]{:S(2)}, u32[]{:S(2)}) collective-permute-start(f32[520,128]{1,0:T(8,128)S(1)} %two.4.mine), channel_id=1, source_target_pairs={{0,16},{1,17},{2,18},{3,19},{4,20},{5,21},{6,22},{7,23},{8,24},{9,... | collective-permute-start | bytes 798728 | tf_op jit(solution)/shard_map/ppermute | solution.py:421
  105.5 22.8 %collective-permute-start.7 = (f32[264,128]{1,0:T(8,128)S(1)}, f32[264,128]{1,0:T(8,128)S(1)}, u32[]{:S(2)}, u32[]{:S(2)}) collective-permute-start(f32[264,128]{1,0:T(8,128)S(1)} %two.3.mine), channel_id=1, source_target_pairs={{0,16},{1,17},{2,18},{3,19},{4,20},{5,21},{6,22},{7,23},{8,24},{9,... | collective-permute-start | bytes 405512 | tf_op jit(solution)/shard_map/ppermute | solution.py:421
  119.8 16.2 %copy-start.8 = (f32[1,128]{1,0:T(1,128)S(1)}, f32[1,128]{1,0:T(1,128)}, u32[]{:S(2)}) copy-start(f32[1,128]{1,0:T(1,128)} %constant.20.clone.mean) | copy-start | bytes 1540
  119.8 11.7 %collective-permute-start.32 = (f32[264,128]{1,0:T(8,128)S(1)}, f32[264,128]{1,0:T(8,128)S(1)}, u32[]{:S(2)}, u32[]{:S(2)}) collective-permute-start(f32[264,128]{1,0:T(8,128)S(1)} %get-tuple-element.90), channel_id=1, source_target_pairs={{0,6},{1,7},{2,0},{3,1},{4,2},{5,3},{6,4},{7,5},{8,14},{9,15},{10,... | collective-permute-start | bytes 405512 | tf_op jit(solution)/shard_map/ppermute | solution.py:421
  122.5 10.3 %collective-permute-start.33 = (f32[264,128]{1,0:T(8,128)S(1)}, f32[264,128]{1,0:T(8,128)S(1)}, u32[]{:S(2)}, u32[]{:S(2)}) collective-permute-start(f32[264,128]{1,0:T(8,128)S(1)} %get-tuple-element.91), channel_id=1, source_target_pairs={{0,4},{1,5},{2,6},{3,7},{4,0},{5,1},{6,2},{7,3},{8,12},{9,13},{10,... | collective-permute-start | bytes 405512 | tf_op jit(solution)/shard_map/ppermute | solution.py:421
  122.5 11.0 %collective-permute-start.34 = (f32[264,128]{1,0:T(8,128)S(1)}, f32[264,128]{1,0:T(8,128)S(1)}, u32[]{:S(2)}, u32[]{:S(2)}) collective-permute-start(f32[264,128]{1,0:T(8,128)S(1)} %get-tuple-element.92), channel_id=1, source_target_pairs={{0,2},{1,3},{2,4},{3,5},{4,6},{5,7},{6,0},{7,1},{8,10},{9,11},{10,... | collective-permute-start | bytes 405512 | tf_op jit(solution)/shard_map/ppermute | solution.py:421
  128.4 7.0 %collective-permute-start.10 = (f32[264,128]{1,0:T(8,128)S(1)}, f32[264,128]{1,0:T(8,128)S(1)}, u32[]{:S(2)}, u32[]{:S(2)}) collective-permute-start(f32[264,128]{1,0:T(8,128)S(1)} %get-tuple-element.64), channel_id=1, source_target_pairs={{0,2},{1,3},{2,4},{3,5},{4,6},{5,7},{6,0},{7,1},{8,10},{9,11},{10,... | collective-permute-start | bytes 405512 | tf_op jit(solution)/shard_map/ppermute | solution.py:421
  129.3 26.3 %collective-permute-start.21 = (f32[520,128]{1,0:T(8,128)S(1)}, f32[520,128]{1,0:T(8,128)S(1)}, u32[]{:S(2)}, u32[]{:S(2)}) collective-permute-start(f32[520,128]{1,0:T(8,128)S(1)} %get-tuple-element.77), channel_id=1, source_target_pairs={{0,6},{1,7},{2,0},{3,1},{4,2},{5,3},{6,4},{7,5},{8,14},{9,15},{10,... | collective-permute-start | bytes 798728 | tf_op jit(solution)/shard_map/ppermute | solution.py:421
  131.5 27.5 %collective-permute-start.22 = (f32[520,128]{1,0:T(8,128)S(1)}, f32[520,128]{1,0:T(8,128)S(1)}, u32[]{:S(2)}, u32[]{:S(2)}) collective-permute-start(f32[520,128]{1,0:T(8,128)S(1)} %get-tuple-element.78), channel_id=1, source_target_pairs={{0,4},{1,5},{2,6},{3,7},{4,0},{5,1},{6,2},{7,3},{8,12},{9,13},{10,... | collective-permute-start | bytes 798728 | tf_op jit(solution)/shard_map/ppermute | solution.py:421
  132.8 26.3 %collective-permute-start.23 = (f32[520,128]{1,0:T(8,128)S(1)}, f32[520,128]{1,0:T(8,128)S(1)}, u32[]{:S(2)}, u32[]{:S(2)}) collective-permute-start(f32[520,128]{1,0:T(8,128)S(1)} %get-tuple-element.79), channel_id=1, source_target_pairs={{0,2},{1,3},{2,4},{3,5},{4,6},{5,7},{6,0},{7,1},{8,10},{9,11},{10,... | collective-permute-start | bytes 798728 | tf_op jit(solution)/shard_map/ppermute | solution.py:421
  133.5 12.2 %collective-permute-start.8 = (f32[264,128]{1,0:T(8,128)S(1)}, f32[264,128]{1,0:T(8,128)S(1)}, u32[]{:S(2)}, u32[]{:S(2)}) collective-permute-start(f32[264,128]{1,0:T(8,128)S(1)} %get-tuple-element.62), channel_id=1, source_target_pairs={{0,6},{1,7},{2,0},{3,1},{4,2},{5,3},{6,4},{7,5},{8,14},{9,15},{10,... | collective-permute-start | bytes 405512 | tf_op jit(solution)/shard_map/ppermute | solution.py:421
  135.5 14.5 %collective-permute-start.9 = (f32[264,128]{1,0:T(8,128)S(1)}, f32[264,128]{1,0:T(8,128)S(1)}, u32[]{:S(2)}, u32[]{:S(2)}) collective-permute-start(f32[264,128]{1,0:T(8,128)S(1)} %get-tuple-element.63), channel_id=1, source_target_pairs={{0,4},{1,5},{2,6},{3,7},{4,0},{5,1},{6,2},{7,3},{8,12},{9,13},{10,... | collective-permute-start | bytes 405512 | tf_op jit(solution)/shard_map/ppermute | solution.py:421
  145.8 55.1 %collective-permute-start.35 = (f32[4,512,128]{2,1,0:T(8,128)S(1)}, f32[4,512,128]{2,1,0:T(8,128)S(1)}, u32[]{:S(2)}, u32[]{:S(2)}) collective-permute-start(f32[4,512,128]{2,1,0:T(8,128)S(1)} %get-tuple-element.94), channel_id=1, source_target_pairs={{0,1},{1,0},{2,3},{3,2},{4,5},{5,4},{6,7},{7,6},{8,9},{9,8},{10,11... | collective-permute-start | bytes 3145736 | tf_op jit(solution)/shard_map/ppermute | solution.py:421
  149.9 20.6 %collective-permute-start.40 = (f32[1,512,128]{2,1,0:T(8,128)S(1)}, f32[1,512,128]{2,1,0:T(8,128)S(1)}, u32[]{:S(2)}, u32[]{:S(2)}) collective-permute-start(f32[1,512,128]{2,1,0:T(8,128)S(1)} %get-tuple-element.99), channel_id=1, source_target_pairs={{0,224},{1,225},{2,226},{3,227},{4,228},{5,229},{6,230},{7,231},{8... | collective-permute-start | bytes 786440 | tf_op jit(solution)/shard_map/ppermute | solution.py:421
  155.6 20.6 %collective-permute-start.41 = (f32[1,512,128]{2,1,0:T(8,128)S(1)}, f32[1,512,128]{2,1,0:T(8,128)S(1)}, u32[]{:S(2)}, u32[]{:S(2)}) collective-permute-start(f32[1,512,128]{2,1,0:T(8,128)S(1)} %get-tuple-element.100), channel_id=1, source_target_pairs={{0,225},{1,224},{2,227},{3,226},{4,229},{5,228},{6,231},{7,230},{8... | collective-permute-start | bytes 786440 | tf_op jit(solution)/shard_map/ppermute | solution.py:421
  159.1 41.7 %collective-permute-start.11 = (f32[4,512,128]{2,1,0:T(8,128)S(1)}, f32[4,512,128]{2,1,0:T(8,128)S(1)}, u32[]{:S(2)}, u32[]{:S(2)}) collective-permute-start(f32[4,512,128]{2,1,0:T(8,128)S(1)} %get-tuple-element.66), channel_id=1, source_target_pairs={{0,1},{1,0},{2,3},{3,2},{4,5},{5,4},{6,7},{7,6},{8,9},{9,8},{10,11... | collective-permute-start | bytes 3145736 | tf_op jit(solution)/shard_map/ppermute | solution.py:421
  170.0 46.8 %collective-permute-start.24 = (f32[4,512,128]{2,1,0:T(8,128)S(1)}, f32[4,512,128]{2,1,0:T(8,128)S(1)}, u32[]{:S(2)}, u32[]{:S(2)}) collective-permute-start(f32[4,512,128]{2,1,0:T(8,128)S(1)} %get-tuple-element.81), channel_id=1, source_target_pairs={{0,1},{1,0},{2,3},{3,2},{4,5},{5,4},{6,7},{7,6},{8,9},{9,8},{10,11... | collective-permute-start | bytes 3145736 | tf_op jit(solution)/shard_map/ppermute | solution.py:421
  170.6 10.9 %collective-permute-start.36 = (f32[1,512,128]{2,1,0:T(8,128)S(1)}, f32[1,512,128]{2,1,0:T(8,128)S(1)}, u32[]{:S(2)}, u32[]{:S(2)}) collective-permute-start(f32[1,512,128]{2,1,0:T(8,128)S(1)} %get-tuple-element.95), channel_id=1, source_target_pairs={{0,224},{1,225},{2,226},{3,227},{4,228},{5,229},{6,230},{7,231},{8... | collective-permute-start | bytes 786440 | tf_op jit(solution)/shard_map/ppermute | solution.py:421
  176.2 18.7 %collective-permute-start.37 = (f32[1,512,128]{2,1,0:T(8,128)S(1)}, f32[1,512,128]{2,1,0:T(8,128)S(1)}, u32[]{:S(2)}, u32[]{:S(2)}) collective-permute-start(f32[1,512,128]{2,1,0:T(8,128)S(1)} %get-tuple-element.96), channel_id=1, source_target_pairs={{0,225},{1,224},{2,227},{3,226},{4,229},{5,228},{6,231},{7,230},{8... | collective-permute-start | bytes 786440 | tf_op jit(solution)/shard_map/ppermute | solution.py:421
  181.5 24.2 %collective-permute-start.38 = (f32[2,512,128]{2,1,0:T(8,128)S(1)}, f32[2,512,128]{2,1,0:T(8,128)S(1)}, u32[]{:S(2)}, u32[]{:S(2)}) collective-permute-start(f32[2,512,128]{2,1,0:T(8,128)S(1)} %get-tuple-element.97), channel_id=1, source_target_pairs={{0,192},{1,193},{2,194},{3,195},{4,196},{5,197},{6,198},{7,199},{8... | collective-permute-start | bytes 1572872 | tf_op jit(solution)/shard_map/ppermute | solution.py:421
  194.9 22.0 %collective-permute-start.39 = (f32[2,512,128]{2,1,0:T(8,128)S(1)}, f32[2,512,128]{2,1,0:T(8,128)S(1)}, u32[]{:S(2)}, u32[]{:S(2)}) collective-permute-start(f32[2,512,128]{2,1,0:T(8,128)S(1)} %get-tuple-element.98), channel_id=1, source_target_pairs={{0,193},{1,192},{2,195},{3,194},{4,197},{5,196},{6,199},{7,198},{8... | collective-permute-start | bytes 1572872 | tf_op jit(solution)/shard_map/ppermute | solution.py:421

commit v2 on v0

v2 whole, which is shorter than its diff:
```python
import functools
import math

import jax
import jax.numpy as jnp
import ml_dtypes
import numpy as np
from jax import lax
from jax.experimental import pallas as pl
from jax.experimental.pallas import tpu as pltpu
from jax.sharding import PartitionSpec as P

GRID = 128
SUB = 4
NSUB = 2
ROUNDS = 2
CORES = 2
YS = 4
ZS = 4
PLANES = 4
ROWS = GRID * PLANES
HALF = SUB // CORES
QUARTER = GRID // YS
EDGE = 2 * QUARTER
CHAINS = ((1, (0, 1)), (0, (0, 1)))
F32 = jnp.float32
BF16 = jnp.bfloat16


@functools.cache
def tables():
    index = np.arange(GRID, dtype=np.int64)
    angle = (index[:, None] * index[None, :] % GRID) * (2.0 * math.pi / GRID)
    cas = (np.cos(angle) + np.sin(angle)).astype(np.float32)
    high = cas.astype(ml_dtypes.bfloat16)
    low = (cas - high.astype(np.float32)).astype(ml_dtypes.bfloat16)
    zero = np.zeros_like(high)
    right = np.block([[high, low], [high, zero]])
    left = np.block([[high, high], [low, zero]])
    roots = 2.0 - 2.0 * np.cos(index * (2.0 * math.pi / GRID))
    screen = (4.0 * math.pi / GRID) ** 2
    shift = screen + roots[:, None] + roots[None, :]
    spread = np.sqrt(shift + shift * shift / 4.0)
    decay = 1.0 / (1.0 + shift / 2.0 + spread)
    scale = 1.0 / (2.0 * spread * GRID**2)
    mean = np.zeros((1, GRID))
    mean[0, 0] = 2.0 * spread[0, 0] / (GRID * screen)
    chips = np.stack([decay ** (8 * k) for k in range(YS)])
    runs = np.stack([decay**32, decay**64, 1.0 / (1.0 - decay**GRID)])
    as32 = lambda value: np.asarray(value, dtype=np.float32)
    return right, left, as32(decay), as32(scale), as32(mean), as32(chips), as32(runs)


def split(value):
    high = value.astype(BF16)
    low = (value - high.astype(F32)).astype(BF16)
    return high, low


def times_right(value, table):
    full = jnp.dot(jnp.concatenate(split(value), axis=1), table, preferred_element_type=F32)
    return full[:, :GRID] + full[:, GRID:]


def times_left(value, table):
    full = jnp.dot(table, jnp.concatenate(split(value), axis=0), preferred_element_type=F32)
    return full[:GRID] + full[GRID:]


def place():
    spot = lax.axis_index("grid")
    return spot // (YS * CORES), (spot // CORES) % YS, spot % CORES


def quarter_of(which):
    return pl.ds(pl.multiple_of(which * QUARTER, QUARTER), QUARTER)


def array(shape, dtype=F32):
    return jax.ShapeDtypeStruct(tuple(shape), dtype)


HBM = pl.BlockSpec(memory_space=pltpu.HBM)
VMEM = pl.BlockSpec(memory_space=pltpu.VMEM)
SMEM = pl.BlockSpec(memory_space=pltpu.SMEM)


def launch(kernel, token, args, in_specs, out_specs, out_shape, name, limit, grid=(), scratch=(), after=()):
    ins, outs, waits = len(args), len(out_shape), 1 + len(after)
    unread = pl.BlockSpec(memory_space=pl.ANY)

    def ordered(*refs):
        kernel(*refs[:ins], *refs[ins + waits : ins + waits + outs], *refs[ins + waits + outs + 1 :])

    result = pl.pallas_call(
        ordered,
        grid=grid,
        in_specs=[*in_specs, *[unread] * waits],
        out_specs=[*out_specs, unread],
        scratch_shapes=list(scratch),
        out_shape=[*out_shape, array(token.shape)],
        compiler_params=pltpu.CompilerParams(vmem_limit_bytes=limit << 20),
        cost_estimate=pl.CostEstimate(flops=0, bytes_accessed=0, transcendentals=0),
        name=name,
    )(*args, token, *after)
    return result[:-1], result[-1]


def message(pairs):
    return array((pairs * EDGE + 8, GRID))


def pairs_of(ref):
    return ref.shape[0] // EDGE


def copy_all(copies, sems):
    started = []
    for number, (source, target) in enumerate(copies):
        copy = pltpu.make_async_copy(source, target, sems.at[number])
        copy.start()
        started.append(copy)
    for copy in started:
        copy.wait()


def pick_kernel(plan, own_a, own_b, index, first, second, sems):
    band_count = lax.axis_size("band")
    band_me = lax.axis_index("band")
    core = place()[2]
    index[0] = plan[0, band_me, 0]
    index[1] = plan[1, (band_me + 2) % band_count, 1]
    index[2] = plan[0, (band_me + 1) % band_count, 1]
    index[3] = plan[1, band_me, 0]
    copies = []
    for step, out in enumerate((first, second)):
        start = index[ROUNDS + step] * SUB + core * HALF
        for source, own in enumerate((own_a, own_b)):
            copies.append((own.at[pl.ds(start, HALF)], out.at[source]))
    copy_all(copies, sems)


def pick(token, plan, own):
    two = array((CORES, HALF, ROWS, GRID))
    outs, token = launch(
        pick_kernel, token, [plan, *own], [SMEM, HBM, VMEM], [SMEM] + [VMEM] * 2,
        [array((2 * ROUNDS,), jnp.int32), two, two], "pick", 2,
        scratch=[pltpu.SemaphoreType.DMA((2 * CORES,))],
    )
    return *outs, token


def pick_own_kernel(index, own_a, own_b, out, sems):
    copy_all(
        [
            (own.at[pl.ds(index[step] * SUB, SUB)], out.at[step, source])
            for step in range(ROUNDS)
            for source, own in enumerate((own_a, own_b))
        ],
        sems,
    )


def pick_own(token, index, own):
    (out,), token = launch(
        pick_own_kernel, token, [index, *own], [SMEM, HBM, VMEM], [VMEM],
        [array((ROUNDS, CORES, SUB, ROWS, GRID))], "pick_own", 2,
        scratch=[pltpu.SemaphoreType.DMA((ROUNDS * CORES,))],
    )
    return out, token


def forward_kernel(step, member, own, part, right, left, decay, scale, spec, a, b, c, d, lines):
    outs = (a, b, c, d)
    _, y, core = place()
    j = pl.program_id(0)
    for i in range(SUB):
        for source in range(CORES):
            spot = i * CORES + source
            lines[spot] = times_right(own[step, source, i] * part[source, member + j], right[...])
            half = (core if source == 0 else 1 - core) * PLANES
            for x in range(0, PLANES, 2):
                two = jnp.concatenate(
                    [lines[spot, pl.ds(x + k, GRID, stride=PLANES), :] for k in range(2)], axis=1
                )
                two = times_left(two, left[...])
                for k in range(2):
                    spec[j * SUB + i, half + x + k] = two[:, k * GRID : (k + 1) * GRID] * scale[...]
    for i in range(SUB):
        pair = j * SUB + i
        base = pl.multiple_of(pair * EDGE, EDGE)
        total = spec[pair, 0, 0:1, :]
        for x in range(1, 2 * PLANES):
            total = total + spec[pair, x, 0:1, :]
        for k in range(YS):
            rows = quarter_of((y + k) % YS)
            ratio = decay[rows, :]
            planes = [spec[pair, x, rows, :] for x in range(2 * PLANES)]
            ahead, behind = planes[0], planes[-1]
            for x in range(1, 2 * PLANES):
                ahead = planes[x] + ratio * ahead
                behind = planes[-1 - x] + ratio * behind
            outs[k][pl.ds(base, QUARTER), :] = ahead
            outs[k][pl.ds(base + QUARTER, QUARTER), :] = behind
            outs[k][pl.ds(pairs_of(a) * EDGE + pair, 1), :] = total


def forward(token, step, members, own, part):
    right, left, decay, scale = tables()[:4]
    pairs = len(members) * SUB
    outs, token = launch(
        functools.partial(forward_kernel, step, members[0]),
        token,
        [own, part, right, left, decay, scale],
        [VMEM] * 6,
        [VMEM] * (1 + YS),
        [array((pairs, 2 * PLANES, GRID, GRID))] + [message(pairs)] * YS,
        "forward", 12, grid=(len(members),),
        scratch=[pltpu.VMEM((SUB * CORES, ROWS, GRID), F32)],
    )
    return outs[0], outs[1:], token


def run_kernel(a, b, c, d, chips, out):
    _, y, _ = place()
    rows = quarter_of(y)
    got = (a, b, c, d)
    from_chip = [(y - k + YS) % YS for k in range(YS)]
    ahead = [chips[YS - 1 - chip, rows, :] for chip in from_chip]
    behind = [chips[chip, rows, :] for chip in from_chip]
    for pair in range(pairs_of(out)):
        base = pair * EDGE
        for weights, start in ((ahead, base), (behind, base + QUARTER)):
            at = slice(start, start + QUARTER)
            out[at, :] = sum(got[k][at, :] * weights[k] for k in range(YS))
    at = slice(pairs_of(out) * EDGE, pairs_of(out) * EDGE + 8)
    out[at, :] = sum(got[k][at, :] for k in range(YS))


def two_kernel(mine, other, runs, out):
    z, y, _ = place()
    power = runs[0, quarter_of(y), :]
    odd = (jnp.zeros(power.shape, jnp.int32) + z % 2) == 1
    ones = jnp.ones_like(power)
    first = jnp.where(odd, ones, power)
    second = jnp.where(odd, power, ones)
    for pair in range(pairs_of(out)):
        base = pair * EDGE
        at = slice(base, base + QUARTER)
        out[at, :] = mine[at, :] * first + other[at, :] * second
        at = slice(base + QUARTER, base + 2 * QUARTER)
        out[at, :] = mine[at, :] * second + other[at, :] * first
    at = slice(pairs_of(mine) * EDGE, pairs_of(mine) * EDGE + 8)
    out[at, :] = mine[at, :] + other[at, :]


def edges_kernel(a, b, c, d, near, mine, other, chips, runs, *rest):
    outs, held = rest[:YS], rest[YS]
    z, y, _ = place()
    rows = quarter_of(y)
    got = (a, b, c, d)
    step, run, two, wrap = chips[1, rows, :], runs[0, rows, :], runs[1, rows, :], runs[2, rows, :]
    odd = (jnp.zeros(step.shape, jnp.int32) + z % 2) == 1
    for k in range(YS):
        held[(y - k + YS) % YS] = got[k][...]
    for pair in range(pairs_of(a)):
        base = pair * EDGE
        ahead = slice(base, base + QUARTER)
        behind = slice(base + QUARTER, base + 2 * QUARTER)
        from_left = (other[ahead, :] + two * mine[ahead, :]) * wrap
        from_right = (other[behind, :] + two * mine[behind, :]) * wrap
        from_left = jnp.where(odd, near[ahead, :] + run * from_left, from_left)
        from_right = jnp.where(odd, from_right, near[behind, :] + run * from_right)
        for chip in range(YS):
            chip_ahead = held[chip, ahead, :]
            held[chip, ahead, :] = from_left
            from_left = chip_ahead + step * from_left
        for chip in reversed(range(YS)):
            chip_behind = held[chip, behind, :]
            held[chip, behind, :] = from_right
            from_right = chip_behind + step * from_right
    at = slice(pairs_of(mine) * EDGE, pairs_of(mine) * EDGE + 8)
    total = mine[at, :] + other[at, :]
    for k in range(YS):
        outs[k][...] = held[(y - k + YS) % YS]
        outs[k][at, :] = total


def small(kernel, token, args, count, name, scratch=(), after=()):
    return launch(
        kernel, token, args, [VMEM] * len(args), [VMEM] * count, [array(args[0].shape)] * count, name, 6,
        scratch=scratch, after=after,
    )


def backward_kernel(step, member, prior, extra, spec, a, b, c, d, own, part, right, left, decay, mean, *rest):
    before, (part_out, own_out_a, own_out_b, field, lines) = rest[: prior + extra], rest[prior + extra :]
    j = pl.program_id(0)
    edges = (a, b, c, d)
    _, y, core = place()
    for i in range(SUB):
        pair = j * SUB + i
        base = pl.multiple_of(pair * EDGE, EDGE)
        for k in range(YS):
            rows = quarter_of((y + k) % YS)
            ratio = decay[rows, :]
            planes = [spec[pair, x, rows, :] for x in range(2 * PLANES)]
            ahead = edges[k][pl.ds(base, QUARTER), :]
            behind = edges[k][pl.ds(base + QUARTER, QUARTER), :]
            sums = []
            for x in range(2 * PLANES):
                ahead = planes[x] + ratio * ahead
                sums.append(ahead)
            for x in reversed(range(2 * PLANES)):
                behind = ratio * behind
                field[i, x, rows, :] = sums[x] + behind
                behind = planes[x] + behind
        average = a[pl.ds(pairs_of(a) * EDGE + pair, 1), :] * mean[...]
        for x in range(2 * PLANES):
            field[i, x, 0:1, :] = field[i, x, 0:1, :] - average
    for source, own_out in enumerate((own_out_a, own_out_b)):
        half = (core if source == 0 else 1 - core) * PLANES
        added = None
        for i in range(SUB):
            spot = i * CORES + source
            for x in range(0, PLANES, 2):
                two = jnp.concatenate([field[i, half + x + k] for k in range(2)], axis=1)
                two = times_left(two, left[...])
                for k in range(2):
                    lines[spot, pl.ds(x + k, GRID, stride=PLANES), :] = two[:, k * GRID : (k + 1) * GRID]
            potential = times_right(lines[spot], right[...])
            to_part = potential * own[step, source, i]
            to_own = potential * part[source, member + j]
            added = to_part if added is None else added + to_part
            if prior:
                own_out[0, i] = before[source][0, i] - to_own
            else:
                own_out[0, i] = jnp.where(j == 0, 0.0, own_out[0, i]) - to_own
        part_out[source, j] = -added
    if extra:
        own_out_b[1] = before[prior][0]


def backward(token, step, members, spec, edges, own, part, prior=(), extra=()):
    right, left, decay, _, mean = tables()[:5]
    args = [spec, *edges, own, part, right, left, decay, mean, *prior, *extra]
    outs, token = launch(
        functools.partial(backward_kernel, step, members[0], len(prior), len(extra)),
        token,
        args,
        [VMEM] * len(args),
        [VMEM] * 3,
        [
            array((CORES, len(members), ROWS, GRID)),
            array((1, SUB, ROWS, GRID)),
            array((1 + len(extra), SUB, ROWS, GRID)),
        ],
        "backward", 12, grid=(len(members),),
        scratch=[
            pltpu.VMEM((SUB, 2 * PLANES, GRID, GRID), F32),
            pltpu.VMEM((SUB * CORES, ROWS, GRID), F32),
        ],
    )
    return outs[0], outs[1:], token


def early_kernel(index, own_first, own_second, swapped, same, cross, out):
    core = place()[2]
    for i in range(SUB):
        out[index[0] * SUB + i] = own_first[0, i] + swapped[0, i]
        out[(NSUB - 1 - index[0]) * SUB + i] = jnp.zeros((ROWS, GRID), F32)
    for i in range(SUB):
        band = index[1] * SUB + i
        out[band] = out[band] + (own_second[0, i] + swapped[1, i])
    for part, target in ((same, core), (cross, 1 - core)):
        for member in range(HALF):
            band = index[ROUNDS + 1] * SUB + target * HALF + member
            out[band] = out[band] + part[0, member]


def add_early(token, index, terms):
    (total,), token = launch(
        early_kernel, token, [index, *terms], [SMEM] + [VMEM] * len(terms),
        [VMEM], [array((NSUB * SUB, ROWS, GRID))], "add_early", 4,
    )
    return total, token


def late_kernel(index, total, same, cross, out, fresh, sems):
    core = place()[2]
    base = index[ROUNDS] * SUB
    other = (NSUB - 1) * SUB - base
    rest = pltpu.make_async_copy(total.at[pl.ds(other, SUB)], out.at[pl.ds(other, SUB)], sems.at[0])
    rest.start()
    for k, (part, target) in enumerate(((same, core), (cross, 1 - core))):
        for member in range(HALF):
            at = target * HALF + member
            fresh[at] = total[base + at] + part[0, member]
    added = pltpu.make_async_copy(fresh, out.at[pl.ds(base, SUB)], sems.at[1])
    added.start()
    rest.wait()
    added.wait()


def add_late(token, index, total, terms):
    (total,), token = launch(
        late_kernel, token, [index, total, *terms], [SMEM] + [VMEM] * 3, [HBM],
        [array(total.shape)], "add_late", 4,
        scratch=[pltpu.VMEM((SUB, ROWS, GRID), F32), pltpu.SemaphoreType.DMA((2,))],
    )
    return total


def body(orbitals, plan):
    bands = lax.axis_size("band")
    spots = lax.axis_size("grid")

    def move(value, target):
        pairs = []
        for band in range(bands):
            for spot in range(spots):
                z, y, core = spot // (YS * CORES), (spot // CORES) % YS, spot % CORES
                b2, z2, y2, c2 = target(band, z, y, core)
                pairs.append((band * spots + spot, (b2 % bands) * spots + (z2 * YS + y2 % YS) * CORES + c2))
        return lax.ppermute(value, ("band", "grid"), pairs)

    def swap_cores(value):
        return move(value, lambda b, z, y, c: (b, z, y, 1 - c))

    def shift(value, steps):
        return move(value, lambda b, z, y, c: (b + steps, z, y, c))

    def along_y(messages, sign):
        return [messages[0]] + [
            move(messages[k], lambda b, z, y, c, k=k: (b, z, y + YS + sign * k, c)) for k in range(1, YS)
        ]

    chips, runs = tables()[5:7]
    blocks = orbitals.reshape(NSUB * SUB, PLANES, GRID, GRID).transpose(0, 2, 1, 3)
    blocks = blocks.reshape(NSUB * SUB, ROWS, GRID)
    both = (blocks, swap_cores(blocks))
    token = jnp.zeros((8, GRID), F32)
    index, *sends, token = pick(token, plan, both)
    parts = [shift(sends[0], 1), shift(sends[1], -2)]
    own, token = pick_own(token, index, both)
    chains = [{} for _ in CHAINS]

    def start(at):
        nonlocal token
        step, members = CHAINS[at]
        chain = chains[at]
        chain["spec"], sums, token = forward(token, step, members, own, parts[step])
        chain["sums"] = along_y(sums, 1)

    def run(at):
        nonlocal token
        chain = chains[at]
        (chain["run"],), token = small(run_kernel, token, [*chain["sums"], chips], 1, "run")
        chain["near"] = move(chain["run"], lambda b, z, y, c: (b, z ^ 1, y, c))

    def two(at):
        nonlocal token
        chain = chains[at]
        (chain["two"],), token = small(two_kernel, token, [chain["run"], chain["near"], runs], 1, "two")
        chain["far"] = move(chain["two"], lambda b, z, y, c: (b, z ^ 2, y, c))

    def edges(at, after=()):
        nonlocal token
        chain = chains[at]
        args = [*chain["sums"], chain["near"], chain["two"], chain["far"], chips, runs]
        outs, token = small(
            edges_kernel, token, args, YS, "edges", [pltpu.VMEM((YS, *chain["run"].shape), F32)], after
        )
        chain["edges"] = along_y(outs, -1)

    def finish(at, prior=(), extra=()):
        nonlocal token
        step, members = CHAINS[at]
        chain = chains[at]
        terms, sums, token = backward(
            token, step, members, chain["spec"], chain["edges"], own, parts[step], prior, extra
        )
        return terms, sums

    def give_back(at, terms):
        steps = (-1, 2)[CHAINS[at][0]]
        return [shift(terms[:1], steps), move(terms[1:], lambda b, z, y, c: (b + steps, z, y, 1 - c))]

    second, first = range(len(CHAINS))
    start(second)
    run(second)
    start(first)
    two(second)
    run(first)
    edges(second)
    two(first)
    terms_b, sums_b = finish(second)
    edges(first)
    terms_a, sums_a = finish(first, extra=sums_b[1:])
    total, token = add_early(
        token, index, [sums_a[0], sums_b[0], swap_cores(sums_a[1]), *give_back(second, terms_b)]
    )
    final = give_back(first, terms_a)
    total = add_late(token, index, total, final)
    total = total.reshape(NSUB * SUB, GRID, PLANES, GRID).transpose(0, 2, 1, 3)
    return total.reshape(NSUB * SUB, PLANES, GRID * GRID)


def solution(mesh):
    in_specs = (P("band", "grid", None), P())
    out_specs = P("band", "grid", None)
    return jax.shard_map(body, mesh=mesh, in_specs=in_specs, out_specs=out_specs, check_vma=False)
```

time: 638 us -> 185 us (0.29)
  the two profiles are of different devices: /device:TPU:243 before, /device:TPU:5 now
where the time goes in v2:
time: 185 us
  waiting for transfers between devices  115 us (62%)
  starting transfers between devices  44.4 us (24%)
  Pallas kernels  22.8 us (12%)
  local copies, waits for them, and re-layouts  2.53 us (1%)
    ppermute x24, waiting for transfers between devices, move(): return lax.ppermute(value, ('band', 'grid'), pairs)  115 us
    ppermute x24, starting transfers between devices, move(): return lax.ppermute(value, ('band', 'grid'), pairs)  44.4 us
    pallas_call x14, Pallas kernels, launch(): pl.pallas_call(ordered, grid=grid, in_specs=[*in_specs, *[unread] * waits...  22.8 us
  transfers between devices with their start and end apart: 24, of which 16 were waited for; matrix products, arithmetic and copies ran while one was open for 0% of the time, Pallas kernels for 8%

profile of v2, /device:TPU:5, one launch (start us, length us, event | category | flops | bytes accessed | tf_op | source)
XLA Modules:
  0.0 185.3 jit_solution(4318197713026455824)
XLA Ops:
  0.0 0.7 collective-permute-start
  0.7 0.8 copy.11.refs_0_
  1.4 3.2 %collective-permute-done.refs_2_ = f32[8,512,128]{2,1,0:T(8,128)S(1)} collective-permute-done((f32[8,512,128]{2,1,0:T(8,128)}, f32[8,512,128]{2,1,0:T(8,128)S(1)}, u32[]{:S(2)}, u32[]{:S(2)}) %collective-permute-start) | collective-permute-done | bytes 2097184 | tf_op jit(solution)/shard_map/ppermute | solution.py:425
  4.7 1.6 copy-done
  6.3 1.5 pick.1
  7.7 0.3 collective-permute-start.2
  8.1 6.9 %collective-permute-start.1 = (f32[2,2,512,128]{3,2,1,0:T(8,128)S(1)}, f32[2,2,512,128]{3,2,1,0:T(8,128)S(1)}, u32[]{:S(2)}, u32[]{:S(2)}) collective-permute-start(f32[2,2,512,128]{3,2,1,0:T(8,128)S(1)} %get-tuple-element.55), channel_id=1, source_target_pairs={{0,32},{1,33},{2,34},{3,35},{4,36},{5,37},{6,38},{7,39},{8,40},{9,... | collective-permute-start | bytes 3145736 | tf_op jit(solution)/shard_map/ppermute | solution.py:425
  15.0 0.0 copy-start.7
  15.0 0.9 pick_own.1
  15.9 16.3 %collective-permute-done.2.refs_1_.refs_6_ = f32[2,2,512,128]{3,2,1,0:T(8,128)S(1)} collective-permute-done((f32[2,2,512,128]{3,2,1,0:T(8,128)S(1)}, f32[2,2,512,128]{3,2,1,0:T(8,128)S(1)}, u32[]{:S(2)}, u32[]{:S(2)}) %collective-permute-start.2) | collective-permute-done | bytes 1048608 | tf_op jit(solution)/shard_map/ppermute | solution.py:425
  32.2 0.0 copy-start.2
  32.2 4.0 %forward.2 = (f32[8,8,128,128]{3,2,1,0:T(8,128)S(1)}, f32[520,128]{1,0:T(8,128)S(1)}, f32[520,128]{1,0:T(8,128)S(1)}, f32[520,128]{1,0:T(8,128)S(1)}, f32[520,128]{1,0:T(8,128)S(1)}, /*index=5*/f32[8,128]{1,0:T(8,128)S(1)}) custom-call(f32[2,2,4,512,128]{4,3,2,1,0:T(8,128)S(1)} %get-tuple-element.54.refs_0_.refs_5_, ...), custom_call_target="tpu_custom_call" | custom-call | tf_op jit(solution)/shard_map/forward/pallas_call | solution.py:95
  36.3 1.4 collective-permute-start.3
  37.6 2.6 %collective-permute-start.4 = (f32[520,128]{1,0:T(8,128)S(1)}, f32[520,128]{1,0:T(8,128)S(1)}, u32[]{:S(2)}, u32[]{:S(2)}) collective-permute-start(f32[520,128]{1,0:T(8,128)S(1)} %get-tuple-element.60), channel_id=1, source_target_pairs={{0,4},{1,5},{2,6},{3,7},{4,0},{5,1},{6,2},{7,3},{8,12},{9,13},{10,... | collective-permute-start | bytes 798728 | tf_op jit(solution)/shard_map/ppermute | solution.py:425
  40.3 1.1 collective-permute-start.5
  41.3 3.0 %collective-permute-done.3.refs_1_ = f32[520,128]{1,0:T(8,128)S(1)} collective-permute-done((f32[520,128]{1,0:T(8,128)S(1)}, f32[520,128]{1,0:T(8,128)S(1)}, u32[]{:S(2)}, u32[]{:S(2)}) %collective-permute-start.3) | collective-permute-done | bytes 266272 | tf_op jit(solution)/shard_map/ppermute | solution.py:425
  44.4 6.8 %collective-permute-done.4.refs_2_ = f32[520,128]{1,0:T(8,128)S(1)} collective-permute-done((f32[520,128]{1,0:T(8,128)S(1)}, f32[520,128]{1,0:T(8,128)S(1)}, u32[]{:S(2)}, u32[]{:S(2)}) %collective-permute-start.4) | collective-permute-done | bytes 266272 | tf_op jit(solution)/shard_map/ppermute | solution.py:425
  51.2 0.1 collective-permute-done.5.refs_3_
  51.3 0.1 run.2
  51.4 1.7 collective-permute-start.9
  53.1 0.0 collective-permute-done.1.refs_1_.refs_6_
  53.1 4.0 %forward.3 = (f32[8,8,128,128]{3,2,1,0:T(8,128)S(1)}, f32[520,128]{1,0:T(8,128)S(1)}, f32[520,128]{1,0:T(8,128)S(1)}, f32[520,128]{1,0:T(8,128)S(1)}, f32[520,128]{1,0:T(8,128)S(1)}, /*index=5*/f32[8,128]{1,0:T(8,128)S(1)}) custom-call(f32[2,2,4,512,128]{4,3,2,1,0:T(8,128)S(1)} %get-tuple-element.54.refs_0_.refs_5_, ...), custom_call_target="tpu_custom_call" | custom-call | tf_op jit(solution)/shard_map/forward/pallas_call | solution.py:95
  57.1 1.9 collective-permute-start.6
  58.9 2.8 %collective-permute-start.7 = (f32[520,128]{1,0:T(8,128)S(1)}, f32[520,128]{1,0:T(8,128)S(1)}, u32[]{:S(2)}, u32[]{:S(2)}) collective-permute-start(f32[520,128]{1,0:T(8,128)S(1)} %get-tuple-element.67), channel_id=1, source_target_pairs={{0,4},{1,5},{2,6},{3,7},{4,0},{5,1},{6,2},{7,3},{8,12},{9,13},{10,... | collective-permute-start | bytes 798728 | tf_op jit(solution)/shard_map/ppermute | solution.py:425
  61.8 5.2 %collective-permute-done.9.refs_1_.refs_4_ = f32[520,128]{1,0:T(8,128)S(1)} collective-permute-done((f32[520,128]{1,0:T(8,128)S(1)}, f32[520,128]{1,0:T(8,128)S(1)}, u32[]{:S(2)}, u32[]{:S(2)}) %collective-permute-start.9) | collective-permute-done | bytes 266272 | tf_op jit(solution)/shard_map/ppermute | solution.py:425
  67.0 0.1 two.2
  67.0 5.3 %collective-permute-start.11 = (f32[520,128]{1,0:T(8,128)S(1)}, f32[520,128]{1,0:T(8,128)S(1)}, u32[]{:S(2)}, u32[]{:S(2)}) collective-permute-start(f32[520,128]{1,0:T(8,128)S(1)} %get-tuple-element.73.refs_5_), channel_id=1, source_target_pairs={{0,16},{1,17},{2,18},{3,19},{4,20},{5,21},{6,22},{7,23},{8,24},{9,... | collective-permute-start | bytes 798728 | tf_op jit(solution)/shard_map/ppermute | solution.py:425
  72.3 0.0 collective-permute-done.6.refs_1_
  72.3 0.0 collective-permute-done.7.refs_2_
  72.3 0.0 collective-permute-done.8.refs_3_
  72.3 0.0 copy-start.8
  72.3 0.1 run.3
  72.5 1.3 collective-permute-start.10
  73.8 10.3 %collective-permute-done.11.refs_6_ = f32[520,128]{1,0:T(8,128)S(1)} collective-permute-done((f32[520,128]{1,0:T(8,128)S(1)}, f32[520,128]{1,0:T(8,128)S(1)}, u32[]{:S(2)}, u32[]{:S(2)}) %collective-permute-start.11) | collective-permute-done | bytes 266272 | tf_op jit(solution)/shard_map/ppermute | solution.py:425
  84.1 0.3 edges.2
  84.4 0.8 collective-permute-start.13
  85.2 1.1 collective-permute-start.14
  86.4 0.0 collective-permute-start.15
  86.4 0.1 two.3
  86.4 4.9 %collective-permute-start.12 = (f32[520,128]{1,0:T(8,128)S(1)}, f32[520,128]{1,0:T(8,128)S(1)}, u32[]{:S(2)}, u32[]{:S(2)}) collective-permute-start(f32[520,128]{1,0:T(8,128)S(1)} %get-tuple-element.76.refs_5_), channel_id=1, source_target_pairs={{0,16},{1,17},{2,18},{3,19},{4,20},{5,21},{6,22},{7,23},{8,24},{9,... | collective-permute-start | bytes 798728 | tf_op jit(solution)/shard_map/ppermute | solution.py:425
  91.3 2.0 %collective-permute-done.14.refs_3_ = f32[520,128]{1,0:T(8,128)S(1)} collective-permute-done((f32[520,128]{1,0:T(8,128)S(1)}, f32[520,128]{1,0:T(8,128)S(1)}, u32[]{:S(2)}, u32[]{:S(2)}) %collective-permute-start.14) | collective-permute-done | bytes 266272 | tf_op jit(solution)/shard_map/ppermute | solution.py:425
  93.4 7.4 %collective-permute-done.15.refs_4_ = f32[520,128]{1,0:T(8,128)S(1)} collective-permute-done((f32[520,128]{1,0:T(8,128)S(1)}, f32[520,128]{1,0:T(8,128)S(1)}, u32[]{:S(2)}, u32[]{:S(2)}) %collective-permute-start.15) | collective-permute-done | bytes 266272 | tf_op jit(solution)/shard_map/ppermute | solution.py:425
  100.8 4.3 %backward.2 = (f32[2,2,512,128]{3,2,1,0:T(8,128)S(1)}, f32[1,4,512,128]{3,2,1,0:T(8,128)S(1)}, f32[1,4,512,128]{3,2,1,0:T(8,128)S(1)}, f32[8,128]{1,0:T(8,128)S(1)}) custom-call(f32[8,8,128,128]{3,2,1,0:T(8,128)S(1)} %get-tuple-element.77.refs_0_, f32[520,128]{1,0:T(8,128)S(1)} %get-tuple-element.78.refs_1_, f32[520,128]{1,0:T(8,128)S(1)} %collective-permute-done.13.refs_2_, ...), custom_call_target="tpu_custom_call" | custom-call | tf_op jit(solution)/shard_map/backward/pallas_call | solution.py:95
  105.1 0.3 edges.3
  105.4 1.0 collective-permute-start.16
  106.3 0.3 collective-permute-start.17
  106.7 0.8 collective-permute-start.18
  107.4 5.5 %collective-permute-done.16.refs_2_ = f32[520,128]{1,0:T(8,128)S(1)} collective-permute-done((f32[520,128]{1,0:T(8,128)S(1)}, f32[520,128]{1,0:T(8,128)S(1)}, u32[]{:S(2)}, u32[]{:S(2)}) %collective-permute-start.16) | collective-permute-done | bytes 266272 | tf_op jit(solution)/shard_map/ppermute | solution.py:425
  112.9 2.1 %collective-permute-done.17.refs_3_ = f32[520,128]{1,0:T(8,128)S(1)} collective-permute-done((f32[520,128]{1,0:T(8,128)S(1)}, f32[520,128]{1,0:T(8,128)S(1)}, u32[]{:S(2)}, u32[]{:S(2)}) %collective-permute-start.17) | collective-permute-done | bytes 266272 | tf_op jit(solution)/shard_map/ppermute | solution.py:425
  115.0 6.8 %collective-permute-done.18.refs_4_ = f32[520,128]{1,0:T(8,128)S(1)} collective-permute-done((f32[520,128]{1,0:T(8,128)S(1)}, f32[520,128]{1,0:T(8,128)S(1)}, u32[]{:S(2)}, u32[]{:S(2)}) %collective-permute-start.18) | collective-permute-done | bytes 266272 | tf_op jit(solution)/shard_map/ppermute | solution.py:425
  121.9 4.3 %backward.3 = (f32[2,2,512,128]{3,2,1,0:T(8,128)S(1)}, f32[1,4,512,128]{3,2,1,0:T(8,128)S(1)}, f32[2,4,512,128]{3,2,1,0:T(8,128)S(1)}, f32[8,128]{1,0:T(8,128)S(1)}) custom-call(f32[8,8,128,128]{3,2,1,0:T(8,128)S(1)} %get-tuple-element.64.refs_0_, f32[520,128]{1,0:T(8,128)S(1)} %get-tuple-element.84.refs_1_, f32[520,128]{1,0:T(8,128)S(1)} %collective-permute-done.16.refs_2_, ...), custom_call_target="tpu_custom_call" | custom-call | tf_op jit(solution)/shard_map/backward/pallas_call | solution.py:95
  126.2 0.6 collective-permute-start.19
  126.8 0.1 fusion.1
  126.8 1.5 collective-permute-start.21
  128.4 2.5 %collective-permute-start.20 = (f32[1,2,512,128]{3,2,1,0:T(8,128)S(1)}, f32[1,2,512,128]{3,2,1,0:T(8,128)S(1)}, u32[]{:S(2)}, u32[]{:S(2)}) collective-permute-start(f32[1,2,512,128]{3,2,1,0:T(8,128)S(1)} %get-tuple-element.102), channel_id=1, source_target_pairs={{0,64},{1,65},{2,66},{3,67},{4,68},{5,69},{6,70},{7,71},{8,72},{9,... | collective-permute-start | bytes 1572872 | tf_op jit(solution)/shard_map/ppermute | solution.py:425
  130.9 0.1 fusion
  130.9 2.5 %collective-permute-start.23 = (f32[1,2,512,128]{3,2,1,0:T(8,128)S(1)}, f32[1,2,512,128]{3,2,1,0:T(8,128)S(1)}, u32[]{:S(2)}, u32[]{:S(2)}) collective-permute-start(f32[1,2,512,128]{3,2,1,0:T(8,128)S(1)} %get-tuple-element.99), channel_id=1, source_target_pairs={{0,225},{1,224},{2,227},{3,226},{4,229},{5,228},{6,231},{7,230},{8... | collective-permute-start | bytes 1572872 | tf_op jit(solution)/shard_map/ppermute | solution.py:425
  133.5 2.2 %collective-permute-start.22 = (f32[1,2,512,128]{3,2,1,0:T(8,128)S(1)}, f32[1,2,512,128]{3,2,1,0:T(8,128)S(1)}, u32[]{:S(2)}, u32[]{:S(2)}) collective-permute-start(f32[1,2,512,128]{3,2,1,0:T(8,128)S(1)} %get-tuple-element.100), channel_id=1, source_target_pairs={{0,224},{1,225},{2,226},{3,227},{4,228},{5,229},{6,230},{7,231},{8... | collective-permute-start | bytes 1572872 | tf_op jit(solution)/shard_map/ppermute | solution.py:425
  135.7 5.7 %collective-permute-done.21.refs_5_ = f32[1,2,512,128]{3,2,1,0:T(8,128)S(1)} collective-permute-done((f32[1,2,512,128]{3,2,1,0:T(8,128)S(1)}, f32[1,2,512,128]{3,2,1,0:T(8,128)S(1)}, u32[]{:S(2)}, u32[]{:S(2)}) %collective-permute-start.21) | collective-permute-done | bytes 524320 | tf_op jit(solution)/shard_map/ppermute | solution.py:425
  141.4 10.0 %collective-permute-done.20.refs_4_ = f32[1,2,512,128]{3,2,1,0:T(8,128)S(1)} collective-permute-done((f32[1,2,512,128]{3,2,1,0:T(8,128)S(1)}, f32[1,2,512,128]{3,2,1,0:T(8,128)S(1)}, u32[]{:S(2)}, u32[]{:S(2)}) %collective-permute-start.20) | collective-permute-done | bytes 524320 | tf_op jit(solution)/shard_map/ppermute | solution.py:425
  151.4 1.0 add_early.1
  152.4 12.4 %collective-permute-done.23.refs_3_ = f32[1,2,512,128]{3,2,1,0:T(8,128)S(1)} collective-permute-done((f32[1,2,512,128]{3,2,1,0:T(8,128)S(1)}, f32[1,2,512,128]{3,2,1,0:T(8,128)S(1)}, u32[]{:S(2)}, u32[]{:S(2)}) %collective-permute-start.23) | collective-permute-done | bytes 524320 | tf_op jit(solution)/shard_map/ppermute | solution.py:425
  164.8 18.4 %collective-permute-done.22.refs_2_ = f32[1,2,512,128]{3,2,1,0:T(8,128)S(1)} collective-permute-done((f32[1,2,512,128]{3,2,1,0:T(8,128)S(1)}, f32[1,2,512,128]{3,2,1,0:T(8,128)S(1)}, u32[]{:S(2)}, u32[]{:S(2)}) %collective-permute-start.22) | collective-permute-done | bytes 524320 | tf_op jit(solution)/shard_map/ppermute | solution.py:425
  183.2 1.9 %add_late.1 = (f32[8,512,128]{2,1,0:T(8,128)}, f32[8,128]{1,0:T(8,128)}) custom-call(s32[4]{0:T(128)S(1)} %get-tuple-element.52.refs_0_, f32[8,512,128]{2,1,0:T(8,128)S(1)} %get-tuple-element.95.refs_1_, f32[1,2,512,128]{3,2,1,0:T(8,128)S(1)} %collective-permute-done.22.refs_2_, f32[1,2,512,128]{3,2,1,0:T(8,128)S(1)} %collective-permute-done.23.refs_3_, ...), custom_call_target="tpu_custom_call" | custom-call | tf_op jit(solution)/shard_map/add_late/pallas_call | solution.py:95
  (20 shorter events, 0.0 us)
Async XLA Ops:
  0.0 4.7 %collective-permute-start = (f32[8,512,128]{2,1,0:T(8,128)}, f32[8,512,128]{2,1,0:T(8,128)S(1)}, u32[]{:S(2)}, u32[]{:S(2)}) collective-permute-start(f32[8,512,128]{2,1,0:T(8,128)} %bitcast.10), channel_id=1, source_target_pairs={{0,1},{1,0},{2,3},{3,2},{4,5},{5,4},{6,7},{7,6},{8,9},{9,8},{10,11... | collective-permute-start | bytes 6291464 | tf_op jit(solution)/shard_map/ppermute | solution.py:425
  4.7 1.6 copy-start
  6.3 8.7 %copy-start.1 = (f32[8,4,16384]{2,1,0:T(4,128)S(1)}, f32[8,4,16384]{2,1,0:T(4,128)}, u32[]{:S(2)}) copy-start(f32[8,4,16384]{2,1,0:T(4,128)} %param.9) | copy-start | bytes 6291460
  7.7 24.5 %collective-permute-start.2 = (f32[2,2,512,128]{3,2,1,0:T(8,128)S(1)}, f32[2,2,512,128]{3,2,1,0:T(8,128)S(1)}, u32[]{:S(2)}, u32[]{:S(2)}) collective-permute-start(f32[2,2,512,128]{3,2,1,0:T(8,128)S(1)} %get-tuple-element.56), channel_id=1, source_target_pairs={{0,192},{1,193},{2,194},{3,195},{4,196},{5,197},{6,198},{7,199},{8... | collective-permute-start | bytes 3145736 | tf_op jit(solution)/shard_map/ppermute | solution.py:425
  8.1 45.0 %collective-permute-start.1 = (f32[2,2,512,128]{3,2,1,0:T(8,128)S(1)}, f32[2,2,512,128]{3,2,1,0:T(8,128)S(1)}, u32[]{:S(2)}, u32[]{:S(2)}) collective-permute-start(f32[2,2,512,128]{3,2,1,0:T(8,128)S(1)} %get-tuple-element.55), channel_id=1, source_target_pairs={{0,32},{1,33},{2,34},{3,35},{4,36},{5,37},{6,38},{7,39},{8,40},{9,... | collective-permute-start | bytes 3145736 | tf_op jit(solution)/shard_map/ppermute | solution.py:425
  15.0 17.2 %copy-start.4 = (bf16[256,256]{1,0:T(8,128)(2,1)S(1)}, bf16[256,256]{1,0:T(8,128)(2,1)}, u32[]{:S(2)}) copy-start(bf16[256,256]{1,0:T(8,128)(2,1)} %constant.17.clone.refs_3_.refs_8_) | copy-start | bytes 393220
  15.0 17.2 %copy-start.5 = (bf16[256,256]{1,0:T(8,128)(2,1)S(1)}, bf16[256,256]{1,0:T(8,128)(2,1)}, u32[]{:S(2)}) copy-start(bf16[256,256]{1,0:T(8,128)(2,1)} %constant.16.clone.refs_2_.refs_7_) | copy-start | bytes 393220
  15.0 17.2 %copy-start.6 = (f32[128,128]{1,0:T(8,128)S(1)}, f32[128,128]{1,0:T(8,128)}, u32[]{:S(2)}) copy-start(f32[128,128]{1,0:T(8,128)} %constant.18.clone.refs_4_.refs_9_) | copy-start | bytes 196612
  15.0 17.2 %copy-start.7 = (f32[128,128]{1,0:T(8,128)S(1)}, f32[128,128]{1,0:T(8,128)}, u32[]{:S(2)}) copy-start(f32[128,128]{1,0:T(8,128)} %constant.19.clone.refs_5_) | copy-start | bytes 196612
  32.2 19.0 %copy-start.2 = (f32[4,128,128]{2,1,0:T(8,128)S(1)}, f32[4,128,128]{2,1,0:T(8,128)}, u32[]{:S(2)}) copy-start(f32[4,128,128]{2,1,0:T(8,128)} %constant.20.clone.refs_4_.refs_7_) | copy-start | bytes 786436
  36.3 8.1 %collective-permute-start.3 = (f32[520,128]{1,0:T(8,128)S(1)}, f32[520,128]{1,0:T(8,128)S(1)}, u32[]{:S(2)}, u32[]{:S(2)}) collective-permute-start(f32[520,128]{1,0:T(8,128)S(1)} %get-tuple-element.59), channel_id=1, source_target_pairs={{0,2},{1,3},{2,4},{3,5},{4,6},{5,7},{6,0},{7,1},{8,10},{9,11},{10,... | collective-permute-start | bytes 798728 | tf_op jit(solution)/shard_map/ppermute | solution.py:425
  37.6 13.5 %collective-permute-start.4 = (f32[520,128]{1,0:T(8,128)S(1)}, f32[520,128]{1,0:T(8,128)S(1)}, u32[]{:S(2)}, u32[]{:S(2)}) collective-permute-start(f32[520,128]{1,0:T(8,128)S(1)} %get-tuple-element.60), channel_id=1, source_target_pairs={{0,4},{1,5},{2,6},{3,7},{4,0},{5,1},{6,2},{7,3},{8,12},{9,13},{10,... | collective-permute-start | bytes 798728 | tf_op jit(solution)/shard_map/ppermute | solution.py:425
  40.3 11.0 %collective-permute-start.5 = (f32[520,128]{1,0:T(8,128)S(1)}, f32[520,128]{1,0:T(8,128)S(1)}, u32[]{:S(2)}, u32[]{:S(2)}) collective-permute-start(f32[520,128]{1,0:T(8,128)S(1)} %get-tuple-element.61), channel_id=1, source_target_pairs={{0,6},{1,7},{2,0},{3,1},{4,2},{5,3},{6,4},{7,5},{8,14},{9,15},{10,... | collective-permute-start | bytes 798728 | tf_op jit(solution)/shard_map/ppermute | solution.py:425
  51.4 15.6 %collective-permute-start.9 = (f32[520,128]{1,0:T(8,128)S(1)}, f32[520,128]{1,0:T(8,128)S(1)}, u32[]{:S(2)}, u32[]{:S(2)}) collective-permute-start(f32[520,128]{1,0:T(8,128)S(1)} %get-tuple-element.69.refs_0_), channel_id=1, source_target_pairs={{0,8},{1,9},{2,10},{3,11},{4,12},{5,13},{6,14},{7,15},{8,0},{9,1},... | collective-permute-start | bytes 798728 | tf_op jit(solution)/shard_map/ppermute | solution.py:425
  53.1 13.9 %copy-start.3 = (f32[3,128,128]{2,1,0:T(8,128)S(1)}, f32[3,128,128]{2,1,0:T(8,128)}, u32[]{:S(2)}) copy-start(f32[3,128,128]{2,1,0:T(8,128)} %constant.21.clone.refs_2_.refs_8_) | copy-start | bytes 589828
  57.1 15.2 %collective-permute-start.6 = (f32[520,128]{1,0:T(8,128)S(1)}, f32[520,128]{1,0:T(8,128)S(1)}, u32[]{:S(2)}, u32[]{:S(2)}) collective-permute-start(f32[520,128]{1,0:T(8,128)S(1)} %get-tuple-element.66), channel_id=1, source_target_pairs={{0,2},{1,3},{2,4},{3,5},{4,6},{5,7},{6,0},{7,1},{8,10},{9,11},{10,... | collective-permute-start | bytes 798728 | tf_op jit(solution)/shard_map/ppermute | solution.py:425
  58.9 13.4 %collective-permute-start.7 = (f32[520,128]{1,0:T(8,128)S(1)}, f32[520,128]{1,0:T(8,128)S(1)}, u32[]{:S(2)}, u32[]{:S(2)}) collective-permute-start(f32[520,128]{1,0:T(8,128)S(1)} %get-tuple-element.67), channel_id=1, source_target_pairs={{0,4},{1,5},{2,6},{3,7},{4,0},{5,1},{6,2},{7,3},{8,12},{9,13},{10,... | collective-permute-start | bytes 798728 | tf_op jit(solution)/shard_map/ppermute | solution.py:425
  61.8 10.6 %collective-permute-start.8 = (f32[520,128]{1,0:T(8,128)S(1)}, f32[520,128]{1,0:T(8,128)S(1)}, u32[]{:S(2)}, u32[]{:S(2)}) collective-permute-start(f32[520,128]{1,0:T(8,128)S(1)} %get-tuple-element.68), channel_id=1, source_target_pairs={{0,6},{1,7},{2,0},{3,1},{4,2},{5,3},{6,4},{7,5},{8,14},{9,15},{10,... | collective-permute-start | bytes 798728 | tf_op jit(solution)/shard_map/ppermute | solution.py:425
  67.0 17.1 %collective-permute-start.11 = (f32[520,128]{1,0:T(8,128)S(1)}, f32[520,128]{1,0:T(8,128)S(1)}, u32[]{:S(2)}, u32[]{:S(2)}) collective-permute-start(f32[520,128]{1,0:T(8,128)S(1)} %get-tuple-element.73.refs_5_), channel_id=1, source_target_pairs={{0,16},{1,17},{2,18},{3,19},{4,20},{5,21},{6,22},{7,23},{8,24},{9,... | collective-permute-start | bytes 798728 | tf_op jit(solution)/shard_map/ppermute | solution.py:425
  72.3 28.4 %copy-start.8 = (f32[1,128]{1,0:T(1,128)S(1)}, f32[1,128]{1,0:T(1,128)}, u32[]{:S(2)}) copy-start(f32[1,128]{1,0:T(1,128)} %constant.22.clone.refs_10_) | copy-start | bytes 1540
  72.5 13.9 %collective-permute-start.10 = (f32[520,128]{1,0:T(8,128)S(1)}, f32[520,128]{1,0:T(8,128)S(1)}, u32[]{:S(2)}, u32[]{:S(2)}) collective-permute-start(f32[520,128]{1,0:T(8,128)S(1)} %get-tuple-element.72.refs_0_), channel_id=1, source_target_pairs={{0,8},{1,9},{2,10},{3,11},{4,12},{5,13},{6,14},{7,15},{8,0},{9,1},... | collective-permute-start | bytes 798728 | tf_op jit(solution)/shard_map/ppermute | solution.py:425
  84.4 6.9 %collective-permute-start.13 = (f32[520,128]{1,0:T(8,128)S(1)}, f32[520,128]{1,0:T(8,128)S(1)}, u32[]{:S(2)}, u32[]{:S(2)}) collective-permute-start(f32[520,128]{1,0:T(8,128)S(1)} %get-tuple-element.79), channel_id=1, source_target_pairs={{0,6},{1,7},{2,0},{3,1},{4,2},{5,3},{6,4},{7,5},{8,14},{9,15},{10,... | collective-permute-start | bytes 798728 | tf_op jit(solution)/shard_map/ppermute | solution.py:425
  85.2 8.1 %collective-permute-start.14 = (f32[520,128]{1,0:T(8,128)S(1)}, f32[520,128]{1,0:T(8,128)S(1)}, u32[]{:S(2)}, u32[]{:S(2)}) collective-permute-start(f32[520,128]{1,0:T(8,128)S(1)} %get-tuple-element.80), channel_id=1, source_target_pairs={{0,4},{1,5},{2,6},{3,7},{4,0},{5,1},{6,2},{7,3},{8,12},{9,13},{10,... | collective-permute-start | bytes 798728 | tf_op jit(solution)/shard_map/ppermute | solution.py:425
  86.4 14.4 %collective-permute-start.15 = (f32[520,128]{1,0:T(8,128)S(1)}, f32[520,128]{1,0:T(8,128)S(1)}, u32[]{:S(2)}, u32[]{:S(2)}) collective-permute-start(f32[520,128]{1,0:T(8,128)S(1)} %get-tuple-element.81), channel_id=1, source_target_pairs={{0,2},{1,3},{2,4},{3,5},{4,6},{5,7},{6,0},{7,1},{8,10},{9,11},{10,... | collective-permute-start | bytes 798728 | tf_op jit(solution)/shard_map/ppermute | solution.py:425
  86.4 18.6 %collective-permute-start.12 = (f32[520,128]{1,0:T(8,128)S(1)}, f32[520,128]{1,0:T(8,128)S(1)}, u32[]{:S(2)}, u32[]{:S(2)}) collective-permute-start(f32[520,128]{1,0:T(8,128)S(1)} %get-tuple-element.76.refs_5_), channel_id=1, source_target_pairs={{0,16},{1,17},{2,18},{3,19},{4,20},{5,21},{6,22},{7,23},{8,24},{9,... | collective-permute-start | bytes 798728 | tf_op jit(solution)/shard_map/ppermute | solution.py:425
  105.4 7.5 %collective-permute-start.16 = (f32[520,128]{1,0:T(8,128)S(1)}, f32[520,128]{1,0:T(8,128)S(1)}, u32[]{:S(2)}, u32[]{:S(2)}) collective-permute-start(f32[520,128]{1,0:T(8,128)S(1)} %get-tuple-element.85), channel_id=1, source_target_pairs={{0,6},{1,7},{2,0},{3,1},{4,2},{5,3},{6,4},{7,5},{8,14},{9,15},{10,... | collective-permute-start | bytes 798728 | tf_op jit(solution)/shard_map/ppermute | solution.py:425
  106.3 8.7 %collective-permute-start.17 = (f32[520,128]{1,0:T(8,128)S(1)}, f32[520,128]{1,0:T(8,128)S(1)}, u32[]{:S(2)}, u32[]{:S(2)}) collective-permute-start(f32[520,128]{1,0:T(8,128)S(1)} %get-tuple-element.86), channel_id=1, source_target_pairs={{0,4},{1,5},{2,6},{3,7},{4,0},{5,1},{6,2},{7,3},{8,12},{9,13},{10,... | collective-permute-start | bytes 798728 | tf_op jit(solution)/shard_map/ppermute | solution.py:425
  106.7 15.2 %collective-permute-start.18 = (f32[520,128]{1,0:T(8,128)S(1)}, f32[520,128]{1,0:T(8,128)S(1)}, u32[]{:S(2)}, u32[]{:S(2)}) collective-permute-start(f32[520,128]{1,0:T(8,128)S(1)} %get-tuple-element.87), channel_id=1, source_target_pairs={{0,2},{1,3},{2,4},{3,5},{4,6},{5,7},{6,0},{7,1},{8,10},{9,11},{10,... | collective-permute-start | bytes 798728 | tf_op jit(solution)/shard_map/ppermute | solution.py:425
  126.2 25.2 %collective-permute-start.19 = (f32[2,4,512,128]{3,2,1,0:T(8,128)S(1)}, f32[2,4,512,128]{3,2,1,0:T(8,128)S(1)}, u32[]{:S(2)}, u32[]{:S(2)}) collective-permute-start(f32[2,4,512,128]{3,2,1,0:T(8,128)S(1)} %get-tuple-element.92), channel_id=1, source_target_pairs={{0,1},{1,0},{2,3},{3,2},{4,5},{5,4},{6,7},{7,6},{8,9},{9,8},{10,11... | collective-permute-start | bytes 6291464 | tf_op jit(solution)/shard_map/ppermute | solution.py:425
  126.8 14.5 %collective-permute-start.21 = (f32[1,2,512,128]{3,2,1,0:T(8,128)S(1)}, f32[1,2,512,128]{3,2,1,0:T(8,128)S(1)}, u32[]{:S(2)}, u32[]{:S(2)}) collective-permute-start(f32[1,2,512,128]{3,2,1,0:T(8,128)S(1)} %get-tuple-element.101), channel_id=1, source_target_pairs={{0,65},{1,64},{2,67},{3,66},{4,69},{5,68},{6,71},{7,70},{8,73},{9,... | collective-permute-start | bytes 1572872 | tf_op jit(solution)/shard_map/ppermute | solution.py:425
  128.4 23.0 %collective-permute-start.20 = (f32[1,2,512,128]{3,2,1,0:T(8,128)S(1)}, f32[1,2,512,128]{3,2,1,0:T(8,128)S(1)}, u32[]{:S(2)}, u32[]{:S(2)}) collective-permute-start(f32[1,2,512,128]{3,2,1,0:T(8,128)S(1)} %get-tuple-element.102), channel_id=1, source_target_pairs={{0,64},{1,65},{2,66},{3,67},{4,68},{5,69},{6,70},{7,71},{8,72},{9,... | collective-permute-start | bytes 1572872 | tf_op jit(solution)/shard_map/ppermute | solution.py:425
  130.9 33.9 %collective-permute-start.23 = (f32[1,2,512,128]{3,2,1,0:T(8,128)S(1)}, f32[1,2,512,128]{3,2,1,0:T(8,128)S(1)}, u32[]{:S(2)}, u32[]{:S(2)}) collective-permute-start(f32[1,2,512,128]{3,2,1,0:T(8,128)S(1)} %get-tuple-element.99), channel_id=1, source_target_pairs={{0,225},{1,224},{2,227},{3,226},{4,229},{5,228},{6,231},{7,230},{8... | collective-permute-start | bytes 1572872 | tf_op jit(solution)/shard_map/ppermute | solution.py:425
  133.5 49.8 %collective-permute-start.22 = (f32[1,2,512,128]{3,2,1,0:T(8,128)S(1)}, f32[1,2,512,128]{3,2,1,0:T(8,128)S(1)}, u32[]{:S(2)}, u32[]{:S(2)}) collective-permute-start(f32[1,2,512,128]{3,2,1,0:T(8,128)S(1)} %get-tuple-element.100), channel_id=1, source_target_pairs={{0,224},{1,225},{2,226},{3,227},{4,228},{5,229},{6,230},{7,231},{8... | collective-permute-start | bytes 1572872 | tf_op jit(solution)/shard_map/ppermute | solution.py:425

commit v3 on v2

--- a/solution.py
+++ b/solution.py
@@ -22,7 +22,7 @@
 HALF = SUB // CORES
 QUARTER = GRID // YS
 EDGE = 2 * QUARTER
-CHAINS = ((1, (0, 1)), (0, (0, 1)))
+CHAINS = ((1, (0, 1)), (0, (0,)), (0, (1,)))
 F32 = jnp.float32
 BF16 = jnp.bfloat16
 
@@ -124,6 +124,20 @@
         copy.wait()
 
 
+def load_kernel(blocks, out, sem):
+    copy = pltpu.make_async_copy(blocks, out, sem)
+    copy.start()
+    copy.wait()
+
+
+def load(token, blocks):
+    (out,), token = launch(
+        load_kernel, token, [blocks], [HBM], [VMEM], [array(blocks.shape)], "load", 2,
+        scratch=[pltpu.SemaphoreType.DMA],
+    )
+    return out, token
+
+
 def pick_kernel(plan, own_a, own_b, index, first, second, sems):
     band_count = lax.axis_size("band")
     band_me = lax.axis_index("band")
@@ -143,7 +157,7 @@
 def pick(token, plan, own):
     two = array((CORES, HALF, ROWS, GRID))
     outs, token = launch(
-        pick_kernel, token, [plan, *own], [SMEM, HBM, VMEM], [SMEM] + [VMEM] * 2,
+        pick_kernel, token, [plan, *own], [SMEM, VMEM, VMEM], [SMEM] + [VMEM] * 2,
         [array((2 * ROUNDS,), jnp.int32), two, two], "pick", 2,
         scratch=[pltpu.SemaphoreType.DMA((2 * CORES,))],
     )
@@ -163,7 +177,7 @@
 
 def pick_own(token, index, own):
     (out,), token = launch(
-        pick_own_kernel, token, [index, *own], [SMEM, HBM, VMEM], [VMEM],
+        pick_own_kernel, token, [index, *own], [SMEM, VMEM, VMEM], [VMEM],
         [array((ROUNDS, CORES, SUB, ROWS, GRID))], "pick_own", 2,
         scratch=[pltpu.SemaphoreType.DMA((ROUNDS * CORES,))],
     )
@@ -341,7 +355,7 @@
         own_out_b[1] = before[prior][0]
 
 
-def backward(token, step, members, spec, edges, own, part, prior=(), extra=()):
+def backward(token, step, members, spec, edges, own, part, prior=(), extra=(), after=()):
     right, left, decay, _, mean = tables()[:5]
     args = [spec, *edges, own, part, right, left, decay, mean, *prior, *extra]
     outs, token = launch(
@@ -360,11 +374,12 @@
             pltpu.VMEM((SUB, 2 * PLANES, GRID, GRID), F32),
             pltpu.VMEM((SUB * CORES, ROWS, GRID), F32),
         ],
+        after=after,
     )
     return outs[0], outs[1:], token
 
 
-def early_kernel(index, own_first, own_second, swapped, same, cross, out):
+def early_kernel(index, own_first, own_second, swapped, first, first_swapped, same, cross, out):
     core = place()[2]
     for i in range(SUB):
         out[index[0] * SUB + i] = own_first[0, i] + swapped[0, i]
@@ -376,6 +391,9 @@
         for member in range(HALF):
             band = index[ROUNDS + 1] * SUB + target * HALF + member
             out[band] = out[band] + part[0, member]
+    for part, target in ((first, core), (first_swapped, 1 - core)):
+        band = index[ROUNDS] * SUB + target * HALF
+        out[band] = out[band] + part[0, 0]
 
 
 def add_early(token, index, terms):
@@ -386,27 +404,34 @@
     return total, token
 
 
-def late_kernel(index, total, same, cross, out, fresh, sems):
+def late_kernel(index, total, same, swapped, out, fresh, sems):
     core = place()[2]
     base = index[ROUNDS] * SUB
     other = (NSUB - 1) * SUB - base
-    rest = pltpu.make_async_copy(total.at[pl.ds(other, SUB)], out.at[pl.ds(other, SUB)], sems.at[0])
-    rest.start()
-    for k, (part, target) in enumerate(((same, core), (cross, 1 - core))):
-        for member in range(HALF):
-            at = target * HALF + member
-            fresh[at] = total[base + at] + part[0, member]
-    added = pltpu.make_async_copy(fresh, out.at[pl.ds(base, SUB)], sems.at[1])
-    added.start()
-    rest.wait()
-    added.wait()
+    copies = [(total.at[pl.ds(other, SUB)], out.at[pl.ds(other, SUB)])]
+    copies += [
+        (total.at[pl.ds(base + HALF * k, 1)], out.at[pl.ds(base + HALF * k, 1)]) for k in range(CORES)
+    ]
+    started = [pltpu.make_async_copy(*copy, sems.at[k]) for k, copy in enumerate(copies)]
+    for copy in started:
+        copy.start()
+    for k, (part, target) in enumerate(((same, core), (swapped, 1 - core))):
+        band = base + target * HALF + 1
+        fresh[k] = total[band] + part[0, 0]
+        copy = pltpu.make_async_copy(
+            fresh.at[pl.ds(k, 1)], out.at[pl.ds(band, 1)], sems.at[len(started)]
+        )
+        copy.start()
+        started.append(copy)
+    for copy in started:
+        copy.wait()
 
 
 def add_late(token, index, total, terms):
     (total,), token = launch(
         late_kernel, token, [index, total, *terms], [SMEM] + [VMEM] * 3, [HBM],
         [array(total.shape)], "add_late", 4,
-        scratch=[pltpu.VMEM((SUB, ROWS, GRID), F32), pltpu.SemaphoreType.DMA((2,))],
+        scratch=[pltpu.VMEM((CORES, ROWS, GRID), F32), pltpu.SemaphoreType.DMA((1 + 2 * CORES,))],
     )
     return total
 
@@ -438,8 +463,9 @@
     chips, runs = tables()[5:7]
     blocks = orbitals.reshape(NSUB * SUB, PLANES, GRID, GRID).transpose(0, 2, 1, 3)
     blocks = blocks.reshape(NSUB * SUB, ROWS, GRID)
-    both = (blocks, swap_cores(blocks))
-    token = jnp.zeros((8, GRID), F32)
+    swapped = swap_cores(blocks)
+    held, token = load(jnp.zeros((8, GRID), F32), blocks)
+    both = (held, swapped)
     index, *sends, token = pick(token, plan, both)
     parts = [shift(sends[0], 1), shift(sends[1], -2)]
     own, token = pick_own(token, index, both)
@@ -473,34 +499,39 @@
         )
         chain["edges"] = along_y(outs, -1)
 
-    def finish(at, prior=(), extra=()):
+    def finish(at, prior=(), extra=(), after=()):
         nonlocal token
         step, members = CHAINS[at]
         chain = chains[at]
         terms, sums, token = backward(
-            token, step, members, chain["spec"], chain["edges"], own, parts[step], prior, extra
+            token, step, members, chain["spec"], chain["edges"], own, parts[step], prior, extra, after
         )
         return terms, sums
 
-    def give_back(at, terms):
-        steps = (-1, 2)[CHAINS[at][0]]
-        return [shift(terms[:1], steps), move(terms[1:], lambda b, z, y, c: (b + steps, z, y, 1 - c))]
-
-    second, first = range(len(CHAINS))
+    second, first, last = range(len(CHAINS))
     start(second)
     run(second)
     start(first)
     two(second)
+    start(last)
     run(first)
+    run(last)
     edges(second)
     two(first)
+    two(last)
+    edges(first)
     terms_b, sums_b = finish(second)
-    edges(first)
-    terms_a, sums_a = finish(first, extra=sums_b[1:])
+    edges(last)
+    terms_a, sums_a = finish(first)
+    back_a = shift(terms_a, -1)
+    terms_a, sums_a = finish(last, sums_a, sums_b[1:], [back_a])
+    back_b = [shift(terms_b[:1], 2), move(terms_b[1:], lambda b, z, y, c: (b + 2, z, y, 1 - c))]
     total, token = add_early(
-        token, index, [sums_a[0], sums_b[0], swap_cores(sums_a[1]), *give_back(second, terms_b)]
-    )
-    final = give_back(first, terms_a)
+        token, index,
+        [sums_a[0], sums_b[0], swap_cores(sums_a[1]), back_a, swap_cores(back_a[1:]), *back_b],
+    )
+    back_a = shift(terms_a, -1)
+    final = [back_a, swap_cores(back_a[1:])]
     total = add_late(token, index, total, final)
     total = total.reshape(NSUB * SUB, GRID, PLANES, GRID).transpose(0, 2, 1, 3)
     return total.reshape(NSUB * SUB, PLANES, GRID * GRID)

time: 185 us -> 178 us (0.962)
  the two profiles are of different devices: /device:TPU:5 before, /device:TPU:1 now
where the time goes in v3:
time: 178 us
  waiting for transfers between devices  75 us (42%)
  starting transfers between devices  74.9 us (42%)
  Pallas kernels  22.7 us (13%)
  local copies, waits for them, and re-layouts  4.72 us (3%)
    ppermute x34, waiting for transfers between devices, move(): return lax.ppermute(value, ('band', 'grid'), pairs)  75 us
    ppermute x34, starting transfers between devices, move(): return lax.ppermute(value, ('band', 'grid'), pairs)  74.9 us
    pallas_call x20, Pallas kernels, launch(): pl.pallas_call(ordered, grid=grid, in_specs=[*in_specs, *[unread] * waits...  22.7 us
    unnamed x23, local copies, waits for them, and re-layouts  4.61 us
  transfers between devices with their start and end apart: 34, of which 19 were waited for; matrix products, arithmetic and copies ran while one was open for 0% of the time, Pallas kernels for 9%

profile of v3, /device:TPU:1, one launch (start us, length us, event | category | flops | bytes accessed | tf_op | source)
XLA Modules:
  0.0 177.7 jit_solution(2103576910867520567)
XLA Ops:
  0.0 3.2 %collective-permute-start = (f32[8,512,128]{2,1,0:T(8,128)}, f32[8,512,128]{2,1,0:T(8,128)S(1)}, u32[]{:S(2)}, u32[]{:S(2)}) collective-permute-start(f32[8,512,128]{2,1,0:T(8,128)} %bitcast.10), channel_id=1, source_target_pairs={{0,1},{1,0},{2,3},{3,2},{4,5},{5,4},{6,7},{7,6},{8,9},{9,8},{10,11... | collective-permute-start | bytes 6291464 | tf_op jit(solution)/shard_map/ppermute | solution.py:450
  3.2 1.6 copy-done.7
  4.8 0.1 load.1
  5.0 1.3 copy-done.1
  6.3 0.1 copy.11.refs_0_
  6.4 0.8 collective-permute-done.refs_2_
  7.2 1.6 copy-done.2
  8.8 1.5 pick.1
  10.3 0.8 collective-permute-start.2
  11.1 6.9 %collective-permute-start.1 = (f32[2,2,512,128]{3,2,1,0:T(8,128)S(1)}, f32[2,2,512,128]{3,2,1,0:T(8,128)S(1)}, u32[]{:S(2)}, u32[]{:S(2)}) collective-permute-start(f32[2,2,512,128]{3,2,1,0:T(8,128)S(1)} %get-tuple-element.78), channel_id=1, source_target_pairs={{0,32},{1,33},{2,34},{3,35},{4,36},{5,37},{6,38},{7,39},{8,40},{9,... | collective-permute-start | bytes 3145736 | tf_op jit(solution)/shard_map/ppermute | solution.py:450
  18.1 0.9 pick_own.1
  18.9 15.8 %collective-permute-done.2.refs_1_.refs_6_ = f32[2,2,512,128]{3,2,1,0:T(8,128)S(1)} collective-permute-done((f32[2,2,512,128]{3,2,1,0:T(8,128)S(1)}, f32[2,2,512,128]{3,2,1,0:T(8,128)S(1)}, u32[]{:S(2)}, u32[]{:S(2)}) %collective-permute-start.2) | collective-permute-done | bytes 1048608 | tf_op jit(solution)/shard_map/ppermute | solution.py:450
  34.8 4.0 %forward.3 = (f32[8,8,128,128]{3,2,1,0:T(8,128)S(1)}, f32[520,128]{1,0:T(8,128)S(1)}, f32[520,128]{1,0:T(8,128)S(1)}, f32[520,128]{1,0:T(8,128)S(1)}, f32[520,128]{1,0:T(8,128)S(1)}, /*index=5*/f32[8,128]{1,0:T(8,128)S(1)}) custom-call(f32[2,2,4,512,128]{4,3,2,1,0:T(8,128)S(1)} %get-tuple-element.77.refs_0_.refs_5_, ...), custom_call_target="tpu_custom_call" | custom-call | tf_op jit(solution)/shard_map/forward/pallas_call | solution.py:95
  38.8 2.4 %collective-permute-start.4 = (f32[520,128]{1,0:T(8,128)S(1)}, f32[520,128]{1,0:T(8,128)S(1)}, u32[]{:S(2)}, u32[]{:S(2)}) collective-permute-start(f32[520,128]{1,0:T(8,128)S(1)} %get-tuple-element.83), channel_id=1, source_target_pairs={{0,4},{1,5},{2,6},{3,7},{4,0},{5,1},{6,2},{7,3},{8,12},{9,13},{10,... | collective-permute-start | bytes 798728 | tf_op jit(solution)/shard_map/ppermute | solution.py:450
  41.3 1.1 collective-permute-start.5
  42.4 4.6 %collective-permute-done.3.refs_1_ = f32[520,128]{1,0:T(8,128)S(1)} collective-permute-done((f32[520,128]{1,0:T(8,128)S(1)}, f32[520,128]{1,0:T(8,128)S(1)}, u32[]{:S(2)}, u32[]{:S(2)}) %collective-permute-start.3) | collective-permute-done | bytes 266272 | tf_op jit(solution)/shard_map/ppermute | solution.py:450
  47.0 5.3 %collective-permute-done.4.refs_2_ = f32[520,128]{1,0:T(8,128)S(1)} collective-permute-done((f32[520,128]{1,0:T(8,128)S(1)}, f32[520,128]{1,0:T(8,128)S(1)}, u32[]{:S(2)}, u32[]{:S(2)}) %collective-permute-start.4) | collective-permute-done | bytes 266272 | tf_op jit(solution)/shard_map/ppermute | solution.py:450
  52.3 1.4 collective-permute-done.5.refs_3_
  53.6 0.1 run.3
  53.8 0.4 collective-permute-start.6
  54.1 2.0 %forward.4 = (f32[4,8,128,128]{3,2,1,0:T(8,128)S(1)}, f32[264,128]{1,0:T(8,128)S(1)}, f32[264,128]{1,0:T(8,128)S(1)}, f32[264,128]{1,0:T(8,128)S(1)}, f32[264,128]{1,0:T(8,128)S(1)}, /*index=5*/f32[8,128]{1,0:T(8,128)S(1)}) custom-call(f32[2,2,4,512,128]{4,3,2,1,0:T(8,128)S(1)} %get-tuple-element.77.refs_0_.refs_5_, ...), custom_call_target="tpu_custom_call" | custom-call | tf_op jit(solution)/shard_map/forward/pallas_call | solution.py:95
  56.1 1.8 %collective-permute-start.10 = (f32[264,128]{1,0:T(8,128)S(1)}, f32[264,128]{1,0:T(8,128)S(1)}, u32[]{:S(2)}, u32[]{:S(2)}) collective-permute-start(f32[264,128]{1,0:T(8,128)S(1)} %get-tuple-element.96), channel_id=1, source_target_pairs={{0,2},{1,3},{2,4},{3,5},{4,6},{5,7},{6,0},{7,1},{8,10},{9,11},{10,... | collective-permute-start | bytes 405512 | tf_op jit(solution)/shard_map/ppermute | solution.py:450
  58.0 2.8 %collective-permute-start.11 = (f32[264,128]{1,0:T(8,128)S(1)}, f32[264,128]{1,0:T(8,128)S(1)}, u32[]{:S(2)}, u32[]{:S(2)}) collective-permute-start(f32[264,128]{1,0:T(8,128)S(1)} %get-tuple-element.97), channel_id=1, source_target_pairs={{0,4},{1,5},{2,6},{3,7},{4,0},{5,1},{6,2},{7,3},{8,12},{9,13},{10,... | collective-permute-start | bytes 405512 | tf_op jit(solution)/shard_map/ppermute | solution.py:450
  60.8 8.8 %collective-permute-done.6.refs_1_.refs_4_ = f32[520,128]{1,0:T(8,128)S(1)} collective-permute-done((f32[520,128]{1,0:T(8,128)S(1)}, f32[520,128]{1,0:T(8,128)S(1)}, u32[]{:S(2)}, u32[]{:S(2)}) %collective-permute-start.6) | collective-permute-done | bytes 266272 | tf_op jit(solution)/shard_map/ppermute | solution.py:450
  69.7 3.2 %collective-permute-start.15 = (f32[520,128]{1,0:T(8,128)S(1)}, f32[520,128]{1,0:T(8,128)S(1)}, u32[]{:S(2)}, u32[]{:S(2)}) collective-permute-start(f32[520,128]{1,0:T(8,128)S(1)} %get-tuple-element.103.refs_5_), channel_id=1, source_target_pairs={{0,16},{1,17},{2,18},{3,19},{4,20},{5,21},{6,22},{7,23},{8,24},{9,... | collective-permute-start | bytes 798728 | tf_op jit(solution)/shard_map/ppermute | solution.py:450
  72.9 1.1 collective-permute-start.12
  74.0 2.0 %forward.5 = (f32[4,8,128,128]{3,2,1,0:T(8,128)S(1)}, f32[264,128]{1,0:T(8,128)S(1)}, f32[264,128]{1,0:T(8,128)S(1)}, f32[264,128]{1,0:T(8,128)S(1)}, f32[264,128]{1,0:T(8,128)S(1)}, /*index=5*/f32[8,128]{1,0:T(8,128)S(1)}) custom-call(f32[2,2,4,512,128]{4,3,2,1,0:T(8,128)S(1)} %get-tuple-element.77.refs_0_.refs_5_, ...), custom_call_target="tpu_custom_call" | custom-call | tf_op jit(solution)/shard_map/forward/pallas_call | solution.py:95
  76.0 0.5 collective-permute-start.7
  76.5 1.2 collective-permute-start.8
  77.7 1.3 collective-permute-start.9
  79.0 1.7 collective-permute-start.14
  80.8 1.3 collective-permute-done.7.refs_1_
  82.0 1.4 collective-permute-done.8.refs_2_
  83.4 0.4 collective-permute-done.9.refs_3_
  83.9 0.3 collective-permute-done.15.refs_6_
  84.2 0.3 edges.3
  84.5 3.5 %collective-permute-start.17 = (f32[520,128]{1,0:T(8,128)S(1)}, f32[520,128]{1,0:T(8,128)S(1)}, u32[]{:S(2)}, u32[]{:S(2)}) collective-permute-start(f32[520,128]{1,0:T(8,128)S(1)} %get-tuple-element.110), channel_id=1, source_target_pairs={{0,6},{1,7},{2,0},{3,1},{4,2},{5,3},{6,4},{7,5},{8,14},{9,15},{10,... | collective-permute-start | bytes 798728 | tf_op jit(solution)/shard_map/ppermute | solution.py:450
  88.1 2.8 %collective-permute-start.20 = (f32[264,128]{1,0:T(8,128)S(1)}, f32[264,128]{1,0:T(8,128)S(1)}, u32[]{:S(2)}, u32[]{:S(2)}) collective-permute-start(f32[264,128]{1,0:T(8,128)S(1)} %get-tuple-element.113.refs_5_), channel_id=1, source_target_pairs={{0,16},{1,17},{2,18},{3,19},{4,20},{5,21},{6,22},{7,23},{8,24},{9,... | collective-permute-start | bytes 405512 | tf_op jit(solution)/shard_map/ppermute | solution.py:450
  90.9 0.4 collective-permute-start.19
  91.3 0.8 collective-permute-done.13.refs_1_.refs_4_
  92.2 1.4 collective-permute-start.16
  93.6 1.5 collective-permute-done.20.refs_6_
  95.1 0.2 edges.4
  95.3 2.0 %collective-permute-start.24 = (f32[264,128]{1,0:T(8,128)S(1)}, f32[264,128]{1,0:T(8,128)S(1)}, u32[]{:S(2)}, u32[]{:S(2)}) collective-permute-start(f32[264,128]{1,0:T(8,128)S(1)} %get-tuple-element.123), channel_id=1, source_target_pairs={{0,6},{1,7},{2,0},{3,1},{4,2},{5,3},{6,4},{7,5},{8,14},{9,15},{10,... | collective-permute-start | bytes 405512 | tf_op jit(solution)/shard_map/ppermute | solution.py:450
  97.2 1.4 collective-permute-done.17.refs_2_
  98.6 4.1 %collective-permute-start.26 = (f32[264,128]{1,0:T(8,128)S(1)}, f32[264,128]{1,0:T(8,128)S(1)}, u32[]{:S(2)}, u32[]{:S(2)}) collective-permute-start(f32[264,128]{1,0:T(8,128)S(1)} %get-tuple-element.125), channel_id=1, source_target_pairs={{0,2},{1,3},{2,4},{3,5},{4,6},{5,7},{6,0},{7,1},{8,10},{9,11},{10,... | collective-permute-start | bytes 405512 | tf_op jit(solution)/shard_map/ppermute | solution.py:450
  102.7 4.2 %backward.3 = (f32[2,2,512,128]{3,2,1,0:T(8,128)S(1)}, f32[1,4,512,128]{3,2,1,0:T(8,128)S(1)}, f32[1,4,512,128]{3,2,1,0:T(8,128)S(1)}, f32[8,128]{1,0:T(8,128)S(1)}) custom-call(f32[8,8,128,128]{3,2,1,0:T(8,128)S(1)} %get-tuple-element.108.refs_0_, f32[520,128]{1,0:T(8,128)S(1)} %get-tuple-element.109.refs_1_, ...), custom_call_target="tpu_custom_call" | custom-call | tf_op jit(solution)/shard_map/backward/pallas_call | solution.py:95
  106.9 0.2 edges.5
  107.1 2.0 %backward.4 = (f32[2,1,512,128]{3,2,1,0:T(8,128)S(1)}, f32[1,4,512,128]{3,2,1,0:T(8,128)S(1)}, f32[1,4,512,128]{3,2,1,0:T(8,128)S(1)}, f32[8,128]{1,0:T(8,128)S(1)}) custom-call(f32[4,8,128,128]{3,2,1,0:T(8,128)S(1)} %get-tuple-element.121.refs_0_, f32[264,128]{1,0:T(8,128)S(1)} %get-tuple-element.122.refs_1_, ...), custom_call_target="tpu_custom_call" | custom-call | tf_op jit(solution)/shard_map/backward/pallas_call | solution.py:95
  109.2 6.3 %collective-permute-start.27 = (f32[2,1,512,128]{3,2,1,0:T(8,128)S(1)}, f32[2,1,512,128]{3,2,1,0:T(8,128)S(1)}, u32[]{:S(2)}, u32[]{:S(2)}) collective-permute-start(f32[2,1,512,128]{3,2,1,0:T(8,128)S(1)} %get-tuple-element.131), channel_id=1, source_target_pairs={{0,224},{1,225},{2,226},{3,227},{4,228},{5,229},{6,230},{7,231},{8... | collective-permute-start | bytes 1572872 | tf_op jit(solution)/shard_map/ppermute | solution.py:450
  115.5 1.5 collective-permute-start.23
  116.9 2.4 %collective-permute-done.21.refs_2_ = f32[264,128]{1,0:T(8,128)S(1)} collective-permute-done((f32[264,128]{1,0:T(8,128)S(1)}, f32[264,128]{1,0:T(8,128)S(1)}, u32[]{:S(2)}, u32[]{:S(2)}) %collective-permute-start.21) | collective-permute-done | bytes 135200 | tf_op jit(solution)/shard_map/ppermute | solution.py:450
  119.3 1.6 collective-permute-done.22.refs_3_
  120.9 1.7 collective-permute-done.23.refs_4_
  122.6 1.0 collective-permute-done.27.refs_15_.refs_4_
  123.6 2.1 %backward.5 = (f32[2,1,512,128]{3,2,1,0:T(8,128)S(1)}, f32[1,4,512,128]{3,2,1,0:T(8,128)S(1)}, f32[2,4,512,128]{3,2,1,0:T(8,128)S(1)}, f32[8,128]{1,0:T(8,128)S(1)}) custom-call(f32[4,8,128,128]{3,2,1,0:T(8,128)S(1)} %get-tuple-element.90.refs_0_, f32[264,128]{1,0:T(8,128)S(1)} %get-tuple-element.117.refs_1_, ...), custom_call_target="tpu_custom_call" | custom-call | tf_op jit(solution)/shard_map/backward/pallas_call | solution.py:95
  125.7 14.2 %collective-permute-start.28 = (f32[2,4,512,128]{3,2,1,0:T(8,128)S(1)}, f32[2,4,512,128]{3,2,1,0:T(8,128)S(1)}, u32[]{:S(2)}, u32[]{:S(2)}) collective-permute-start(f32[2,4,512,128]{3,2,1,0:T(8,128)S(1)} %get-tuple-element.134), channel_id=1, source_target_pairs={{0,1},{1,0},{2,3},{3,2},{4,5},{5,4},{6,7},{7,6},{8,9},{9,8},{10,11... | collective-permute-start | bytes 6291464 | tf_op jit(solution)/shard_map/ppermute | solution.py:450
  139.9 8.4 %collective-permute-start.32 = (f32[2,1,512,128]{3,2,1,0:T(8,128)S(1)}, f32[2,1,512,128]{3,2,1,0:T(8,128)S(1)}, u32[]{:S(2)}, u32[]{:S(2)}) collective-permute-start(f32[2,1,512,128]{3,2,1,0:T(8,128)S(1)} %get-tuple-element.138), channel_id=1, source_target_pairs={{0,224},{1,225},{2,226},{3,227},{4,228},{5,229},{6,230},{7,231},{8... | collective-permute-start | bytes 1572872 | tf_op jit(solution)/shard_map/ppermute | solution.py:450
  148.5 0.4 collective-permute-start.29
  149.0 21.6 %collective-permute-done.32.refs_2_ = f32[2,1,512,128]{3,2,1,0:T(8,128)S(1)} collective-permute-done((f32[2,1,512,128]{3,2,1,0:T(8,128)S(1)}, f32[2,1,512,128]{3,2,1,0:T(8,128)S(1)}, u32[]{:S(2)}, u32[]{:S(2)}) %collective-permute-start.32) | collective-permute-done | bytes 524320 | tf_op jit(solution)/shard_map/ppermute | solution.py:450
  170.6 1.0 collective-permute-start.33
  171.6 2.9 %collective-permute-done.31.refs_7_ = f32[1,2,512,128]{3,2,1,0:T(8,128)S(1)} collective-permute-done((f32[1,2,512,128]{3,2,1,0:T(8,128)S(1)}, f32[1,2,512,128]{3,2,1,0:T(8,128)S(1)}, u32[]{:S(2)}, u32[]{:S(2)}) %collective-permute-start.31) | collective-permute-done | bytes 524320 | tf_op jit(solution)/shard_map/ppermute | solution.py:450
  174.5 1.1 add_early.1
  175.6 1.9 %add_late.1 = (f32[8,512,128]{2,1,0:T(8,128)}, f32[8,128]{1,0:T(8,128)}) custom-call(s32[4]{0:T(128)S(1)} %get-tuple-element.75.refs_0_, f32[8,512,128]{2,1,0:T(8,128)S(1)} %get-tuple-element.137.refs_1_, f32[2,1,512,128]{3,2,1,0:T(8,128)S(1)} %collective-permute-done.32.refs_2_, f32[1,1,512,128]{3,2,1,0:T(8,128)S(1)} %collective-permute-done.33.refs_3_, ...), custom_call_target="tpu_custom_call" | custom-call | tf_op jit(solution)/shard_map/add_late/pallas_call | solution.py:95
  (51 shorter events, 0.7 us)
Async XLA Ops:
  0.0 6.3 %copy-start.10 = (s32[2,8,2]{1,2,0:T(2,128)S(1)}, s32[2,8,2]{1,2,0:T(2,128)}, u32[]{:S(2)}) copy-start(s32[2,8,2]{1,2,0:T(2,128)} %param.10) | copy-start | bytes 388
  0.0 7.2 %collective-permute-start = (f32[8,512,128]{2,1,0:T(8,128)}, f32[8,512,128]{2,1,0:T(8,128)S(1)}, u32[]{:S(2)}, u32[]{:S(2)}) collective-permute-start(f32[8,512,128]{2,1,0:T(8,128)} %bitcast.10), channel_id=1, source_target_pairs={{0,1},{1,0},{2,3},{3,2},{4,5},{5,4},{6,7},{7,6},{8,9},{9,8},{10,11... | collective-permute-start | bytes 6291464 | tf_op jit(solution)/shard_map/ppermute | solution.py:450
  3.2 1.6 copy-start.7
  5.0 1.3 copy-start.1
  7.2 1.6 copy-start.2
  10.3 24.5 %collective-permute-start.2 = (f32[2,2,512,128]{3,2,1,0:T(8,128)S(1)}, f32[2,2,512,128]{3,2,1,0:T(8,128)S(1)}, u32[]{:S(2)}, u32[]{:S(2)}) collective-permute-start(f32[2,2,512,128]{3,2,1,0:T(8,128)S(1)} %get-tuple-element.79), channel_id=1, source_target_pairs={{0,192},{1,193},{2,194},{3,195},{4,196},{5,197},{6,198},{7,199},{8... | collective-permute-start | bytes 3145736 | tf_op jit(solution)/shard_map/ppermute | solution.py:450
  11.1 43.0 %collective-permute-start.1 = (f32[2,2,512,128]{3,2,1,0:T(8,128)S(1)}, f32[2,2,512,128]{3,2,1,0:T(8,128)S(1)}, u32[]{:S(2)}, u32[]{:S(2)}) collective-permute-start(f32[2,2,512,128]{3,2,1,0:T(8,128)S(1)} %get-tuple-element.78), channel_id=1, source_target_pairs={{0,32},{1,33},{2,34},{3,35},{4,36},{5,37},{6,38},{7,39},{8,40},{9,... | collective-permute-start | bytes 3145736 | tf_op jit(solution)/shard_map/ppermute | solution.py:450
  18.0 16.7 %copy-start.4 = (bf16[256,256]{1,0:T(8,128)(2,1)S(1)}, bf16[256,256]{1,0:T(8,128)(2,1)}, u32[]{:S(2)}) copy-start(bf16[256,256]{1,0:T(8,128)(2,1)} %constant.16.clone.refs_2_.refs_7_) | copy-start | bytes 393220
  18.0 16.7 %copy-start.5 = (bf16[256,256]{1,0:T(8,128)(2,1)S(1)}, bf16[256,256]{1,0:T(8,128)(2,1)}, u32[]{:S(2)}) copy-start(bf16[256,256]{1,0:T(8,128)(2,1)} %constant.17.clone.refs_3_.refs_8_) | copy-start | bytes 393220
  18.0 16.7 %copy-start.6 = (f32[128,128]{1,0:T(8,128)S(1)}, f32[128,128]{1,0:T(8,128)}, u32[]{:S(2)}) copy-start(f32[128,128]{1,0:T(8,128)} %constant.18.clone.refs_4_.refs_9_) | copy-start | bytes 196612
  18.0 16.7 %copy-start.8 = (f32[128,128]{1,0:T(8,128)S(1)}, f32[128,128]{1,0:T(8,128)}, u32[]{:S(2)}) copy-start(f32[128,128]{1,0:T(8,128)} %constant.19.clone.refs_5_) | copy-start | bytes 196612
  34.8 18.8 %copy-start = (f32[4,128,128]{2,1,0:T(8,128)S(1)}, f32[4,128,128]{2,1,0:T(8,128)}, u32[]{:S(2)}) copy-start(f32[4,128,128]{2,1,0:T(8,128)} %constant.20.clone.refs_4_.refs_7_) | copy-start | bytes 786436
  38.8 8.2 %collective-permute-start.3 = (f32[520,128]{1,0:T(8,128)S(1)}, f32[520,128]{1,0:T(8,128)S(1)}, u32[]{:S(2)}, u32[]{:S(2)}) collective-permute-start(f32[520,128]{1,0:T(8,128)S(1)} %get-tuple-element.82), channel_id=1, source_target_pairs={{0,2},{1,3},{2,4},{3,5},{4,6},{5,7},{6,0},{7,1},{8,10},{9,11},{10,... | collective-permute-start | bytes 798728 | tf_op jit(solution)/shard_map/ppermute | solution.py:450
  38.8 13.4 %collective-permute-start.4 = (f32[520,128]{1,0:T(8,128)S(1)}, f32[520,128]{1,0:T(8,128)S(1)}, u32[]{:S(2)}, u32[]{:S(2)}) collective-permute-start(f32[520,128]{1,0:T(8,128)S(1)} %get-tuple-element.83), channel_id=1, source_target_pairs={{0,4},{1,5},{2,6},{3,7},{4,0},{5,1},{6,2},{7,3},{8,12},{9,13},{10,... | collective-permute-start | bytes 798728 | tf_op jit(solution)/shard_map/ppermute | solution.py:450
  41.3 12.3 %collective-permute-start.5 = (f32[520,128]{1,0:T(8,128)S(1)}, f32[520,128]{1,0:T(8,128)S(1)}, u32[]{:S(2)}, u32[]{:S(2)}) collective-permute-start(f32[520,128]{1,0:T(8,128)S(1)} %get-tuple-element.84), channel_id=1, source_target_pairs={{0,6},{1,7},{2,0},{3,1},{4,2},{5,3},{6,4},{7,5},{8,14},{9,15},{10,... | collective-permute-start | bytes 798728 | tf_op jit(solution)/shard_map/ppermute | solution.py:450
  53.8 15.9 %collective-permute-start.6 = (f32[520,128]{1,0:T(8,128)S(1)}, f32[520,128]{1,0:T(8,128)S(1)}, u32[]{:S(2)}, u32[]{:S(2)}) collective-permute-start(f32[520,128]{1,0:T(8,128)S(1)} %get-tuple-element.86.refs_0_), channel_id=1, source_target_pairs={{0,8},{1,9},{2,10},{3,11},{4,12},{5,13},{6,14},{7,15},{8,0},{9,1},... | collective-permute-start | bytes 798728 | tf_op jit(solution)/shard_map/ppermute | solution.py:450
  54.1 15.5 %copy-start.3 = (f32[3,128,128]{2,1,0:T(8,128)S(1)}, f32[3,128,128]{2,1,0:T(8,128)}, u32[]{:S(2)}) copy-start(f32[3,128,128]{2,1,0:T(8,128)} %constant.21.clone.refs_2_.refs_8_) | copy-start | bytes 589828
  56.1 20.3 %collective-permute-start.10 = (f32[264,128]{1,0:T(8,128)S(1)}, f32[264,128]{1,0:T(8,128)S(1)}, u32[]{:S(2)}, u32[]{:S(2)}) collective-permute-start(f32[264,128]{1,0:T(8,128)S(1)} %get-tuple-element.96), channel_id=1, source_target_pairs={{0,2},{1,3},{2,4},{3,5},{4,6},{5,7},{6,0},{7,1},{8,10},{9,11},{10,... | collective-permute-start | bytes 405512 | tf_op jit(solution)/shard_map/ppermute | solution.py:450
  58.0 19.7 %collective-permute-start.11 = (f32[264,128]{1,0:T(8,128)S(1)}, f32[264,128]{1,0:T(8,128)S(1)}, u32[]{:S(2)}, u32[]{:S(2)}) collective-permute-start(f32[264,128]{1,0:T(8,128)S(1)} %get-tuple-element.97), channel_id=1, source_target_pairs={{0,4},{1,5},{2,6},{3,7},{4,0},{5,1},{6,2},{7,3},{8,12},{9,13},{10,... | collective-permute-start | bytes 405512 | tf_op jit(solution)/shard_map/ppermute | solution.py:450
  69.7 14.5 %collective-permute-start.15 = (f32[520,128]{1,0:T(8,128)S(1)}, f32[520,128]{1,0:T(8,128)S(1)}, u32[]{:S(2)}, u32[]{:S(2)}) collective-permute-start(f32[520,128]{1,0:T(8,128)S(1)} %get-tuple-element.103.refs_5_), channel_id=1, source_target_pairs={{0,16},{1,17},{2,18},{3,19},{4,20},{5,21},{6,22},{7,23},{8,24},{9,... | collective-permute-start | bytes 798728 | tf_op jit(solution)/shard_map/ppermute | solution.py:450
  72.9 6.0 %collective-permute-start.12 = (f32[264,128]{1,0:T(8,128)S(1)}, f32[264,128]{1,0:T(8,128)S(1)}, u32[]{:S(2)}, u32[]{:S(2)}) collective-permute-start(f32[264,128]{1,0:T(8,128)S(1)} %get-tuple-element.98), channel_id=1, source_target_pairs={{0,6},{1,7},{2,0},{3,1},{4,2},{5,3},{6,4},{7,5},{8,14},{9,15},{10,... | collective-permute-start | bytes 405512 | tf_op jit(solution)/shard_map/ppermute | solution.py:450
  76.0 6.0 %collective-permute-start.7 = (f32[264,128]{1,0:T(8,128)S(1)}, f32[264,128]{1,0:T(8,128)S(1)}, u32[]{:S(2)}, u32[]{:S(2)}) collective-permute-start(f32[264,128]{1,0:T(8,128)S(1)} %get-tuple-element.92), channel_id=1, source_target_pairs={{0,2},{1,3},{2,4},{3,5},{4,6},{5,7},{6,0},{7,1},{8,10},{9,11},{10,... | collective-permute-start | bytes 405512 | tf_op jit(solution)/shard_map/ppermute | solution.py:450
  76.5 7.0 %collective-permute-start.8 = (f32[264,128]{1,0:T(8,128)S(1)}, f32[264,128]{1,0:T(8,128)S(1)}, u32[]{:S(2)}, u32[]{:S(2)}) collective-permute-start(f32[264,128]{1,0:T(8,128)S(1)} %get-tuple-element.93), channel_id=1, source_target_pairs={{0,4},{1,5},{2,6},{3,7},{4,0},{5,1},{6,2},{7,3},{8,12},{9,13},{10,... | collective-permute-start | bytes 405512 | tf_op jit(solution)/shard_map/ppermute | solution.py:450
  77.7 6.2 %collective-permute-start.9 = (f32[264,128]{1,0:T(8,128)S(1)}, f32[264,128]{1,0:T(8,128)S(1)}, u32[]{:S(2)}, u32[]{:S(2)}) collective-permute-start(f32[264,128]{1,0:T(8,128)S(1)} %get-tuple-element.94), channel_id=1, source_target_pairs={{0,6},{1,7},{2,0},{3,1},{4,2},{5,3},{6,4},{7,5},{8,14},{9,15},{10,... | collective-permute-start | bytes 405512 | tf_op jit(solution)/shard_map/ppermute | solution.py:450
  79.0 9.0 %collective-permute-start.14 = (f32[264,128]{1,0:T(8,128)S(1)}, f32[264,128]{1,0:T(8,128)S(1)}, u32[]{:S(2)}, u32[]{:S(2)}) collective-permute-start(f32[264,128]{1,0:T(8,128)S(1)} %get-tuple-element.102.refs_0_), channel_id=1, source_target_pairs={{0,8},{1,9},{2,10},{3,11},{4,12},{5,13},{6,14},{7,15},{8,0},{9,1},... | collective-permute-start | bytes 405512 | tf_op jit(solution)/shard_map/ppermute | solution.py:450
  84.2 18.6 %copy-start.9 = (f32[1,128]{1,0:T(1,128)S(1)}, f32[1,128]{1,0:T(1,128)}, u32[]{:S(2)}) copy-start(f32[1,128]{1,0:T(1,128)} %constant.22.clone.refs_10_) | copy-start | bytes 1540
  84.5 14.1 %collective-permute-start.17 = (f32[520,128]{1,0:T(8,128)S(1)}, f32[520,128]{1,0:T(8,128)S(1)}, u32[]{:S(2)}, u32[]{:S(2)}) collective-permute-start(f32[520,128]{1,0:T(8,128)S(1)} %get-tuple-element.110), channel_id=1, source_target_pairs={{0,6},{1,7},{2,0},{3,1},{4,2},{5,3},{6,4},{7,5},{8,14},{9,15},{10,... | collective-permute-start | bytes 798728 | tf_op jit(solution)/shard_map/ppermute | solution.py:450
  88.0 10.6 %collective-permute-start.18 = (f32[520,128]{1,0:T(8,128)S(1)}, f32[520,128]{1,0:T(8,128)S(1)}, u32[]{:S(2)}, u32[]{:S(2)}) collective-permute-start(f32[520,128]{1,0:T(8,128)S(1)} %get-tuple-element.111), channel_id=1, source_target_pairs={{0,4},{1,5},{2,6},{3,7},{4,0},{5,1},{6,2},{7,3},{8,12},{9,13},{10,... | collective-permute-start | bytes 798728 | tf_op jit(solution)/shard_map/ppermute | solution.py:450
  88.0 4.2 %collective-permute-start.13 = (f32[264,128]{1,0:T(8,128)S(1)}, f32[264,128]{1,0:T(8,128)S(1)}, u32[]{:S(2)}, u32[]{:S(2)}) collective-permute-start(f32[264,128]{1,0:T(8,128)S(1)} %get-tuple-element.101.refs_0_), channel_id=1, source_target_pairs={{0,8},{1,9},{2,10},{3,11},{4,12},{5,13},{6,14},{7,15},{8,0},{9,1},... | collective-permute-start | bytes 405512 | tf_op jit(solution)/shard_map/ppermute | solution.py:450
  88.1 7.0 %collective-permute-start.20 = (f32[264,128]{1,0:T(8,128)S(1)}, f32[264,128]{1,0:T(8,128)S(1)}, u32[]{:S(2)}, u32[]{:S(2)}) collective-permute-start(f32[264,128]{1,0:T(8,128)S(1)} %get-tuple-element.113.refs_5_), channel_id=1, source_target_pairs={{0,16},{1,17},{2,18},{3,19},{4,20},{5,21},{6,22},{7,23},{8,24},{9,... | collective-permute-start | bytes 405512 | tf_op jit(solution)/shard_map/ppermute | solution.py:450
  90.9 11.8 %collective-permute-start.19 = (f32[520,128]{1,0:T(8,128)S(1)}, f32[520,128]{1,0:T(8,128)S(1)}, u32[]{:S(2)}, u32[]{:S(2)}) collective-permute-start(f32[520,128]{1,0:T(8,128)S(1)} %get-tuple-element.112), channel_id=1, source_target_pairs={{0,2},{1,3},{2,4},{3,5},{4,6},{5,7},{6,0},{7,1},{8,10},{9,11},{10,... | collective-permute-start | bytes 798728 | tf_op jit(solution)/shard_map/ppermute | solution.py:450
  92.2 14.7 %collective-permute-start.16 = (f32[264,128]{1,0:T(8,128)S(1)}, f32[264,128]{1,0:T(8,128)S(1)}, u32[]{:S(2)}, u32[]{:S(2)}) collective-permute-start(f32[264,128]{1,0:T(8,128)S(1)} %get-tuple-element.107.refs_5_), channel_id=1, source_target_pairs={{0,16},{1,17},{2,18},{3,19},{4,20},{5,21},{6,22},{7,23},{8,24},{9,... | collective-permute-start | bytes 405512 | tf_op jit(solution)/shard_map/ppermute | solution.py:450
  95.3 11.9 %collective-permute-start.24 = (f32[264,128]{1,0:T(8,128)S(1)}, f32[264,128]{1,0:T(8,128)S(1)}, u32[]{:S(2)}, u32[]{:S(2)}) collective-permute-start(f32[264,128]{1,0:T(8,128)S(1)} %get-tuple-element.123), channel_id=1, source_target_pairs={{0,6},{1,7},{2,0},{3,1},{4,2},{5,3},{6,4},{7,5},{8,14},{9,15},{10,... | collective-permute-start | bytes 405512 | tf_op jit(solution)/shard_map/ppermute | solution.py:450
  98.6 8.5 %collective-permute-start.25 = (f32[264,128]{1,0:T(8,128)S(1)}, f32[264,128]{1,0:T(8,128)S(1)}, u32[]{:S(2)}, u32[]{:S(2)}) collective-permute-start(f32[264,128]{1,0:T(8,128)S(1)} %get-tuple-element.124), channel_id=1, source_target_pairs={{0,4},{1,5},{2,6},{3,7},{4,0},{5,1},{6,2},{7,3},{8,12},{9,13},{10,... | collective-permute-start | bytes 405512 | tf_op jit(solution)/shard_map/ppermute | solution.py:450
  98.6 8.5 %collective-permute-start.26 = (f32[264,128]{1,0:T(8,128)S(1)}, f32[264,128]{1,0:T(8,128)S(1)}, u32[]{:S(2)}, u32[]{:S(2)}) collective-permute-start(f32[264,128]{1,0:T(8,128)S(1)} %get-tuple-element.125), channel_id=1, source_target_pairs={{0,2},{1,3},{2,4},{3,5},{4,6},{5,7},{6,0},{7,1},{8,10},{9,11},{10,... | collective-permute-start | bytes 405512 | tf_op jit(solution)/shard_map/ppermute | solution.py:450
  109.2 14.4 %collective-permute-start.27 = (f32[2,1,512,128]{3,2,1,0:T(8,128)S(1)}, f32[2,1,512,128]{3,2,1,0:T(8,128)S(1)}, u32[]{:S(2)}, u32[]{:S(2)}) collective-permute-start(f32[2,1,512,128]{3,2,1,0:T(8,128)S(1)} %get-tuple-element.131), channel_id=1, source_target_pairs={{0,224},{1,225},{2,226},{3,227},{4,228},{5,229},{6,230},{7,231},{8... | collective-permute-start | bytes 1572872 | tf_op jit(solution)/shard_map/ppermute | solution.py:450
  115.5 3.9 %collective-permute-start.21 = (f32[264,128]{1,0:T(8,128)S(1)}, f32[264,128]{1,0:T(8,128)S(1)}, u32[]{:S(2)}, u32[]{:S(2)}) collective-permute-start(f32[264,128]{1,0:T(8,128)S(1)} %get-tuple-element.118), channel_id=1, source_target_pairs={{0,6},{1,7},{2,0},{3,1},{4,2},{5,3},{6,4},{7,5},{8,14},{9,15},{10,... | collective-permute-start | bytes 405512 | tf_op jit(solution)/shard_map/ppermute | solution.py:450
  115.5 5.4 %collective-permute-start.22 = (f32[264,128]{1,0:T(8,128)S(1)}, f32[264,128]{1,0:T(8,128)S(1)}, u32[]{:S(2)}, u32[]{:S(2)}) collective-permute-start(f32[264,128]{1,0:T(8,128)S(1)} %get-tuple-element.119), channel_id=1, source_target_pairs={{0,4},{1,5},{2,6},{3,7},{4,0},{5,1},{6,2},{7,3},{8,12},{9,13},{10,... | collective-permute-start | bytes 405512 | tf_op jit(solution)/shard_map/ppermute | solution.py:450
  115.5 7.1 %collective-permute-start.23 = (f32[264,128]{1,0:T(8,128)S(1)}, f32[264,128]{1,0:T(8,128)S(1)}, u32[]{:S(2)}, u32[]{:S(2)}) collective-permute-start(f32[264,128]{1,0:T(8,128)S(1)} %get-tuple-element.120), channel_id=1, source_target_pairs={{0,2},{1,3},{2,4},{3,5},{4,6},{5,7},{6,0},{7,1},{8,10},{9,11},{10,... | collective-permute-start | bytes 405512 | tf_op jit(solution)/shard_map/ppermute | solution.py:450
  125.7 48.9 %collective-permute-start.28 = (f32[2,4,512,128]{3,2,1,0:T(8,128)S(1)}, f32[2,4,512,128]{3,2,1,0:T(8,128)S(1)}, u32[]{:S(2)}, u32[]{:S(2)}) collective-permute-start(f32[2,4,512,128]{3,2,1,0:T(8,128)S(1)} %get-tuple-element.134), channel_id=1, source_target_pairs={{0,1},{1,0},{2,3},{3,2},{4,5},{5,4},{6,7},{7,6},{8,9},{9,8},{10,11... | collective-permute-start | bytes 6291464 | tf_op jit(solution)/shard_map/ppermute | solution.py:450
  139.9 30.7 %collective-permute-start.32 = (f32[2,1,512,128]{3,2,1,0:T(8,128)S(1)}, f32[2,1,512,128]{3,2,1,0:T(8,128)S(1)}, u32[]{:S(2)}, u32[]{:S(2)}) collective-permute-start(f32[2,1,512,128]{3,2,1,0:T(8,128)S(1)} %get-tuple-element.138), channel_id=1, source_target_pairs={{0,224},{1,225},{2,226},{3,227},{4,228},{5,229},{6,230},{7,231},{8... | collective-permute-start | bytes 1572872 | tf_op jit(solution)/shard_map/ppermute | solution.py:450
  148.3 23.3 %collective-permute-start.30 = (f32[1,2,512,128]{3,2,1,0:T(8,128)S(1)}, f32[1,2,512,128]{3,2,1,0:T(8,128)S(1)}, u32[]{:S(2)}, u32[]{:S(2)}) collective-permute-start(f32[1,2,512,128]{3,2,1,0:T(8,128)S(1)} %get-tuple-element.142), channel_id=1, source_target_pairs={{0,64},{1,65},{2,66},{3,67},{4,68},{5,69},{6,70},{7,71},{8,72},{9,... | collective-permute-start | bytes 1572872 | tf_op jit(solution)/shard_map/ppermute | solution.py:450
  148.4 26.1 %collective-permute-start.31 = (f32[1,2,512,128]{3,2,1,0:T(8,128)S(1)}, f32[1,2,512,128]{3,2,1,0:T(8,128)S(1)}, u32[]{:S(2)}, u32[]{:S(2)}) collective-permute-start(f32[1,2,512,128]{3,2,1,0:T(8,128)S(1)} %get-tuple-element.141), channel_id=1, source_target_pairs={{0,65},{1,64},{2,67},{3,66},{4,69},{5,68},{6,71},{7,70},{8,73},{9,... | collective-permute-start | bytes 1572872 | tf_op jit(solution)/shard_map/ppermute | solution.py:450
  148.5 26.0 %collective-permute-start.29 = (f32[1,1,512,128]{3,2,1,0:T(8,128)S(1)}, f32[1,1,512,128]{3,2,1,0:T(8,128)S(1)}, u32[]{:S(2)}, u32[]{:S(2)}) collective-permute-start(f32[1,1,512,128]{3,2,1,0:T(8,128)S(1)} %slice.16), channel_id=1, source_target_pairs={{0,1},{1,0},{2,3},{3,2},{4,5},{5,4},{6,7},{7,6},{8,9},{9,8},{10,11... | collective-permute-start | bytes 786440 | tf_op jit(solution)/shard_map/ppermute | solution.py:450
  170.6 5.0 %collective-permute-start.33 = (f32[1,1,512,128]{3,2,1,0:T(8,128)S(1)}, f32[1,1,512,128]{3,2,1,0:T(8,128)S(1)}, u32[]{:S(2)}, u32[]{:S(2)}) collective-permute-start(f32[1,1,512,128]{3,2,1,0:T(8,128)S(1)} %slice.17), channel_id=1, source_target_pairs={{0,1},{1,0},{2,3},{3,2},{4,5},{5,4},{6,7},{7,6},{8,9},{9,8},{10,11... | collective-permute-start | bytes 786440 | tf_op jit(solution)/shard_map/ppermute | solution.py:450

commit v4 on v3

--- a/solution.py
+++ b/solution.py
@@ -85,8 +85,9 @@
 SMEM = pl.BlockSpec(memory_space=pltpu.SMEM)
 
 
-def launch(kernel, token, args, in_specs, out_specs, out_shape, name, limit, grid=(), scratch=(), after=()):
-    ins, outs, waits = len(args), len(out_shape), 1 + len(after)
+def launch(kernel, token, args, in_specs, out_specs, out_shape, name, limit, grid=(), scratch=(), after=(), work=0):
+    tokens = [] if token is None else [token]
+    ins, outs, waits = len(args), len(out_shape), len(tokens) + len(after)
     unread = pl.BlockSpec(memory_space=pl.ANY)
 
     def ordered(*refs):
@@ -98,11 +99,11 @@
         in_specs=[*in_specs, *[unread] * waits],
         out_specs=[*out_specs, unread],
         scratch_shapes=list(scratch),
-        out_shape=[*out_shape, array(token.shape)],
+        out_shape=[*out_shape, array((8, GRID))],
         compiler_params=pltpu.CompilerParams(vmem_limit_bytes=limit << 20),
-        cost_estimate=pl.CostEstimate(flops=0, bytes_accessed=0, transcendentals=0),
+        cost_estimate=pl.CostEstimate(flops=work, bytes_accessed=work // 256, transcendentals=0),
         name=name,
-    )(*args, token, *after)
+    )(*args, *tokens, *after)
     return result[:-1], result[-1]
 
 
@@ -122,20 +123,6 @@
         started.append(copy)
     for copy in started:
         copy.wait()
-
-
-def load_kernel(blocks, out, sem):
-    copy = pltpu.make_async_copy(blocks, out, sem)
-    copy.start()
-    copy.wait()
-
-
-def load(token, blocks):
-    (out,), token = launch(
-        load_kernel, token, [blocks], [HBM], [VMEM], [array(blocks.shape)], "load", 2,
-        scratch=[pltpu.SemaphoreType.DMA],
-    )
-    return out, token
 
 
 def pick_kernel(plan, own_a, own_b, index, first, second, sems):
@@ -154,10 +141,10 @@
     copy_all(copies, sems)
 
 
-def pick(token, plan, own):
+def pick(plan, own):
     two = array((CORES, HALF, ROWS, GRID))
     outs, token = launch(
-        pick_kernel, token, [plan, *own], [SMEM, VMEM, VMEM], [SMEM] + [VMEM] * 2,
+        pick_kernel, None, [plan, *own], [SMEM, HBM, VMEM], [SMEM] + [VMEM] * 2,
         [array((2 * ROUNDS,), jnp.int32), two, two], "pick", 2,
         scratch=[pltpu.SemaphoreType.DMA((2 * CORES,))],
     )
@@ -177,7 +164,7 @@
 
 def pick_own(token, index, own):
     (out,), token = launch(
-        pick_own_kernel, token, [index, *own], [SMEM, VMEM, VMEM], [VMEM],
+        pick_own_kernel, token, [index, *own], [SMEM, HBM, VMEM], [VMEM],
         [array((ROUNDS, CORES, SUB, ROWS, GRID))], "pick_own", 2,
         scratch=[pltpu.SemaphoreType.DMA((ROUNDS * CORES,))],
     )
@@ -347,15 +334,15 @@
             to_own = potential * part[source, member + j]
             added = to_part if added is None else added + to_part
             if prior:
-                own_out[0, i] = before[source][0, i] - to_own
+                own_out[i] = before[source][i] - to_own
             else:
-                own_out[0, i] = jnp.where(j == 0, 0.0, own_out[0, i]) - to_own
+                own_out[i] = jnp.where(j == 0, 0.0, own_out[i]) - to_own
         part_out[source, j] = -added
     if extra:
-        own_out_b[1] = before[prior][0]
-
-
-def backward(token, step, members, spec, edges, own, part, prior=(), extra=(), after=()):
+        own_out_b[SUB : 2 * SUB] = before[prior][...]
+
+
+def backward(token, step, members, spec, edges, own, part, prior=(), extra=()):
     right, left, decay, _, mean = tables()[:5]
     args = [spec, *edges, own, part, right, left, decay, mean, *prior, *extra]
     outs, token = launch(
@@ -366,45 +353,61 @@
         [VMEM] * 3,
         [
             array((CORES, len(members), ROWS, GRID)),
-            array((1, SUB, ROWS, GRID)),
-            array((1 + len(extra), SUB, ROWS, GRID)),
+            array((SUB, ROWS, GRID)),
+            array((2 * SUB if extra else SUB, ROWS, GRID)),
         ],
         "backward", 12, grid=(len(members),),
         scratch=[
             pltpu.VMEM((SUB, 2 * PLANES, GRID, GRID), F32),
             pltpu.VMEM((SUB * CORES, ROWS, GRID), F32),
         ],
-        after=after,
     )
     return outs[0], outs[1:], token
 
 
-def early_kernel(index, own_first, own_second, swapped, first, first_swapped, same, cross, out):
-    core = place()[2]
+def early_kernel(index, own_first, own_second, out):
     for i in range(SUB):
-        out[index[0] * SUB + i] = own_first[0, i] + swapped[0, i]
+        out[index[0] * SUB + i] = own_first[i]
         out[(NSUB - 1 - index[0]) * SUB + i] = jnp.zeros((ROWS, GRID), F32)
     for i in range(SUB):
         band = index[1] * SUB + i
-        out[band] = out[band] + (own_second[0, i] + swapped[1, i])
+        out[band] = out[band] + own_second[i]
+
+
+def add_early(token, index, terms):
+    (total,), token = launch(
+        early_kernel, token, [index, *terms], [SMEM] + [VMEM] * len(terms),
+        [VMEM], [array((NSUB * SUB, ROWS, GRID))], "add_early", 4, work=40_000_000_000,
+    )
+    return total, token
+
+
+def middle_kernel(index, total, swapped, same, cross, first_same, first_cross, out):
+    core = place()[2]
+    for band in range(NSUB * SUB):
+        out[band] = total[band]
+    for step in range(ROUNDS):
+        for i in range(SUB):
+            band = index[step] * SUB + i
+            out[band] = out[band] + swapped[step * SUB + i]
     for part, target in ((same, core), (cross, 1 - core)):
         for member in range(HALF):
             band = index[ROUNDS + 1] * SUB + target * HALF + member
             out[band] = out[band] + part[0, member]
-    for part, target in ((first, core), (first_swapped, 1 - core)):
+    for part, target in ((first_same, core), (first_cross, 1 - core)):
         band = index[ROUNDS] * SUB + target * HALF
         out[band] = out[band] + part[0, 0]
 
 
-def add_early(token, index, terms):
+def add_middle(token, index, terms):
     (total,), token = launch(
-        early_kernel, token, [index, *terms], [SMEM] + [VMEM] * len(terms),
-        [VMEM], [array((NSUB * SUB, ROWS, GRID))], "add_early", 4,
+        middle_kernel, token, [index, *terms], [SMEM] + [VMEM] * len(terms),
+        [VMEM], [array((NSUB * SUB, ROWS, GRID))], "add_middle", 4,
     )
     return total, token
 
 
-def late_kernel(index, total, same, swapped, out, fresh, sems):
+def late_kernel(index, total, same, cross, out, fresh, sems):
     core = place()[2]
     base = index[ROUNDS] * SUB
     other = (NSUB - 1) * SUB - base
@@ -415,7 +418,7 @@
     started = [pltpu.make_async_copy(*copy, sems.at[k]) for k, copy in enumerate(copies)]
     for copy in started:
         copy.start()
-    for k, (part, target) in enumerate(((same, core), (swapped, 1 - core))):
+    for k, (part, target) in enumerate(((same, core), (cross, 1 - core))):
         band = base + target * HALF + 1
         fresh[k] = total[band] + part[0, 0]
         copy = pltpu.make_async_copy(
@@ -455,6 +458,9 @@
     def shift(value, steps):
         return move(value, lambda b, z, y, c: (b + steps, z, y, c))
 
+    def there_and_across(values, steps):
+        return [shift(values[0], steps), move(values[1], lambda b, z, y, c: (b + steps, z, y, 1 - c))]
+
     def along_y(messages, sign):
         return [messages[0]] + [
             move(messages[k], lambda b, z, y, c, k=k: (b, z, y + YS + sign * k, c)) for k in range(1, YS)
@@ -463,10 +469,8 @@
     chips, runs = tables()[5:7]
     blocks = orbitals.reshape(NSUB * SUB, PLANES, GRID, GRID).transpose(0, 2, 1, 3)
     blocks = blocks.reshape(NSUB * SUB, ROWS, GRID)
-    swapped = swap_cores(blocks)
-    held, token = load(jnp.zeros((8, GRID), F32), blocks)
-    both = (held, swapped)
-    index, *sends, token = pick(token, plan, both)
+    both = (blocks, swap_cores(blocks))
+    index, *sends, token = pick(plan, both)
     parts = [shift(sends[0], 1), shift(sends[1], -2)]
     own, token = pick_own(token, index, both)
     chains = [{} for _ in CHAINS]
@@ -478,10 +482,10 @@
         chain["spec"], sums, token = forward(token, step, members, own, parts[step])
         chain["sums"] = along_y(sums, 1)
 
-    def run(at):
+    def run(at, after=()):
         nonlocal token
         chain = chains[at]
-        (chain["run"],), token = small(run_kernel, token, [*chain["sums"], chips], 1, "run")
+        (chain["run"],), token = small(run_kernel, token, [*chain["sums"], chips], 1, "run", after=after)
         chain["near"] = move(chain["run"], lambda b, z, y, c: (b, z ^ 1, y, c))
 
     def two(at):
@@ -499,12 +503,12 @@
         )
         chain["edges"] = along_y(outs, -1)
 
-    def finish(at, prior=(), extra=(), after=()):
+    def finish(at, prior=(), extra=()):
         nonlocal token
         step, members = CHAINS[at]
         chain = chains[at]
         terms, sums, token = backward(
-            token, step, members, chain["spec"], chain["edges"], own, parts[step], prior, extra, after
+            token, step, members, chain["spec"], chain["edges"], own, parts[step], prior, extra
         )
         return terms, sums
 
@@ -524,14 +528,13 @@
     edges(last)
     terms_a, sums_a = finish(first)
     back_a = shift(terms_a, -1)
-    terms_a, sums_a = finish(last, sums_a, sums_b[1:], [back_a])
-    back_b = [shift(terms_b[:1], 2), move(terms_b[1:], lambda b, z, y, c: (b + 2, z, y, 1 - c))]
-    total, token = add_early(
-        token, index,
-        [sums_a[0], sums_b[0], swap_cores(sums_a[1]), back_a, swap_cores(back_a[1:]), *back_b],
-    )
-    back_a = shift(terms_a, -1)
-    final = [back_a, swap_cores(back_a[1:])]
+    terms_a, sums_a = finish(last, sums_a, sums_b[1:])
+    final = there_and_across((terms_a[:1], terms_a[1:]), -1)
+    back_b = there_and_across((terms_b[:1], terms_b[1:]), 2)
+    total, token = add_early(token, index, [sums_a[0], sums_b[0]])
+    total, token = add_middle(
+        token, index, [total, swap_cores(sums_a[1]), *back_b, back_a, swap_cores(back_a[1:])]
+    )
     total = add_late(token, index, total, final)
     total = total.reshape(NSUB * SUB, GRID, PLANES, GRID).transpose(0, 2, 1, 3)
     return total.reshape(NSUB * SUB, PLANES, GRID * GRID)

time: 178 us -> 166 us (0.933)
  waiting for transfers between devices: 75 us -> 53.1 us
  starting transfers between devices: 74.9 us -> 86.5 us
  local copies, waits for them, and re-layouts: 4.72 us -> 2.51 us
    ppermute x34, waiting for transfers between devices: 75 us -> 53.1 us  [move(): return lax.ppermute(value, ('band', 'grid'), pairs)]
    ppermute x34, starting transfers between devices: 74.9 us -> 86.5 us  [move(): return lax.ppermute(value, ('band', 'grid'), pairs)]
    unnamed x23 -> x19, local copies, waits for them, and re-layouts: 4.61 us -> 2.39 us
  transfers between devices with their start and end apart: 34 -> 34, of which waited for: 19 -> 16; matrix products, arithmetic and copies ran while one was open for 0% -> 1% of each run, Pallas kernels for 9% -> 11%
where the time goes in v4:
time: 166 us
  starting transfers between devices  86.5 us (52%)
  waiting for transfers between devices  53.1 us (32%)
  Pallas kernels  23.2 us (14%)
  local copies, waits for them, and re-layouts  2.51 us (2%)
    ppermute x34, starting transfers between devices, move(): return lax.ppermute(value, ('band', 'grid'), pairs)  86.5 us
    ppermute x34, waiting for transfers between devices, move(): return lax.ppermute(value, ('band', 'grid'), pairs)  53.1 us
    pallas_call x20, Pallas kernels, launch(): pl.pallas_call(ordered, grid=grid, in_specs=[*in_specs, *[unread] * waits...  23.2 us
  transfers between devices with their start and end apart: 34, of which 16 were waited for; matrix products, arithmetic and copies ran while one was open for 1% of the time, Pallas kernels for 11%

profile of v4, /device:TPU:1, one launch (start us, length us, event | category | flops | bytes accessed | tf_op | source)
XLA Modules:
  0.0 165.7 jit_solution(10776625122124251522)
XLA Ops:
  0.0 3.2 %collective-permute-start = (f32[8,512,128]{2,1,0:T(8,128)}, f32[8,512,128]{2,1,0:T(8,128)S(1)}, u32[]{:S(2)}, u32[]{:S(2)}) collective-permute-start(f32[8,512,128]{2,1,0:T(8,128)} %bitcast.10), channel_id=1, source_target_pairs={{0,1},{1,0},{2,3},{3,2},{4,5},{5,4},{6,7},{7,6},{8,9},{9,8},{10,11... | collective-permute-start | bytes 6291464 | tf_op jit(solution)/shard_map/ppermute | solution.py:453
  3.2 0.8 copy.11.refs_0_
  4.0 3.2 %collective-permute-done.refs_2_ = f32[8,512,128]{2,1,0:T(8,128)S(1)} collective-permute-done((f32[8,512,128]{2,1,0:T(8,128)}, f32[8,512,128]{2,1,0:T(8,128)S(1)}, u32[]{:S(2)}, u32[]{:S(2)}) %collective-permute-start) | collective-permute-done | bytes 2097184 | tf_op jit(solution)/shard_map/ppermute | solution.py:453
  7.2 1.6 copy-done.1
  8.8 1.5 pick.1
  10.3 0.8 collective-permute-start.2
  11.1 6.9 %collective-permute-start.1 = (f32[2,2,512,128]{3,2,1,0:T(8,128)S(1)}, f32[2,2,512,128]{3,2,1,0:T(8,128)S(1)}, u32[]{:S(2)}, u32[]{:S(2)}) collective-permute-start(f32[2,2,512,128]{3,2,1,0:T(8,128)S(1)} %get-tuple-element.76), channel_id=1, source_target_pairs={{0,32},{1,33},{2,34},{3,35},{4,36},{5,37},{6,38},{7,39},{8,40},{9,... | collective-permute-start | bytes 3145736 | tf_op jit(solution)/shard_map/ppermute | solution.py:453
  18.1 0.9 pick_own.1
  18.9 15.8 %collective-permute-done.2.refs_1_.refs_6_ = f32[2,2,512,128]{3,2,1,0:T(8,128)S(1)} collective-permute-done((f32[2,2,512,128]{3,2,1,0:T(8,128)S(1)}, f32[2,2,512,128]{3,2,1,0:T(8,128)S(1)}, u32[]{:S(2)}, u32[]{:S(2)}) %collective-permute-start.2) | collective-permute-done | bytes 1048608 | tf_op jit(solution)/shard_map/ppermute | solution.py:453
  34.8 4.0 %forward.3 = (f32[8,8,128,128]{3,2,1,0:T(8,128)S(1)}, f32[520,128]{1,0:T(8,128)S(1)}, f32[520,128]{1,0:T(8,128)S(1)}, f32[520,128]{1,0:T(8,128)S(1)}, f32[520,128]{1,0:T(8,128)S(1)}, /*index=5*/f32[8,128]{1,0:T(8,128)S(1)}) custom-call(f32[2,2,4,512,128]{4,3,2,1,0:T(8,128)S(1)} %get-tuple-element.75.refs_0_.refs_5_, ...), custom_call_target="tpu_custom_call" | custom-call | tf_op jit(solution)/shard_map/forward/pallas_call | solution.py:96
  38.8 0.1 collective-permute-start.3
  38.8 2.4 %collective-permute-start.4 = (f32[520,128]{1,0:T(8,128)S(1)}, f32[520,128]{1,0:T(8,128)S(1)}, u32[]{:S(2)}, u32[]{:S(2)}) collective-permute-start(f32[520,128]{1,0:T(8,128)S(1)} %get-tuple-element.81), channel_id=1, source_target_pairs={{0,4},{1,5},{2,6},{3,7},{4,0},{5,1},{6,2},{7,3},{8,12},{9,13},{10,... | collective-permute-start | bytes 798728 | tf_op jit(solution)/shard_map/ppermute | solution.py:453
  41.3 1.1 collective-permute-start.5
  42.4 4.6 %collective-permute-done.3.refs_1_ = f32[520,128]{1,0:T(8,128)S(1)} collective-permute-done((f32[520,128]{1,0:T(8,128)S(1)}, f32[520,128]{1,0:T(8,128)S(1)}, u32[]{:S(2)}, u32[]{:S(2)}) %collective-permute-start.3) | collective-permute-done | bytes 266272 | tf_op jit(solution)/shard_map/ppermute | solution.py:453
  46.9 5.3 %collective-permute-done.4.refs_2_ = f32[520,128]{1,0:T(8,128)S(1)} collective-permute-done((f32[520,128]{1,0:T(8,128)S(1)}, f32[520,128]{1,0:T(8,128)S(1)}, u32[]{:S(2)}, u32[]{:S(2)}) %collective-permute-start.4) | collective-permute-done | bytes 266272 | tf_op jit(solution)/shard_map/ppermute | solution.py:453
  52.3 1.4 collective-permute-done.5.refs_3_
  53.6 0.1 run.3
  53.8 0.4 collective-permute-start.6
  54.1 2.0 %forward.4 = (f32[4,8,128,128]{3,2,1,0:T(8,128)S(1)}, f32[264,128]{1,0:T(8,128)S(1)}, f32[264,128]{1,0:T(8,128)S(1)}, f32[264,128]{1,0:T(8,128)S(1)}, f32[264,128]{1,0:T(8,128)S(1)}, /*index=5*/f32[8,128]{1,0:T(8,128)S(1)}) custom-call(f32[2,2,4,512,128]{4,3,2,1,0:T(8,128)S(1)} %get-tuple-element.75.refs_0_.refs_5_, ...), custom_call_target="tpu_custom_call" | custom-call | tf_op jit(solution)/shard_map/forward/pallas_call | solution.py:96
  56.1 1.8 %collective-permute-start.10 = (f32[264,128]{1,0:T(8,128)S(1)}, f32[264,128]{1,0:T(8,128)S(1)}, u32[]{:S(2)}, u32[]{:S(2)}) collective-permute-start(f32[264,128]{1,0:T(8,128)S(1)} %get-tuple-element.94), channel_id=1, source_target_pairs={{0,2},{1,3},{2,4},{3,5},{4,6},{5,7},{6,0},{7,1},{8,10},{9,11},{10,... | collective-permute-start | bytes 405512 | tf_op jit(solution)/shard_map/ppermute | solution.py:453
  58.0 2.8 %collective-permute-start.11 = (f32[264,128]{1,0:T(8,128)S(1)}, f32[264,128]{1,0:T(8,128)S(1)}, u32[]{:S(2)}, u32[]{:S(2)}) collective-permute-start(f32[264,128]{1,0:T(8,128)S(1)} %get-tuple-element.95), channel_id=1, source_target_pairs={{0,4},{1,5},{2,6},{3,7},{4,0},{5,1},{6,2},{7,3},{8,12},{9,13},{10,... | collective-permute-start | bytes 405512 | tf_op jit(solution)/shard_map/ppermute | solution.py:453
  60.8 8.9 %collective-permute-done.6.refs_1_.refs_4_ = f32[520,128]{1,0:T(8,128)S(1)} collective-permute-done((f32[520,128]{1,0:T(8,128)S(1)}, f32[520,128]{1,0:T(8,128)S(1)}, u32[]{:S(2)}, u32[]{:S(2)}) %collective-permute-start.6) | collective-permute-done | bytes 266272 | tf_op jit(solution)/shard_map/ppermute | solution.py:453
  69.7 3.2 %collective-permute-start.15 = (f32[520,128]{1,0:T(8,128)S(1)}, f32[520,128]{1,0:T(8,128)S(1)}, u32[]{:S(2)}, u32[]{:S(2)}) collective-permute-start(f32[520,128]{1,0:T(8,128)S(1)} %get-tuple-element.101.refs_5_), channel_id=1, source_target_pairs={{0,16},{1,17},{2,18},{3,19},{4,20},{5,21},{6,22},{7,23},{8,24},{9,... | collective-permute-start | bytes 798728 | tf_op jit(solution)/shard_map/ppermute | solution.py:453
  72.9 1.1 collective-permute-start.12
  74.0 2.0 %forward.5 = (f32[4,8,128,128]{3,2,1,0:T(8,128)S(1)}, f32[264,128]{1,0:T(8,128)S(1)}, f32[264,128]{1,0:T(8,128)S(1)}, f32[264,128]{1,0:T(8,128)S(1)}, f32[264,128]{1,0:T(8,128)S(1)}, /*index=5*/f32[8,128]{1,0:T(8,128)S(1)}) custom-call(f32[2,2,4,512,128]{4,3,2,1,0:T(8,128)S(1)} %get-tuple-element.75.refs_0_.refs_5_, ...), custom_call_target="tpu_custom_call" | custom-call | tf_op jit(solution)/shard_map/forward/pallas_call | solution.py:96
  75.9 0.5 collective-permute-start.7
  76.4 1.2 collective-permute-start.8
  77.6 1.3 collective-permute-start.9
  79.0 1.7 %collective-permute-start.14 = (f32[264,128]{1,0:T(8,128)S(1)}, f32[264,128]{1,0:T(8,128)S(1)}, u32[]{:S(2)}, u32[]{:S(2)}) collective-permute-start(f32[264,128]{1,0:T(8,128)S(1)} %get-tuple-element.100.refs_0_), channel_id=1, source_target_pairs={{0,8},{1,9},{2,10},{3,11},{4,12},{5,13},{6,14},{7,15},{8,0},{9,1},... | collective-permute-start | bytes 405512 | tf_op jit(solution)/shard_map/ppermute | solution.py:453
  80.7 1.3 collective-permute-done.7.refs_1_
  82.0 1.4 collective-permute-done.8.refs_2_
  83.4 0.5 collective-permute-done.9.refs_3_
  83.9 0.3 collective-permute-done.15.refs_6_
  84.2 0.3 edges.3
  84.5 3.5 %collective-permute-start.17 = (f32[520,128]{1,0:T(8,128)S(1)}, f32[520,128]{1,0:T(8,128)S(1)}, u32[]{:S(2)}, u32[]{:S(2)}) collective-permute-start(f32[520,128]{1,0:T(8,128)S(1)} %get-tuple-element.108), channel_id=1, source_target_pairs={{0,6},{1,7},{2,0},{3,1},{4,2},{5,3},{6,4},{7,5},{8,14},{9,15},{10,... | collective-permute-start | bytes 798728 | tf_op jit(solution)/shard_map/ppermute | solution.py:453
  88.1 2.9 %collective-permute-start.20 = (f32[264,128]{1,0:T(8,128)S(1)}, f32[264,128]{1,0:T(8,128)S(1)}, u32[]{:S(2)}, u32[]{:S(2)}) collective-permute-start(f32[264,128]{1,0:T(8,128)S(1)} %get-tuple-element.111.refs_5_), channel_id=1, source_target_pairs={{0,16},{1,17},{2,18},{3,19},{4,20},{5,21},{6,22},{7,23},{8,24},{9,... | collective-permute-start | bytes 405512 | tf_op jit(solution)/shard_map/ppermute | solution.py:453
  90.9 0.4 collective-permute-start.19
  91.3 0.8 collective-permute-done.13.refs_1_.refs_4_
  92.2 1.5 collective-permute-start.16
  93.6 1.4 collective-permute-done.20.refs_6_
  95.1 0.2 edges.4
  95.2 2.0 %collective-permute-start.24 = (f32[264,128]{1,0:T(8,128)S(1)}, f32[264,128]{1,0:T(8,128)S(1)}, u32[]{:S(2)}, u32[]{:S(2)}) collective-permute-start(f32[264,128]{1,0:T(8,128)S(1)} %get-tuple-element.121), channel_id=1, source_target_pairs={{0,6},{1,7},{2,0},{3,1},{4,2},{5,3},{6,4},{7,5},{8,14},{9,15},{10,... | collective-permute-start | bytes 405512 | tf_op jit(solution)/shard_map/ppermute | solution.py:453
  97.2 1.3 collective-permute-done.17.refs_2_
  98.6 4.1 %collective-permute-start.26 = (f32[264,128]{1,0:T(8,128)S(1)}, f32[264,128]{1,0:T(8,128)S(1)}, u32[]{:S(2)}, u32[]{:S(2)}) collective-permute-start(f32[264,128]{1,0:T(8,128)S(1)} %get-tuple-element.123), channel_id=1, source_target_pairs={{0,2},{1,3},{2,4},{3,5},{4,6},{5,7},{6,0},{7,1},{8,10},{9,11},{10,... | collective-permute-start | bytes 405512 | tf_op jit(solution)/shard_map/ppermute | solution.py:453
  102.7 4.1 %backward.3 = (f32[2,2,512,128]{3,2,1,0:T(8,128)S(1)}, f32[4,512,128]{2,1,0:T(8,128)S(1)}, f32[4,512,128]{2,1,0:T(8,128)S(1)}, f32[8,128]{1,0:T(8,128)S(1)}) custom-call(f32[8,8,128,128]{3,2,1,0:T(8,128)S(1)} %get-tuple-element.106.refs_0_, f32[520,128]{1,0:T(8,128)S(1)} %get-tuple-element.107.refs_1_, f32[520,128]{1,0:T(8,128)S(1)} %collective-permute-done.17.refs_2_, ...), custom_call_target="tpu_custom_call" | custom-call | tf_op jit(solution)/shard_map/backward/pallas_call | solution.py:96
  106.8 0.2 edges.5
  107.0 2.0 %backward.4 = (f32[2,1,512,128]{3,2,1,0:T(8,128)S(1)}, f32[4,512,128]{2,1,0:T(8,128)S(1)}, f32[4,512,128]{2,1,0:T(8,128)S(1)}, f32[8,128]{1,0:T(8,128)S(1)}) custom-call(f32[4,8,128,128]{3,2,1,0:T(8,128)S(1)} %get-tuple-element.119.refs_0_, f32[264,128]{1,0:T(8,128)S(1)} %get-tuple-element.120.refs_1_, f32[264,128]{1,0:T(8,128)S(1)} %collective-permute-done.24.refs_2_, ...), custom_call_target="tpu_custom_call" | custom-call | tf_op jit(solution)/shard_map/backward/pallas_call | solution.py:96
  109.0 6.3 %collective-permute-start.30 = (f32[2,1,512,128]{3,2,1,0:T(8,128)S(1)}, f32[2,1,512,128]{3,2,1,0:T(8,128)S(1)}, u32[]{:S(2)}, u32[]{:S(2)}) collective-permute-start(f32[2,1,512,128]{3,2,1,0:T(8,128)S(1)} %get-tuple-element.135), channel_id=1, source_target_pairs={{0,224},{1,225},{2,226},{3,227},{4,228},{5,229},{6,230},{7,231},{8... | collective-permute-start | bytes 1572872 | tf_op jit(solution)/shard_map/ppermute | solution.py:453
  115.5 0.1 collective-permute-start.28
  115.6 0.1 collective-permute-start.21
  115.6 0.1 collective-permute-start.22
  115.7 1.4 collective-permute-start.23
  117.1 2.4 %collective-permute-done.21.refs_2_ = f32[264,128]{1,0:T(8,128)S(1)} collective-permute-done((f32[264,128]{1,0:T(8,128)S(1)}, f32[264,128]{1,0:T(8,128)S(1)}, u32[]{:S(2)}, u32[]{:S(2)}) %collective-permute-start.21) | collective-permute-done | bytes 135200 | tf_op jit(solution)/shard_map/ppermute | solution.py:453
  119.5 6.0 %collective-permute-start.29 = (f32[1,2,512,128]{3,2,1,0:T(8,128)S(1)}, f32[1,2,512,128]{3,2,1,0:T(8,128)S(1)}, u32[]{:S(2)}, u32[]{:S(2)}) collective-permute-start(f32[1,2,512,128]{3,2,1,0:T(8,128)S(1)} %get-tuple-element.141), channel_id=1, source_target_pairs={{0,65},{1,64},{2,67},{3,66},{4,69},{5,68},{6,71},{7,70},{8,73},{9,... | collective-permute-start | bytes 1572872 | tf_op jit(solution)/shard_map/ppermute | solution.py:453
  125.5 2.1 %backward.5 = (f32[2,1,512,128]{3,2,1,0:T(8,128)S(1)}, f32[4,512,128]{2,1,0:T(8,128)S(1)}, f32[8,512,128]{2,1,0:T(8,128)S(1)}, f32[8,128]{1,0:T(8,128)S(1)}) custom-call(f32[4,8,128,128]{3,2,1,0:T(8,128)S(1)} %get-tuple-element.88.refs_0_, f32[264,128]{1,0:T(8,128)S(1)} %get-tuple-element.115.refs_1_, f32[264,128]{1,0:T(8,128)S(1)} %collective-permute-done.21.refs_2_, ...), custom_call_target="tpu_custom_call" | custom-call | tf_op jit(solution)/shard_map/backward/pallas_call | solution.py:96
  127.6 3.9 %collective-permute-start.27 = (f32[8,512,128]{2,1,0:T(8,128)S(1)}, f32[8,512,128]{2,1,0:T(8,128)S(1)}, u32[]{:S(2)}, u32[]{:S(2)}) collective-permute-start(f32[8,512,128]{2,1,0:T(8,128)S(1)} %get-tuple-element.133), channel_id=1, source_target_pairs={{0,1},{1,0},{2,3},{3,2},{4,5},{5,4},{6,7},{7,6},{8,9},{9,8},{10,11... | collective-permute-start | bytes 6291464 | tf_op jit(solution)/shard_map/ppermute | solution.py:453
  131.5 3.6 %collective-permute-start.32 = (f32[1,1,512,128]{3,2,1,0:T(8,128)S(1)}, f32[1,1,512,128]{3,2,1,0:T(8,128)S(1)}, u32[]{:S(2)}, u32[]{:S(2)}) collective-permute-start(f32[1,1,512,128]{3,2,1,0:T(8,128)S(1)} %get-tuple-element.144), channel_id=1, source_target_pairs={{0,224},{1,225},{2,226},{3,227},{4,228},{5,229},{6,230},{7,231},{8... | collective-permute-start | bytes 786440 | tf_op jit(solution)/shard_map/ppermute | solution.py:453
  135.1 22.0 %collective-permute-start.33 = (f32[1,1,512,128]{3,2,1,0:T(8,128)S(1)}, f32[1,1,512,128]{3,2,1,0:T(8,128)S(1)}, u32[]{:S(2)}, u32[]{:S(2)}) collective-permute-start(f32[1,1,512,128]{3,2,1,0:T(8,128)S(1)} %get-tuple-element.143), channel_id=1, source_target_pairs={{0,225},{1,224},{2,227},{3,226},{4,229},{5,228},{6,231},{7,230},{8... | collective-permute-start | bytes 786440 | tf_op jit(solution)/shard_map/ppermute | solution.py:453
  157.2 0.1 collective-permute-start.31
  157.3 0.8 add_early.1
  158.1 0.7 collective-permute-done.31.refs_6_
  158.8 1.1 add_middle.1
  159.9 3.7 %collective-permute-done.33.refs_3_ = f32[1,1,512,128]{3,2,1,0:T(8,128)S(1)} collective-permute-done((f32[1,1,512,128]{3,2,1,0:T(8,128)S(1)}, f32[1,1,512,128]{3,2,1,0:T(8,128)S(1)}, u32[]{:S(2)}, u32[]{:S(2)}) %collective-permute-start.33) | collective-permute-done | bytes 262176 | tf_op jit(solution)/shard_map/ppermute | solution.py:453
  163.6 1.9 %add_late.1 = (f32[8,512,128]{2,1,0:T(8,128)}, f32[8,128]{1,0:T(8,128)}) custom-call(s32[4]{0:T(128)S(1)} %get-tuple-element.73.refs_0_, f32[8,512,128]{2,1,0:T(8,128)S(1)} %get-tuple-element.137.refs_1_, f32[1,1,512,128]{3,2,1,0:T(8,128)S(1)} %collective-permute-done.32.refs_2_, f32[1,1,512,128]{3,2,1,0:T(8,128)S(1)} %collective-permute-done.33.refs_3_, ...), custom_call_target="tpu_custom_call" | custom-call | tf_op jit(solution)/shard_map/add_late/pallas_call | solution.py:96
  (46 shorter events, 0.5 us)
Async XLA Ops:
  0.0 7.2 %collective-permute-start = (f32[8,512,128]{2,1,0:T(8,128)}, f32[8,512,128]{2,1,0:T(8,128)S(1)}, u32[]{:S(2)}, u32[]{:S(2)}) collective-permute-start(f32[8,512,128]{2,1,0:T(8,128)} %bitcast.10), channel_id=1, source_target_pairs={{0,1},{1,0},{2,3},{3,2},{4,5},{5,4},{6,7},{7,6},{8,9},{9,8},{10,11... | collective-permute-start | bytes 6291464 | tf_op jit(solution)/shard_map/ppermute | solution.py:453
  7.2 1.6 copy-start.1
  8.8 9.2 %copy-start.2 = (f32[8,4,16384]{2,1,0:T(4,128)S(1)}, f32[8,4,16384]{2,1,0:T(4,128)}, u32[]{:S(2)}) copy-start(f32[8,4,16384]{2,1,0:T(4,128)} %param.9) | copy-start | bytes 6291460
  10.3 24.5 %collective-permute-start.2 = (f32[2,2,512,128]{3,2,1,0:T(8,128)S(1)}, f32[2,2,512,128]{3,2,1,0:T(8,128)S(1)}, u32[]{:S(2)}, u32[]{:S(2)}) collective-permute-start(f32[2,2,512,128]{3,2,1,0:T(8,128)S(1)} %get-tuple-element.77), channel_id=1, source_target_pairs={{0,192},{1,193},{2,194},{3,195},{4,196},{5,197},{6,198},{7,199},{8... | collective-permute-start | bytes 3145736 | tf_op jit(solution)/shard_map/ppermute | solution.py:453
  11.1 43.0 %collective-permute-start.1 = (f32[2,2,512,128]{3,2,1,0:T(8,128)S(1)}, f32[2,2,512,128]{3,2,1,0:T(8,128)S(1)}, u32[]{:S(2)}, u32[]{:S(2)}) collective-permute-start(f32[2,2,512,128]{3,2,1,0:T(8,128)S(1)} %get-tuple-element.76), channel_id=1, source_target_pairs={{0,32},{1,33},{2,34},{3,35},{4,36},{5,37},{6,38},{7,39},{8,40},{9,... | collective-permute-start | bytes 3145736 | tf_op jit(solution)/shard_map/ppermute | solution.py:453
  18.0 16.7 %copy-start.4 = (bf16[256,256]{1,0:T(8,128)(2,1)S(1)}, bf16[256,256]{1,0:T(8,128)(2,1)}, u32[]{:S(2)}) copy-start(bf16[256,256]{1,0:T(8,128)(2,1)} %constant.14.clone.refs_2_.refs_7_) | copy-start | bytes 393220
  18.0 16.7 %copy-start.5 = (bf16[256,256]{1,0:T(8,128)(2,1)S(1)}, bf16[256,256]{1,0:T(8,128)(2,1)}, u32[]{:S(2)}) copy-start(bf16[256,256]{1,0:T(8,128)(2,1)} %constant.15.clone.refs_3_.refs_8_) | copy-start | bytes 393220
  18.0 16.7 %copy-start.6 = (f32[128,128]{1,0:T(8,128)S(1)}, f32[128,128]{1,0:T(8,128)}, u32[]{:S(2)}) copy-start(f32[128,128]{1,0:T(8,128)} %constant.16.clone.refs_4_.refs_9_) | copy-start | bytes 196612
  18.1 16.7 %copy-start.7 = (f32[128,128]{1,0:T(8,128)S(1)}, f32[128,128]{1,0:T(8,128)}, u32[]{:S(2)}) copy-start(f32[128,128]{1,0:T(8,128)} %constant.17.clone.refs_5_) | copy-start | bytes 196612
  34.8 18.8 %copy-start = (f32[4,128,128]{2,1,0:T(8,128)S(1)}, f32[4,128,128]{2,1,0:T(8,128)}, u32[]{:S(2)}) copy-start(f32[4,128,128]{2,1,0:T(8,128)} %constant.18.clone.refs_4_.refs_7_) | copy-start | bytes 786436
  38.8 8.2 %collective-permute-start.3 = (f32[520,128]{1,0:T(8,128)S(1)}, f32[520,128]{1,0:T(8,128)S(1)}, u32[]{:S(2)}, u32[]{:S(2)}) collective-permute-start(f32[520,128]{1,0:T(8,128)S(1)} %get-tuple-element.80), channel_id=1, source_target_pairs={{0,2},{1,3},{2,4},{3,5},{4,6},{5,7},{6,0},{7,1},{8,10},{9,11},{10,... | collective-permute-start | bytes 798728 | tf_op jit(solution)/shard_map/ppermute | solution.py:453
  38.8 13.4 %collective-permute-start.4 = (f32[520,128]{1,0:T(8,128)S(1)}, f32[520,128]{1,0:T(8,128)S(1)}, u32[]{:S(2)}, u32[]{:S(2)}) collective-permute-start(f32[520,128]{1,0:T(8,128)S(1)} %get-tuple-element.81), channel_id=1, source_target_pairs={{0,4},{1,5},{2,6},{3,7},{4,0},{5,1},{6,2},{7,3},{8,12},{9,13},{10,... | collective-permute-start | bytes 798728 | tf_op jit(solution)/shard_map/ppermute | solution.py:453
  41.3 12.3 %collective-permute-start.5 = (f32[520,128]{1,0:T(8,128)S(1)}, f32[520,128]{1,0:T(8,128)S(1)}, u32[]{:S(2)}, u32[]{:S(2)}) collective-permute-start(f32[520,128]{1,0:T(8,128)S(1)} %get-tuple-element.82), channel_id=1, source_target_pairs={{0,6},{1,7},{2,0},{3,1},{4,2},{5,3},{6,4},{7,5},{8,14},{9,15},{10,... | collective-permute-start | bytes 798728 | tf_op jit(solution)/shard_map/ppermute | solution.py:453
  53.8 15.9 %collective-permute-start.6 = (f32[520,128]{1,0:T(8,128)S(1)}, f32[520,128]{1,0:T(8,128)S(1)}, u32[]{:S(2)}, u32[]{:S(2)}) collective-permute-start(f32[520,128]{1,0:T(8,128)S(1)} %get-tuple-element.84.refs_0_), channel_id=1, source_target_pairs={{0,8},{1,9},{2,10},{3,11},{4,12},{5,13},{6,14},{7,15},{8,0},{9,1},... | collective-permute-start | bytes 798728 | tf_op jit(solution)/shard_map/ppermute | solution.py:453
  54.1 15.5 %copy-start.3 = (f32[3,128,128]{2,1,0:T(8,128)S(1)}, f32[3,128,128]{2,1,0:T(8,128)}, u32[]{:S(2)}) copy-start(f32[3,128,128]{2,1,0:T(8,128)} %constant.19.clone.refs_2_.refs_8_) | copy-start | bytes 589828
  56.1 20.3 %collective-permute-start.10 = (f32[264,128]{1,0:T(8,128)S(1)}, f32[264,128]{1,0:T(8,128)S(1)}, u32[]{:S(2)}, u32[]{:S(2)}) collective-permute-start(f32[264,128]{1,0:T(8,128)S(1)} %get-tuple-element.94), channel_id=1, source_target_pairs={{0,2},{1,3},{2,4},{3,5},{4,6},{5,7},{6,0},{7,1},{8,10},{9,11},{10,... | collective-permute-start | bytes 405512 | tf_op jit(solution)/shard_map/ppermute | solution.py:453
  58.0 19.7 %collective-permute-start.11 = (f32[264,128]{1,0:T(8,128)S(1)}, f32[264,128]{1,0:T(8,128)S(1)}, u32[]{:S(2)}, u32[]{:S(2)}) collective-permute-start(f32[264,128]{1,0:T(8,128)S(1)} %get-tuple-element.95), channel_id=1, source_target_pairs={{0,4},{1,5},{2,6},{3,7},{4,0},{5,1},{6,2},{7,3},{8,12},{9,13},{10,... | collective-permute-start | bytes 405512 | tf_op jit(solution)/shard_map/ppermute | solution.py:453
  69.7 14.5 %collective-permute-start.15 = (f32[520,128]{1,0:T(8,128)S(1)}, f32[520,128]{1,0:T(8,128)S(1)}, u32[]{:S(2)}, u32[]{:S(2)}) collective-permute-start(f32[520,128]{1,0:T(8,128)S(1)} %get-tuple-element.101.refs_5_), channel_id=1, source_target_pairs={{0,16},{1,17},{2,18},{3,19},{4,20},{5,21},{6,22},{7,23},{8,24},{9,... | collective-permute-start | bytes 798728 | tf_op jit(solution)/shard_map/ppermute | solution.py:453
  72.9 6.0 %collective-permute-start.12 = (f32[264,128]{1,0:T(8,128)S(1)}, f32[264,128]{1,0:T(8,128)S(1)}, u32[]{:S(2)}, u32[]{:S(2)}) collective-permute-start(f32[264,128]{1,0:T(8,128)S(1)} %get-tuple-element.96), channel_id=1, source_target_pairs={{0,6},{1,7},{2,0},{3,1},{4,2},{5,3},{6,4},{7,5},{8,14},{9,15},{10,... | collective-permute-start | bytes 405512 | tf_op jit(solution)/shard_map/ppermute | solution.py:453
  75.9 6.0 %collective-permute-start.7 = (f32[264,128]{1,0:T(8,128)S(1)}, f32[264,128]{1,0:T(8,128)S(1)}, u32[]{:S(2)}, u32[]{:S(2)}) collective-permute-start(f32[264,128]{1,0:T(8,128)S(1)} %get-tuple-element.90), channel_id=1, source_target_pairs={{0,2},{1,3},{2,4},{3,5},{4,6},{5,7},{6,0},{7,1},{8,10},{9,11},{10,... | collective-permute-start | bytes 405512 | tf_op jit(solution)/shard_map/ppermute | solution.py:453
  76.4 7.0 %collective-permute-start.8 = (f32[264,128]{1,0:T(8,128)S(1)}, f32[264,128]{1,0:T(8,128)S(1)}, u32[]{:S(2)}, u32[]{:S(2)}) collective-permute-start(f32[264,128]{1,0:T(8,128)S(1)} %get-tuple-element.91), channel_id=1, source_target_pairs={{0,4},{1,5},{2,6},{3,7},{4,0},{5,1},{6,2},{7,3},{8,12},{9,13},{10,... | collective-permute-start | bytes 405512 | tf_op jit(solution)/shard_map/ppermute | solution.py:453
  77.6 6.2 %collective-permute-start.9 = (f32[264,128]{1,0:T(8,128)S(1)}, f32[264,128]{1,0:T(8,128)S(1)}, u32[]{:S(2)}, u32[]{:S(2)}) collective-permute-start(f32[264,128]{1,0:T(8,128)S(1)} %get-tuple-element.92), channel_id=1, source_target_pairs={{0,6},{1,7},{2,0},{3,1},{4,2},{5,3},{6,4},{7,5},{8,14},{9,15},{10,... | collective-permute-start | bytes 405512 | tf_op jit(solution)/shard_map/ppermute | solution.py:453
  79.0 9.0 %collective-permute-start.14 = (f32[264,128]{1,0:T(8,128)S(1)}, f32[264,128]{1,0:T(8,128)S(1)}, u32[]{:S(2)}, u32[]{:S(2)}) collective-permute-start(f32[264,128]{1,0:T(8,128)S(1)} %get-tuple-element.100.refs_0_), channel_id=1, source_target_pairs={{0,8},{1,9},{2,10},{3,11},{4,12},{5,13},{6,14},{7,15},{8,0},{9,1},... | collective-permute-start | bytes 405512 | tf_op jit(solution)/shard_map/ppermute | solution.py:453
  84.2 18.5 %copy-start.8 = (f32[1,128]{1,0:T(1,128)S(1)}, f32[1,128]{1,0:T(1,128)}, u32[]{:S(2)}) copy-start(f32[1,128]{1,0:T(1,128)} %constant.20.clone.refs_10_) | copy-start | bytes 1540
  84.5 14.1 %collective-permute-start.17 = (f32[520,128]{1,0:T(8,128)S(1)}, f32[520,128]{1,0:T(8,128)S(1)}, u32[]{:S(2)}, u32[]{:S(2)}) collective-permute-start(f32[520,128]{1,0:T(8,128)S(1)} %get-tuple-element.108), channel_id=1, source_target_pairs={{0,6},{1,7},{2,0},{3,1},{4,2},{5,3},{6,4},{7,5},{8,14},{9,15},{10,... | collective-permute-start | bytes 798728 | tf_op jit(solution)/shard_map/ppermute | solution.py:453
  88.0 10.6 %collective-permute-start.18 = (f32[520,128]{1,0:T(8,128)S(1)}, f32[520,128]{1,0:T(8,128)S(1)}, u32[]{:S(2)}, u32[]{:S(2)}) collective-permute-start(f32[520,128]{1,0:T(8,128)S(1)} %get-tuple-element.109), channel_id=1, source_target_pairs={{0,4},{1,5},{2,6},{3,7},{4,0},{5,1},{6,2},{7,3},{8,12},{9,13},{10,... | collective-permute-start | bytes 798728 | tf_op jit(solution)/shard_map/ppermute | solution.py:453
  88.0 4.2 %collective-permute-start.13 = (f32[264,128]{1,0:T(8,128)S(1)}, f32[264,128]{1,0:T(8,128)S(1)}, u32[]{:S(2)}, u32[]{:S(2)}) collective-permute-start(f32[264,128]{1,0:T(8,128)S(1)} %get-tuple-element.99.refs_0_), channel_id=1, source_target_pairs={{0,8},{1,9},{2,10},{3,11},{4,12},{5,13},{6,14},{7,15},{8,0},{9,1},... | collective-permute-start | bytes 405512 | tf_op jit(solution)/shard_map/ppermute | solution.py:453
  88.1 7.0 %collective-permute-start.20 = (f32[264,128]{1,0:T(8,128)S(1)}, f32[264,128]{1,0:T(8,128)S(1)}, u32[]{:S(2)}, u32[]{:S(2)}) collective-permute-start(f32[264,128]{1,0:T(8,128)S(1)} %get-tuple-element.111.refs_5_), channel_id=1, source_target_pairs={{0,16},{1,17},{2,18},{3,19},{4,20},{5,21},{6,22},{7,23},{8,24},{9,... | collective-permute-start | bytes 405512 | tf_op jit(solution)/shard_map/ppermute | solution.py:453
  90.9 11.8 %collective-permute-start.19 = (f32[520,128]{1,0:T(8,128)S(1)}, f32[520,128]{1,0:T(8,128)S(1)}, u32[]{:S(2)}, u32[]{:S(2)}) collective-permute-start(f32[520,128]{1,0:T(8,128)S(1)} %get-tuple-element.110), channel_id=1, source_target_pairs={{0,2},{1,3},{2,4},{3,5},{4,6},{5,7},{6,0},{7,1},{8,10},{9,11},{10,... | collective-permute-start | bytes 798728 | tf_op jit(solution)/shard_map/ppermute | solution.py:453
  92.2 14.6 %collective-permute-start.16 = (f32[264,128]{1,0:T(8,128)S(1)}, f32[264,128]{1,0:T(8,128)S(1)}, u32[]{:S(2)}, u32[]{:S(2)}) collective-permute-start(f32[264,128]{1,0:T(8,128)S(1)} %get-tuple-element.105.refs_5_), channel_id=1, source_target_pairs={{0,16},{1,17},{2,18},{3,19},{4,20},{5,21},{6,22},{7,23},{8,24},{9,... | collective-permute-start | bytes 405512 | tf_op jit(solution)/shard_map/ppermute | solution.py:453
  95.2 11.8 %collective-permute-start.24 = (f32[264,128]{1,0:T(8,128)S(1)}, f32[264,128]{1,0:T(8,128)S(1)}, u32[]{:S(2)}, u32[]{:S(2)}) collective-permute-start(f32[264,128]{1,0:T(8,128)S(1)} %get-tuple-element.121), channel_id=1, source_target_pairs={{0,6},{1,7},{2,0},{3,1},{4,2},{5,3},{6,4},{7,5},{8,14},{9,15},{10,... | collective-permute-start | bytes 405512 | tf_op jit(solution)/shard_map/ppermute | solution.py:453
  98.6 8.4 %collective-permute-start.25 = (f32[264,128]{1,0:T(8,128)S(1)}, f32[264,128]{1,0:T(8,128)S(1)}, u32[]{:S(2)}, u32[]{:S(2)}) collective-permute-start(f32[264,128]{1,0:T(8,128)S(1)} %get-tuple-element.122), channel_id=1, source_target_pairs={{0,4},{1,5},{2,6},{3,7},{4,0},{5,1},{6,2},{7,3},{8,12},{9,13},{10,... | collective-permute-start | bytes 405512 | tf_op jit(solution)/shard_map/ppermute | solution.py:453
  98.6 8.4 %collective-permute-start.26 = (f32[264,128]{1,0:T(8,128)S(1)}, f32[264,128]{1,0:T(8,128)S(1)}, u32[]{:S(2)}, u32[]{:S(2)}) collective-permute-start(f32[264,128]{1,0:T(8,128)S(1)} %get-tuple-element.123), channel_id=1, source_target_pairs={{0,2},{1,3},{2,4},{3,5},{4,6},{5,7},{6,0},{7,1},{8,10},{9,11},{10,... | collective-permute-start | bytes 405512 | tf_op jit(solution)/shard_map/ppermute | solution.py:453
  109.0 26.1 %collective-permute-start.30 = (f32[2,1,512,128]{3,2,1,0:T(8,128)S(1)}, f32[2,1,512,128]{3,2,1,0:T(8,128)S(1)}, u32[]{:S(2)}, u32[]{:S(2)}) collective-permute-start(f32[2,1,512,128]{3,2,1,0:T(8,128)S(1)} %get-tuple-element.135), channel_id=1, source_target_pairs={{0,224},{1,225},{2,226},{3,227},{4,228},{5,229},{6,230},{7,231},{8... | collective-permute-start | bytes 1572872 | tf_op jit(solution)/shard_map/ppermute | solution.py:453
  115.5 41.7 %collective-permute-start.28 = (f32[1,2,512,128]{3,2,1,0:T(8,128)S(1)}, f32[1,2,512,128]{3,2,1,0:T(8,128)S(1)}, u32[]{:S(2)}, u32[]{:S(2)}) collective-permute-start(f32[1,2,512,128]{3,2,1,0:T(8,128)S(1)} %get-tuple-element.142), channel_id=1, source_target_pairs={{0,64},{1,65},{2,66},{3,67},{4,68},{5,69},{6,70},{7,71},{8,72},{9,... | collective-permute-start | bytes 1572872 | tf_op jit(solution)/shard_map/ppermute | solution.py:453
  115.6 3.9 %collective-permute-start.21 = (f32[264,128]{1,0:T(8,128)S(1)}, f32[264,128]{1,0:T(8,128)S(1)}, u32[]{:S(2)}, u32[]{:S(2)}) collective-permute-start(f32[264,128]{1,0:T(8,128)S(1)} %get-tuple-element.116), channel_id=1, source_target_pairs={{0,6},{1,7},{2,0},{3,1},{4,2},{5,3},{6,4},{7,5},{8,14},{9,15},{10,... | collective-permute-start | bytes 405512 | tf_op jit(solution)/shard_map/ppermute | solution.py:453
  115.6 9.9 %collective-permute-start.22 = (f32[264,128]{1,0:T(8,128)S(1)}, f32[264,128]{1,0:T(8,128)S(1)}, u32[]{:S(2)}, u32[]{:S(2)}) collective-permute-start(f32[264,128]{1,0:T(8,128)S(1)} %get-tuple-element.117), channel_id=1, source_target_pairs={{0,4},{1,5},{2,6},{3,7},{4,0},{5,1},{6,2},{7,3},{8,12},{9,13},{10,... | collective-permute-start | bytes 405512 | tf_op jit(solution)/shard_map/ppermute | solution.py:453
  115.7 9.8 %collective-permute-start.23 = (f32[264,128]{1,0:T(8,128)S(1)}, f32[264,128]{1,0:T(8,128)S(1)}, u32[]{:S(2)}, u32[]{:S(2)}) collective-permute-start(f32[264,128]{1,0:T(8,128)S(1)} %get-tuple-element.118), channel_id=1, source_target_pairs={{0,2},{1,3},{2,4},{3,5},{4,6},{5,7},{6,0},{7,1},{8,10},{9,11},{10,... | collective-permute-start | bytes 405512 | tf_op jit(solution)/shard_map/ppermute | solution.py:453
  119.5 38.6 %collective-permute-start.29 = (f32[1,2,512,128]{3,2,1,0:T(8,128)S(1)}, f32[1,2,512,128]{3,2,1,0:T(8,128)S(1)}, u32[]{:S(2)}, u32[]{:S(2)}) collective-permute-start(f32[1,2,512,128]{3,2,1,0:T(8,128)S(1)} %get-tuple-element.141), channel_id=1, source_target_pairs={{0,65},{1,64},{2,67},{3,66},{4,69},{5,68},{6,71},{7,70},{8,73},{9,... | collective-permute-start | bytes 1572872 | tf_op jit(solution)/shard_map/ppermute | solution.py:453
  127.6 31.2 %collective-permute-start.27 = (f32[8,512,128]{2,1,0:T(8,128)S(1)}, f32[8,512,128]{2,1,0:T(8,128)S(1)}, u32[]{:S(2)}, u32[]{:S(2)}) collective-permute-start(f32[8,512,128]{2,1,0:T(8,128)S(1)} %get-tuple-element.133), channel_id=1, source_target_pairs={{0,1},{1,0},{2,3},{3,2},{4,5},{5,4},{6,7},{7,6},{8,9},{9,8},{10,11... | collective-permute-start | bytes 6291464 | tf_op jit(solution)/shard_map/ppermute | solution.py:453
  131.5 28.4 %collective-permute-start.32 = (f32[1,1,512,128]{3,2,1,0:T(8,128)S(1)}, f32[1,1,512,128]{3,2,1,0:T(8,128)S(1)}, u32[]{:S(2)}, u32[]{:S(2)}) collective-permute-start(f32[1,1,512,128]{3,2,1,0:T(8,128)S(1)} %get-tuple-element.144), channel_id=1, source_target_pairs={{0,224},{1,225},{2,226},{3,227},{4,228},{5,229},{6,230},{7,231},{8... | collective-permute-start | bytes 786440 | tf_op jit(solution)/shard_map/ppermute | solution.py:453
  135.1 28.5 %collective-permute-start.33 = (f32[1,1,512,128]{3,2,1,0:T(8,128)S(1)}, f32[1,1,512,128]{3,2,1,0:T(8,128)S(1)}, u32[]{:S(2)}, u32[]{:S(2)}) collective-permute-start(f32[1,1,512,128]{3,2,1,0:T(8,128)S(1)} %get-tuple-element.143), channel_id=1, source_target_pairs={{0,225},{1,224},{2,227},{3,226},{4,229},{5,228},{6,231},{7,230},{8... | collective-permute-start | bytes 786440 | tf_op jit(solution)/shard_map/ppermute | solution.py:453
  157.2 1.6 collective-permute-start.31

commit v5 on v4

--- a/solution.py
+++ b/solution.py
@@ -342,7 +342,7 @@
         own_out_b[SUB : 2 * SUB] = before[prior][...]
 
 
-def backward(token, step, members, spec, edges, own, part, prior=(), extra=()):
+def backward(token, step, members, spec, edges, own, part, prior=(), extra=(), after=()):
     right, left, decay, _, mean = tables()[:5]
     args = [spec, *edges, own, part, right, left, decay, mean, *prior, *extra]
     outs, token = launch(
@@ -361,6 +361,7 @@
             pltpu.VMEM((SUB, 2 * PLANES, GRID, GRID), F32),
             pltpu.VMEM((SUB * CORES, ROWS, GRID), F32),
         ],
+        after=after,
     )
     return outs[0], outs[1:], token
 
@@ -503,12 +504,12 @@
         )
         chain["edges"] = along_y(outs, -1)
 
-    def finish(at, prior=(), extra=()):
+    def finish(at, prior=(), extra=(), after=()):
         nonlocal token
         step, members = CHAINS[at]
         chain = chains[at]
         terms, sums, token = backward(
-            token, step, members, chain["spec"], chain["edges"], own, parts[step], prior, extra
+            token, step, members, chain["spec"], chain["edges"], own, parts[step], prior, extra, after
         )
         return terms, sums
 
@@ -516,18 +517,18 @@
     start(second)
     run(second)
     start(first)
+    start(last)
+    run(first, [chains[second]["near"]])
+    two(first)
     two(second)
-    start(last)
-    run(first)
     run(last)
+    edges(first)
+    two(last)
+    terms_a, sums_a = finish(first, after=[chains[last]["far"]])
+    back_a = shift(terms_a, -1)
+    edges(last)
     edges(second)
-    two(first)
-    two(last)
-    edges(first)
     terms_b, sums_b = finish(second)
-    edges(last)
-    terms_a, sums_a = finish(first)
-    back_a = shift(terms_a, -1)
     terms_a, sums_a = finish(last, sums_a, sums_b[1:])
     final = there_and_across((terms_a[:1], terms_a[1:]), -1)
     back_b = there_and_across((terms_b[:1], terms_b[1:]), 2)

time: 166 us -> 174 us (1.048)
  waiting for transfers between devices: 53.1 us -> 81.6 us
  starting transfers between devices: 86.5 us -> 65.7 us
    ppermute x34, waiting for transfers between devices: 53.1 us -> 81.6 us  [move(): return lax.ppermute(value, ('band', 'grid'), pairs)]
    ppermute x34, starting transfers between devices: 86.5 us -> 65.7 us  [move(): return lax.ppermute(value, ('band', 'grid'), pairs)]
  transfers between devices with their start and end apart: 34 -> 34, of which waited for: 16 -> 15; matrix products, arithmetic and copies ran while one was open for 1% -> 1% of each run, Pallas kernels for 11% -> 11%
where the time goes in v5:
time: 174 us
  waiting for transfers between devices  81.6 us (47%)
  starting transfers between devices  65.7 us (38%)
  Pallas kernels  23.4 us (13%)
  local copies, waits for them, and re-layouts  2.51 us (1%)
    ppermute x34, waiting for transfers between devices, move(): return lax.ppermute(value, ('band', 'grid'), pairs)  81.6 us
    ppermute x34, starting transfers between devices, move(): return lax.ppermute(value, ('band', 'grid'), pairs)  65.7 us
    pallas_call x20, Pallas kernels, launch(): pl.pallas_call(ordered, grid=grid, in_specs=[*in_specs, *[unread] * waits...  23.4 us
  transfers between devices with their start and end apart: 34, of which 15 were waited for; matrix products, arithmetic and copies ran while one was open for 1% of the time, Pallas kernels for 11%

profile of v5, /device:TPU:1, one launch (start us, length us, event | category | flops | bytes accessed | tf_op | source)
XLA Modules:
  0.0 173.7 jit_solution(2425235398233578962)
XLA Ops:
  0.0 3.2 %collective-permute-start = (f32[8,512,128]{2,1,0:T(8,128)}, f32[8,512,128]{2,1,0:T(8,128)S(1)}, u32[]{:S(2)}, u32[]{:S(2)}) collective-permute-start(f32[8,512,128]{2,1,0:T(8,128)} %bitcast.10), channel_id=1, source_target_pairs={{0,1},{1,0},{2,3},{3,2},{4,5},{5,4},{6,7},{7,6},{8,9},{9,8},{10,11... | collective-permute-start | bytes 6291464 | tf_op jit(solution)/shard_map/ppermute | solution.py:454
  3.2 0.8 copy.11.refs_0_
  4.0 3.2 %collective-permute-done.refs_2_ = f32[8,512,128]{2,1,0:T(8,128)S(1)} collective-permute-done((f32[8,512,128]{2,1,0:T(8,128)}, f32[8,512,128]{2,1,0:T(8,128)S(1)}, u32[]{:S(2)}, u32[]{:S(2)}) %collective-permute-start) | collective-permute-done | bytes 2097184 | tf_op jit(solution)/shard_map/ppermute | solution.py:454
  7.2 1.6 copy-done.1
  8.8 1.5 pick.1
  10.3 0.8 collective-permute-start.2
  11.1 6.9 %collective-permute-start.1 = (f32[2,2,512,128]{3,2,1,0:T(8,128)S(1)}, f32[2,2,512,128]{3,2,1,0:T(8,128)S(1)}, u32[]{:S(2)}, u32[]{:S(2)}) collective-permute-start(f32[2,2,512,128]{3,2,1,0:T(8,128)S(1)} %get-tuple-element.76), channel_id=1, source_target_pairs={{0,32},{1,33},{2,34},{3,35},{4,36},{5,37},{6,38},{7,39},{8,40},{9,... | collective-permute-start | bytes 3145736 | tf_op jit(solution)/shard_map/ppermute | solution.py:454
  18.1 0.9 pick_own.1
  18.9 15.8 %collective-permute-done.2.refs_1_.refs_6_ = f32[2,2,512,128]{3,2,1,0:T(8,128)S(1)} collective-permute-done((f32[2,2,512,128]{3,2,1,0:T(8,128)S(1)}, f32[2,2,512,128]{3,2,1,0:T(8,128)S(1)}, u32[]{:S(2)}, u32[]{:S(2)}) %collective-permute-start.2) | collective-permute-done | bytes 1048608 | tf_op jit(solution)/shard_map/ppermute | solution.py:454
  34.8 4.0 %forward.3 = (f32[8,8,128,128]{3,2,1,0:T(8,128)S(1)}, f32[520,128]{1,0:T(8,128)S(1)}, f32[520,128]{1,0:T(8,128)S(1)}, f32[520,128]{1,0:T(8,128)S(1)}, f32[520,128]{1,0:T(8,128)S(1)}, /*index=5*/f32[8,128]{1,0:T(8,128)S(1)}) custom-call(f32[2,2,4,512,128]{4,3,2,1,0:T(8,128)S(1)} %get-tuple-element.75.refs_0_.refs_5_, ...), custom_call_target="tpu_custom_call" | custom-call | tf_op jit(solution)/shard_map/forward/pallas_call | solution.py:96
  38.8 0.1 collective-permute-start.3
  38.9 2.4 %collective-permute-start.4 = (f32[520,128]{1,0:T(8,128)S(1)}, f32[520,128]{1,0:T(8,128)S(1)}, u32[]{:S(2)}, u32[]{:S(2)}) collective-permute-start(f32[520,128]{1,0:T(8,128)S(1)} %get-tuple-element.81), channel_id=1, source_target_pairs={{0,4},{1,5},{2,6},{3,7},{4,0},{5,1},{6,2},{7,3},{8,12},{9,13},{10,... | collective-permute-start | bytes 798728 | tf_op jit(solution)/shard_map/ppermute | solution.py:454
  41.3 1.1 collective-permute-start.5
  42.4 4.6 %collective-permute-done.3.refs_1_ = f32[520,128]{1,0:T(8,128)S(1)} collective-permute-done((f32[520,128]{1,0:T(8,128)S(1)}, f32[520,128]{1,0:T(8,128)S(1)}, u32[]{:S(2)}, u32[]{:S(2)}) %collective-permute-start.3) | collective-permute-done | bytes 266272 | tf_op jit(solution)/shard_map/ppermute | solution.py:454
  47.0 5.3 %collective-permute-done.4.refs_2_ = f32[520,128]{1,0:T(8,128)S(1)} collective-permute-done((f32[520,128]{1,0:T(8,128)S(1)}, f32[520,128]{1,0:T(8,128)S(1)}, u32[]{:S(2)}, u32[]{:S(2)}) %collective-permute-start.4) | collective-permute-done | bytes 266272 | tf_op jit(solution)/shard_map/ppermute | solution.py:454
  52.3 1.4 collective-permute-done.5.refs_3_
  53.7 0.1 run.3
  53.8 0.4 collective-permute-start.9
  54.2 2.0 %forward.4 = (f32[4,8,128,128]{3,2,1,0:T(8,128)S(1)}, f32[264,128]{1,0:T(8,128)S(1)}, f32[264,128]{1,0:T(8,128)S(1)}, f32[264,128]{1,0:T(8,128)S(1)}, f32[264,128]{1,0:T(8,128)S(1)}, /*index=5*/f32[8,128]{1,0:T(8,128)S(1)}) custom-call(f32[2,2,4,512,128]{4,3,2,1,0:T(8,128)S(1)} %get-tuple-element.75.refs_0_.refs_5_, ...), custom_call_target="tpu_custom_call" | custom-call | tf_op jit(solution)/shard_map/forward/pallas_call | solution.py:96
  56.2 1.8 %collective-permute-start.10 = (f32[264,128]{1,0:T(8,128)S(1)}, f32[264,128]{1,0:T(8,128)S(1)}, u32[]{:S(2)}, u32[]{:S(2)}) collective-permute-start(f32[264,128]{1,0:T(8,128)S(1)} %get-tuple-element.93), channel_id=1, source_target_pairs={{0,2},{1,3},{2,4},{3,5},{4,6},{5,7},{6,0},{7,1},{8,10},{9,11},{10,... | collective-permute-start | bytes 405512 | tf_op jit(solution)/shard_map/ppermute | solution.py:454
  58.0 2.8 %collective-permute-start.11 = (f32[264,128]{1,0:T(8,128)S(1)}, f32[264,128]{1,0:T(8,128)S(1)}, u32[]{:S(2)}, u32[]{:S(2)}) collective-permute-start(f32[264,128]{1,0:T(8,128)S(1)} %get-tuple-element.94), channel_id=1, source_target_pairs={{0,4},{1,5},{2,6},{3,7},{4,0},{5,1},{6,2},{7,3},{8,12},{9,13},{10,... | collective-permute-start | bytes 405512 | tf_op jit(solution)/shard_map/ppermute | solution.py:454
  60.9 2.0 %forward.5 = (f32[4,8,128,128]{3,2,1,0:T(8,128)S(1)}, f32[264,128]{1,0:T(8,128)S(1)}, f32[264,128]{1,0:T(8,128)S(1)}, f32[264,128]{1,0:T(8,128)S(1)}, f32[264,128]{1,0:T(8,128)S(1)}, /*index=5*/f32[8,128]{1,0:T(8,128)S(1)}) custom-call(f32[2,2,4,512,128]{4,3,2,1,0:T(8,128)S(1)} %get-tuple-element.75.refs_0_.refs_5_, ...), custom_call_target="tpu_custom_call" | custom-call | tf_op jit(solution)/shard_map/forward/pallas_call | solution.py:96
  62.9 1.8 %collective-permute-done.11.refs_2_ = f32[264,128]{1,0:T(8,128)S(1)} collective-permute-done((f32[264,128]{1,0:T(8,128)S(1)}, f32[264,128]{1,0:T(8,128)S(1)}, u32[]{:S(2)}, u32[]{:S(2)}) %collective-permute-start.11) | collective-permute-done | bytes 135200 | tf_op jit(solution)/shard_map/ppermute | solution.py:454
  64.7 4.9 %collective-permute-done.9.refs_6_.refs_1_.refs_4_ = f32[520,128]{1,0:T(8,128)S(1)} collective-permute-done((f32[520,128]{1,0:T(8,128)S(1)}, f32[520,128]{1,0:T(8,128)S(1)}, u32[]{:S(2)}, u32[]{:S(2)}) %collective-permute-start.9) | collective-permute-done | bytes 266272 | tf_op jit(solution)/shard_map/ppermute | solution.py:454
  69.7 4.2 %collective-permute-start.13 = (f32[264,128]{1,0:T(8,128)S(1)}, f32[264,128]{1,0:T(8,128)S(1)}, u32[]{:S(2)}, u32[]{:S(2)}) collective-permute-start(f32[264,128]{1,0:T(8,128)S(1)} %get-tuple-element.97.refs_0_), channel_id=1, source_target_pairs={{0,8},{1,9},{2,10},{3,11},{4,12},{5,13},{6,14},{7,15},{8,0},{9,1},... | collective-permute-start | bytes 405512 | tf_op jit(solution)/shard_map/ppermute | solution.py:454
  73.9 0.5 collective-permute-start.6
  74.5 2.8 %collective-permute-start.7 = (f32[264,128]{1,0:T(8,128)S(1)}, f32[264,128]{1,0:T(8,128)S(1)}, u32[]{:S(2)}, u32[]{:S(2)}) collective-permute-start(f32[264,128]{1,0:T(8,128)S(1)} %get-tuple-element.89), channel_id=1, source_target_pairs={{0,4},{1,5},{2,6},{3,7},{4,0},{5,1},{6,2},{7,3},{8,12},{9,13},{10,... | collective-permute-start | bytes 405512 | tf_op jit(solution)/shard_map/ppermute | solution.py:454
  77.3 0.7 collective-permute-start.8
  78.1 5.2 %collective-permute-start.15 = (f32[264,128]{1,0:T(8,128)S(1)}, f32[264,128]{1,0:T(8,128)S(1)}, u32[]{:S(2)}, u32[]{:S(2)}) collective-permute-start(f32[264,128]{1,0:T(8,128)S(1)} %get-tuple-element.102.refs_5_), channel_id=1, source_target_pairs={{0,16},{1,17},{2,18},{3,19},{4,20},{5,21},{6,22},{7,23},{8,24},{9,... | collective-permute-start | bytes 405512 | tf_op jit(solution)/shard_map/ppermute | solution.py:454
  83.4 0.1 run.5
  83.4 1.4 collective-permute-start.14
  84.8 3.2 %collective-permute-start.23 = (f32[520,128]{1,0:T(8,128)S(1)}, f32[520,128]{1,0:T(8,128)S(1)}, u32[]{:S(2)}, u32[]{:S(2)}) collective-permute-start(f32[520,128]{1,0:T(8,128)S(1)} %get-tuple-element.120.refs_5_), channel_id=1, source_target_pairs={{0,16},{1,17},{2,18},{3,19},{4,20},{5,21},{6,22},{7,23},{8,24},{9,... | collective-permute-start | bytes 798728 | tf_op jit(solution)/shard_map/ppermute | solution.py:454
  88.0 0.2 edges.3
  88.1 2.1 %collective-permute-start.17 = (f32[264,128]{1,0:T(8,128)S(1)}, f32[264,128]{1,0:T(8,128)S(1)}, u32[]{:S(2)}, u32[]{:S(2)}) collective-permute-start(f32[264,128]{1,0:T(8,128)S(1)} %get-tuple-element.108), channel_id=1, source_target_pairs={{0,6},{1,7},{2,0},{3,1},{4,2},{5,3},{6,4},{7,5},{8,14},{9,15},{10,... | collective-permute-start | bytes 405512 | tf_op jit(solution)/shard_map/ppermute | solution.py:454
  90.2 1.1 collective-permute-start.18
  91.4 0.6 collective-permute-start.16
  92.0 1.6 collective-permute-done.17.refs_2_
  93.6 2.0 %collective-permute-done.18.refs_3_ = f32[264,128]{1,0:T(8,128)S(1)} collective-permute-done((f32[264,128]{1,0:T(8,128)S(1)}, f32[264,128]{1,0:T(8,128)S(1)}, u32[]{:S(2)}, u32[]{:S(2)}) %collective-permute-start.18) | collective-permute-done | bytes 135200 | tf_op jit(solution)/shard_map/ppermute | solution.py:454
  95.6 1.5 collective-permute-done.19.refs_4_
  97.2 9.0 %collective-permute-done.16.refs_12_.refs_6_ = f32[264,128]{1,0:T(8,128)S(1)} collective-permute-done((f32[264,128]{1,0:T(8,128)S(1)}, f32[264,128]{1,0:T(8,128)S(1)}, u32[]{:S(2)}, u32[]{:S(2)}) %collective-permute-start.16) | collective-permute-done | bytes 135200 | tf_op jit(solution)/shard_map/ppermute | solution.py:454
  106.2 2.0 %backward.3 = (f32[2,1,512,128]{3,2,1,0:T(8,128)S(1)}, f32[4,512,128]{2,1,0:T(8,128)S(1)}, f32[4,512,128]{2,1,0:T(8,128)S(1)}, f32[8,128]{1,0:T(8,128)S(1)}) custom-call(f32[4,8,128,128]{3,2,1,0:T(8,128)S(1)} %get-tuple-element.106.refs_0_, f32[264,128]{1,0:T(8,128)S(1)} %get-tuple-element.107.refs_1_, f32[264,128]{1,0:T(8,128)S(1)} %collective-permute-done.17.refs_2_, ...), custom_call_target="tpu_custom_call" | custom-call | tf_op jit(solution)/shard_map/backward/pallas_call | solution.py:96
  108.2 0.2 edges.4
  108.3 0.3 edges.5
  108.6 2.3 %collective-permute-start.24 = (f32[520,128]{1,0:T(8,128)S(1)}, f32[520,128]{1,0:T(8,128)S(1)}, u32[]{:S(2)}, u32[]{:S(2)}) collective-permute-start(f32[520,128]{1,0:T(8,128)S(1)} %get-tuple-element.123), channel_id=1, source_target_pairs={{0,6},{1,7},{2,0},{3,1},{4,2},{5,3},{6,4},{7,5},{8,14},{9,15},{10,... | collective-permute-start | bytes 798728 | tf_op jit(solution)/shard_map/ppermute | solution.py:454
  110.9 0.7 collective-permute-start.25
  111.6 4.3 %collective-permute-start.30 = (f32[2,1,512,128]{3,2,1,0:T(8,128)S(1)}, f32[2,1,512,128]{3,2,1,0:T(8,128)S(1)}, u32[]{:S(2)}, u32[]{:S(2)}) collective-permute-start(f32[2,1,512,128]{3,2,1,0:T(8,128)S(1)} %get-tuple-element.135), channel_id=1, source_target_pairs={{0,224},{1,225},{2,226},{3,227},{4,228},{5,229},{6,230},{7,231},{8... | collective-permute-start | bytes 1572872 | tf_op jit(solution)/shard_map/ppermute | solution.py:454
  115.9 0.5 collective-permute-start.26
  116.5 2.1 %collective-permute-start.20 = (f32[264,128]{1,0:T(8,128)S(1)}, f32[264,128]{1,0:T(8,128)S(1)}, u32[]{:S(2)}, u32[]{:S(2)}) collective-permute-start(f32[264,128]{1,0:T(8,128)S(1)} %get-tuple-element.114), channel_id=1, source_target_pairs={{0,6},{1,7},{2,0},{3,1},{4,2},{5,3},{6,4},{7,5},{8,14},{9,15},{10,... | collective-permute-start | bytes 405512 | tf_op jit(solution)/shard_map/ppermute | solution.py:454
  118.6 0.7 collective-permute-start.21
  119.3 1.6 collective-permute-start.22
  121.0 6.3 %collective-permute-done.26.refs_4_ = f32[520,128]{1,0:T(8,128)S(1)} collective-permute-done((f32[520,128]{1,0:T(8,128)S(1)}, f32[520,128]{1,0:T(8,128)S(1)}, u32[]{:S(2)}, u32[]{:S(2)}) %collective-permute-start.26) | collective-permute-done | bytes 266272 | tf_op jit(solution)/shard_map/ppermute | solution.py:454
  127.2 4.2 %backward.4 = (f32[2,2,512,128]{3,2,1,0:T(8,128)S(1)}, f32[4,512,128]{2,1,0:T(8,128)S(1)}, f32[4,512,128]{2,1,0:T(8,128)S(1)}, f32[8,128]{1,0:T(8,128)S(1)}) custom-call(f32[8,8,128,128]{3,2,1,0:T(8,128)S(1)} %get-tuple-element.119.refs_0_, f32[520,128]{1,0:T(8,128)S(1)} %get-tuple-element.122.refs_1_, f32[520,128]{1,0:T(8,128)S(1)} %collective-permute-done.24.refs_2_, ...), custom_call_target="tpu_custom_call" | custom-call | tf_op jit(solution)/shard_map/backward/pallas_call | solution.py:96
  131.5 2.1 %backward.5 = (f32[2,1,512,128]{3,2,1,0:T(8,128)S(1)}, f32[4,512,128]{2,1,0:T(8,128)S(1)}, f32[8,512,128]{2,1,0:T(8,128)S(1)}, f32[8,128]{1,0:T(8,128)S(1)}) custom-call(f32[4,8,128,128]{3,2,1,0:T(8,128)S(1)} %get-tuple-element.86.refs_0_, f32[264,128]{1,0:T(8,128)S(1)} %get-tuple-element.113.refs_1_, f32[264,128]{1,0:T(8,128)S(1)} %collective-permute-done.20.refs_2_, ...), custom_call_target="tpu_custom_call" | custom-call | tf_op jit(solution)/shard_map/backward/pallas_call | solution.py:96
  133.6 7.0 %collective-permute-start.33 = (f32[1,1,512,128]{3,2,1,0:T(8,128)S(1)}, f32[1,1,512,128]{3,2,1,0:T(8,128)S(1)}, u32[]{:S(2)}, u32[]{:S(2)}) collective-permute-start(f32[1,1,512,128]{3,2,1,0:T(8,128)S(1)} %get-tuple-element.143), channel_id=1, source_target_pairs={{0,225},{1,224},{2,227},{3,226},{4,229},{5,228},{6,231},{7,230},{8... | collective-permute-start | bytes 786440 | tf_op jit(solution)/shard_map/ppermute | solution.py:454
  140.6 3.0 %collective-permute-start.32 = (f32[1,1,512,128]{3,2,1,0:T(8,128)S(1)}, f32[1,1,512,128]{3,2,1,0:T(8,128)S(1)}, u32[]{:S(2)}, u32[]{:S(2)}) collective-permute-start(f32[1,1,512,128]{3,2,1,0:T(8,128)S(1)} %get-tuple-element.144), channel_id=1, source_target_pairs={{0,224},{1,225},{2,226},{3,227},{4,228},{5,229},{6,230},{7,231},{8... | collective-permute-start | bytes 786440 | tf_op jit(solution)/shard_map/ppermute | solution.py:454
  143.7 0.1 collective-permute-start.31
  143.9 1.4 collective-permute-start.29
  145.2 0.1 collective-permute-done.31.refs_6_
  145.3 0.4 collective-permute-start.27
  145.7 0.8 add_early.1
  146.5 13.2 %collective-permute-done.29.refs_4_ = f32[1,2,512,128]{3,2,1,0:T(8,128)S(1)} collective-permute-done((f32[1,2,512,128]{3,2,1,0:T(8,128)S(1)}, f32[1,2,512,128]{3,2,1,0:T(8,128)S(1)}, u32[]{:S(2)}, u32[]{:S(2)}) %collective-permute-start.29) | collective-permute-done | bytes 524320 | tf_op jit(solution)/shard_map/ppermute | solution.py:454
  159.7 10.8 %collective-permute-done.28.refs_3_ = f32[1,2,512,128]{3,2,1,0:T(8,128)S(1)} collective-permute-done((f32[1,2,512,128]{3,2,1,0:T(8,128)S(1)}, f32[1,2,512,128]{3,2,1,0:T(8,128)S(1)}, u32[]{:S(2)}, u32[]{:S(2)}) %collective-permute-start.28) | collective-permute-done | bytes 524320 | tf_op jit(solution)/shard_map/ppermute | solution.py:454
  170.5 1.1 add_middle.1
  171.7 1.9 %add_late.1 = (f32[8,512,128]{2,1,0:T(8,128)}, f32[8,128]{1,0:T(8,128)}) custom-call(s32[4]{0:T(128)S(1)} %get-tuple-element.73.refs_0_, f32[8,512,128]{2,1,0:T(8,128)S(1)} %get-tuple-element.137.refs_1_, f32[1,1,512,128]{3,2,1,0:T(8,128)S(1)} %collective-permute-done.32.refs_2_, f32[1,1,512,128]{3,2,1,0:T(8,128)S(1)} %collective-permute-done.33.refs_3_, ...), custom_call_target="tpu_custom_call" | custom-call | tf_op jit(solution)/shard_map/add_late/pallas_call | solution.py:96
  (46 shorter events, 0.4 us)
Async XLA Ops:
  0.0 7.2 %collective-permute-start = (f32[8,512,128]{2,1,0:T(8,128)}, f32[8,512,128]{2,1,0:T(8,128)S(1)}, u32[]{:S(2)}, u32[]{:S(2)}) collective-permute-start(f32[8,512,128]{2,1,0:T(8,128)} %bitcast.10), channel_id=1, source_target_pairs={{0,1},{1,0},{2,3},{3,2},{4,5},{5,4},{6,7},{7,6},{8,9},{9,8},{10,11... | collective-permute-start | bytes 6291464 | tf_op jit(solution)/shard_map/ppermute | solution.py:454
  7.2 1.6 copy-start.1
  8.8 9.2 %copy-start.2 = (f32[8,4,16384]{2,1,0:T(4,128)S(1)}, f32[8,4,16384]{2,1,0:T(4,128)}, u32[]{:S(2)}) copy-start(f32[8,4,16384]{2,1,0:T(4,128)} %param.9) | copy-start | bytes 6291460
  10.3 24.5 %collective-permute-start.2 = (f32[2,2,512,128]{3,2,1,0:T(8,128)S(1)}, f32[2,2,512,128]{3,2,1,0:T(8,128)S(1)}, u32[]{:S(2)}, u32[]{:S(2)}) collective-permute-start(f32[2,2,512,128]{3,2,1,0:T(8,128)S(1)} %get-tuple-element.77), channel_id=1, source_target_pairs={{0,192},{1,193},{2,194},{3,195},{4,196},{5,197},{6,198},{7,199},{8... | collective-permute-start | bytes 3145736 | tf_op jit(solution)/shard_map/ppermute | solution.py:454
  11.1 43.0 %collective-permute-start.1 = (f32[2,2,512,128]{3,2,1,0:T(8,128)S(1)}, f32[2,2,512,128]{3,2,1,0:T(8,128)S(1)}, u32[]{:S(2)}, u32[]{:S(2)}) collective-permute-start(f32[2,2,512,128]{3,2,1,0:T(8,128)S(1)} %get-tuple-element.76), channel_id=1, source_target_pairs={{0,32},{1,33},{2,34},{3,35},{4,36},{5,37},{6,38},{7,39},{8,40},{9,... | collective-permute-start | bytes 3145736 | tf_op jit(solution)/shard_map/ppermute | solution.py:454
  18.0 16.7 %copy-start.4 = (bf16[256,256]{1,0:T(8,128)(2,1)S(1)}, bf16[256,256]{1,0:T(8,128)(2,1)}, u32[]{:S(2)}) copy-start(bf16[256,256]{1,0:T(8,128)(2,1)} %constant.15.clone.refs_3_.refs_8_) | copy-start | bytes 393220
  18.0 16.7 %copy-start.5 = (bf16[256,256]{1,0:T(8,128)(2,1)S(1)}, bf16[256,256]{1,0:T(8,128)(2,1)}, u32[]{:S(2)}) copy-start(bf16[256,256]{1,0:T(8,128)(2,1)} %constant.14.clone.refs_2_.refs_7_) | copy-start | bytes 393220
  18.0 16.7 %copy-start.6 = (f32[128,128]{1,0:T(8,128)S(1)}, f32[128,128]{1,0:T(8,128)}, u32[]{:S(2)}) copy-start(f32[128,128]{1,0:T(8,128)} %constant.16.clone.refs_4_.refs_9_) | copy-start | bytes 196612
  18.1 16.7 %copy-start.7 = (f32[128,128]{1,0:T(8,128)S(1)}, f32[128,128]{1,0:T(8,128)}, u32[]{:S(2)}) copy-start(f32[128,128]{1,0:T(8,128)} %constant.17.clone.refs_5_) | copy-start | bytes 196612
  34.8 18.9 %copy-start = (f32[4,128,128]{2,1,0:T(8,128)S(1)}, f32[4,128,128]{2,1,0:T(8,128)}, u32[]{:S(2)}) copy-start(f32[4,128,128]{2,1,0:T(8,128)} %constant.18.clone.refs_4_.refs_7_) | copy-start | bytes 786436
  38.8 8.2 %collective-permute-start.3 = (f32[520,128]{1,0:T(8,128)S(1)}, f32[520,128]{1,0:T(8,128)S(1)}, u32[]{:S(2)}, u32[]{:S(2)}) collective-permute-start(f32[520,128]{1,0:T(8,128)S(1)} %get-tuple-element.80), channel_id=1, source_target_pairs={{0,2},{1,3},{2,4},{3,5},{4,6},{5,7},{6,0},{7,1},{8,10},{9,11},{10,... | collective-permute-start | bytes 798728 | tf_op jit(solution)/shard_map/ppermute | solution.py:454
  38.9 13.4 %collective-permute-start.4 = (f32[520,128]{1,0:T(8,128)S(1)}, f32[520,128]{1,0:T(8,128)S(1)}, u32[]{:S(2)}, u32[]{:S(2)}) collective-permute-start(f32[520,128]{1,0:T(8,128)S(1)} %get-tuple-element.81), channel_id=1, source_target_pairs={{0,4},{1,5},{2,6},{3,7},{4,0},{5,1},{6,2},{7,3},{8,12},{9,13},{10,... | collective-permute-start | bytes 798728 | tf_op jit(solution)/shard_map/ppermute | solution.py:454
  41.3 12.3 %collective-permute-start.5 = (f32[520,128]{1,0:T(8,128)S(1)}, f32[520,128]{1,0:T(8,128)S(1)}, u32[]{:S(2)}, u32[]{:S(2)}) collective-permute-start(f32[520,128]{1,0:T(8,128)S(1)} %get-tuple-element.82), channel_id=1, source_target_pairs={{0,6},{1,7},{2,0},{3,1},{4,2},{5,3},{6,4},{7,5},{8,14},{9,15},{10,... | collective-permute-start | bytes 798728 | tf_op jit(solution)/shard_map/ppermute | solution.py:454
  53.8 15.9 %collective-permute-start.9 = (f32[520,128]{1,0:T(8,128)S(1)}, f32[520,128]{1,0:T(8,128)S(1)}, u32[]{:S(2)}, u32[]{:S(2)}) collective-permute-start(f32[520,128]{1,0:T(8,128)S(1)} %get-tuple-element.91.refs_0_), channel_id=1, source_target_pairs={{0,8},{1,9},{2,10},{3,11},{4,12},{5,13},{6,14},{7,15},{8,0},{9,1},... | collective-permute-start | bytes 798728 | tf_op jit(solution)/shard_map/ppermute | solution.py:454
  56.2 6.7 %collective-permute-start.10 = (f32[264,128]{1,0:T(8,128)S(1)}, f32[264,128]{1,0:T(8,128)S(1)}, u32[]{:S(2)}, u32[]{:S(2)}) collective-permute-start(f32[264,128]{1,0:T(8,128)S(1)} %get-tuple-element.93), channel_id=1, source_target_pairs={{0,2},{1,3},{2,4},{3,5},{4,6},{5,7},{6,0},{7,1},{8,10},{9,11},{10,... | collective-permute-start | bytes 405512 | tf_op jit(solution)/shard_map/ppermute | solution.py:454
  58.0 6.7 %collective-permute-start.11 = (f32[264,128]{1,0:T(8,128)S(1)}, f32[264,128]{1,0:T(8,128)S(1)}, u32[]{:S(2)}, u32[]{:S(2)}) collective-permute-start(f32[264,128]{1,0:T(8,128)S(1)} %get-tuple-element.94), channel_id=1, source_target_pairs={{0,4},{1,5},{2,6},{3,7},{4,0},{5,1},{6,2},{7,3},{8,12},{9,13},{10,... | collective-permute-start | bytes 405512 | tf_op jit(solution)/shard_map/ppermute | solution.py:454
  60.8 3.9 %collective-permute-start.12 = (f32[264,128]{1,0:T(8,128)S(1)}, f32[264,128]{1,0:T(8,128)S(1)}, u32[]{:S(2)}, u32[]{:S(2)}) collective-permute-start(f32[264,128]{1,0:T(8,128)S(1)} %get-tuple-element.95), channel_id=1, source_target_pairs={{0,6},{1,7},{2,0},{3,1},{4,2},{5,3},{6,4},{7,5},{8,14},{9,15},{10,... | collective-permute-start | bytes 405512 | tf_op jit(solution)/shard_map/ppermute | solution.py:454
  60.8 17.2 %copy-start.3 = (f32[3,128,128]{2,1,0:T(8,128)S(1)}, f32[3,128,128]{2,1,0:T(8,128)}, u32[]{:S(2)}) copy-start(f32[3,128,128]{2,1,0:T(8,128)} %constant.19.clone.refs_2_.refs_8_) | copy-start | bytes 589828
  69.7 36.5 %copy-start.8 = (f32[1,128]{1,0:T(1,128)S(1)}, f32[1,128]{1,0:T(1,128)}, u32[]{:S(2)}) copy-start(f32[1,128]{1,0:T(1,128)} %constant.20.clone.refs_10_) | copy-start | bytes 1540
  69.7 8.3 %collective-permute-start.13 = (f32[264,128]{1,0:T(8,128)S(1)}, f32[264,128]{1,0:T(8,128)S(1)}, u32[]{:S(2)}, u32[]{:S(2)}) collective-permute-start(f32[264,128]{1,0:T(8,128)S(1)} %get-tuple-element.97.refs_0_), channel_id=1, source_target_pairs={{0,8},{1,9},{2,10},{3,11},{4,12},{5,13},{6,14},{7,15},{8,0},{9,1},... | collective-permute-start | bytes 405512 | tf_op jit(solution)/shard_map/ppermute | solution.py:454
  73.9 9.4 %collective-permute-start.6 = (f32[264,128]{1,0:T(8,128)S(1)}, f32[264,128]{1,0:T(8,128)S(1)}, u32[]{:S(2)}, u32[]{:S(2)}) collective-permute-start(f32[264,128]{1,0:T(8,128)S(1)} %get-tuple-element.88), channel_id=1, source_target_pairs={{0,2},{1,3},{2,4},{3,5},{4,6},{5,7},{6,0},{7,1},{8,10},{9,11},{10,... | collective-permute-start | bytes 405512 | tf_op jit(solution)/shard_map/ppermute | solution.py:454
  74.5 8.9 %collective-permute-start.7 = (f32[264,128]{1,0:T(8,128)S(1)}, f32[264,128]{1,0:T(8,128)S(1)}, u32[]{:S(2)}, u32[]{:S(2)}) collective-permute-start(f32[264,128]{1,0:T(8,128)S(1)} %get-tuple-element.89), channel_id=1, source_target_pairs={{0,4},{1,5},{2,6},{3,7},{4,0},{5,1},{6,2},{7,3},{8,12},{9,13},{10,... | collective-permute-start | bytes 405512 | tf_op jit(solution)/shard_map/ppermute | solution.py:454
  77.3 6.1 %collective-permute-start.8 = (f32[264,128]{1,0:T(8,128)S(1)}, f32[264,128]{1,0:T(8,128)S(1)}, u32[]{:S(2)}, u32[]{:S(2)}) collective-permute-start(f32[264,128]{1,0:T(8,128)S(1)} %get-tuple-element.90), channel_id=1, source_target_pairs={{0,6},{1,7},{2,0},{3,1},{4,2},{5,3},{6,4},{7,5},{8,14},{9,15},{10,... | collective-permute-start | bytes 405512 | tf_op jit(solution)/shard_map/ppermute | solution.py:454
  78.1 9.9 %collective-permute-start.15 = (f32[264,128]{1,0:T(8,128)S(1)}, f32[264,128]{1,0:T(8,128)S(1)}, u32[]{:S(2)}, u32[]{:S(2)}) collective-permute-start(f32[264,128]{1,0:T(8,128)S(1)} %get-tuple-element.102.refs_5_), channel_id=1, source_target_pairs={{0,16},{1,17},{2,18},{3,19},{4,20},{5,21},{6,22},{7,23},{8,24},{9,... | collective-permute-start | bytes 405512 | tf_op jit(solution)/shard_map/ppermute | solution.py:454
  83.4 7.9 %collective-permute-start.14 = (f32[264,128]{1,0:T(8,128)S(1)}, f32[264,128]{1,0:T(8,128)S(1)}, u32[]{:S(2)}, u32[]{:S(2)}) collective-permute-start(f32[264,128]{1,0:T(8,128)S(1)} %get-tuple-element.101.refs_0_), channel_id=1, source_target_pairs={{0,8},{1,9},{2,10},{3,11},{4,12},{5,13},{6,14},{7,15},{8,0},{9,1},... | collective-permute-start | bytes 405512 | tf_op jit(solution)/shard_map/ppermute | solution.py:454
  84.8 23.5 %collective-permute-start.23 = (f32[520,128]{1,0:T(8,128)S(1)}, f32[520,128]{1,0:T(8,128)S(1)}, u32[]{:S(2)}, u32[]{:S(2)}) collective-permute-start(f32[520,128]{1,0:T(8,128)S(1)} %get-tuple-element.120.refs_5_), channel_id=1, source_target_pairs={{0,16},{1,17},{2,18},{3,19},{4,20},{5,21},{6,22},{7,23},{8,24},{9,... | collective-permute-start | bytes 798728 | tf_op jit(solution)/shard_map/ppermute | solution.py:454
  88.1 5.5 %collective-permute-start.17 = (f32[264,128]{1,0:T(8,128)S(1)}, f32[264,128]{1,0:T(8,128)S(1)}, u32[]{:S(2)}, u32[]{:S(2)}) collective-permute-start(f32[264,128]{1,0:T(8,128)S(1)} %get-tuple-element.108), channel_id=1, source_target_pairs={{0,6},{1,7},{2,0},{3,1},{4,2},{5,3},{6,4},{7,5},{8,14},{9,15},{10,... | collective-permute-start | bytes 405512 | tf_op jit(solution)/shard_map/ppermute | solution.py:454
  90.2 5.4 %collective-permute-start.18 = (f32[264,128]{1,0:T(8,128)S(1)}, f32[264,128]{1,0:T(8,128)S(1)}, u32[]{:S(2)}, u32[]{:S(2)}) collective-permute-start(f32[264,128]{1,0:T(8,128)S(1)} %get-tuple-element.109), channel_id=1, source_target_pairs={{0,4},{1,5},{2,6},{3,7},{4,0},{5,1},{6,2},{7,3},{8,12},{9,13},{10,... | collective-permute-start | bytes 405512 | tf_op jit(solution)/shard_map/ppermute | solution.py:454
  91.3 5.9 %collective-permute-start.19 = (f32[264,128]{1,0:T(8,128)S(1)}, f32[264,128]{1,0:T(8,128)S(1)}, u32[]{:S(2)}, u32[]{:S(2)}) collective-permute-start(f32[264,128]{1,0:T(8,128)S(1)} %get-tuple-element.110), channel_id=1, source_target_pairs={{0,2},{1,3},{2,4},{3,5},{4,6},{5,7},{6,0},{7,1},{8,10},{9,11},{10,... | collective-permute-start | bytes 405512 | tf_op jit(solution)/shard_map/ppermute | solution.py:454
  91.4 14.8 %collective-permute-start.16 = (f32[264,128]{1,0:T(8,128)S(1)}, f32[264,128]{1,0:T(8,128)S(1)}, u32[]{:S(2)}, u32[]{:S(2)}) collective-permute-start(f32[264,128]{1,0:T(8,128)S(1)} %get-tuple-element.105.refs_5_), channel_id=1, source_target_pairs={{0,16},{1,17},{2,18},{3,19},{4,20},{5,21},{6,22},{7,23},{8,24},{9,... | collective-permute-start | bytes 405512 | tf_op jit(solution)/shard_map/ppermute | solution.py:454
  108.6 10.0 %collective-permute-start.24 = (f32[520,128]{1,0:T(8,128)S(1)}, f32[520,128]{1,0:T(8,128)S(1)}, u32[]{:S(2)}, u32[]{:S(2)}) collective-permute-start(f32[520,128]{1,0:T(8,128)S(1)} %get-tuple-element.123), channel_id=1, source_target_pairs={{0,6},{1,7},{2,0},{3,1},{4,2},{5,3},{6,4},{7,5},{8,14},{9,15},{10,... | collective-permute-start | bytes 798728 | tf_op jit(solution)/shard_map/ppermute | solution.py:454
  110.9 8.4 %collective-permute-start.25 = (f32[520,128]{1,0:T(8,128)S(1)}, f32[520,128]{1,0:T(8,128)S(1)}, u32[]{:S(2)}, u32[]{:S(2)}) collective-permute-start(f32[520,128]{1,0:T(8,128)S(1)} %get-tuple-element.124), channel_id=1, source_target_pairs={{0,4},{1,5},{2,6},{3,7},{4,0},{5,1},{6,2},{7,3},{8,12},{9,13},{10,... | collective-permute-start | bytes 798728 | tf_op jit(solution)/shard_map/ppermute | solution.py:454
  111.6 32.1 %collective-permute-start.30 = (f32[2,1,512,128]{3,2,1,0:T(8,128)S(1)}, f32[2,1,512,128]{3,2,1,0:T(8,128)S(1)}, u32[]{:S(2)}, u32[]{:S(2)}) collective-permute-start(f32[2,1,512,128]{3,2,1,0:T(8,128)S(1)} %get-tuple-element.135), channel_id=1, source_target_pairs={{0,224},{1,225},{2,226},{3,227},{4,228},{5,229},{6,230},{7,231},{8... | collective-permute-start | bytes 1572872 | tf_op jit(solution)/shard_map/ppermute | solution.py:454
  115.9 11.3 %collective-permute-start.26 = (f32[520,128]{1,0:T(8,128)S(1)}, f32[520,128]{1,0:T(8,128)S(1)}, u32[]{:S(2)}, u32[]{:S(2)}) collective-permute-start(f32[520,128]{1,0:T(8,128)S(1)} %get-tuple-element.125), channel_id=1, source_target_pairs={{0,2},{1,3},{2,4},{3,5},{4,6},{5,7},{6,0},{7,1},{8,10},{9,11},{10,... | collective-permute-start | bytes 798728 | tf_op jit(solution)/shard_map/ppermute | solution.py:454
  116.5 15.0 %collective-permute-start.20 = (f32[264,128]{1,0:T(8,128)S(1)}, f32[264,128]{1,0:T(8,128)S(1)}, u32[]{:S(2)}, u32[]{:S(2)}) collective-permute-start(f32[264,128]{1,0:T(8,128)S(1)} %get-tuple-element.114), channel_id=1, source_target_pairs={{0,6},{1,7},{2,0},{3,1},{4,2},{5,3},{6,4},{7,5},{8,14},{9,15},{10,... | collective-permute-start | bytes 405512 | tf_op jit(solution)/shard_map/ppermute | solution.py:454
  118.6 12.8 %collective-permute-start.21 = (f32[264,128]{1,0:T(8,128)S(1)}, f32[264,128]{1,0:T(8,128)S(1)}, u32[]{:S(2)}, u32[]{:S(2)}) collective-permute-start(f32[264,128]{1,0:T(8,128)S(1)} %get-tuple-element.115), channel_id=1, source_target_pairs={{0,4},{1,5},{2,6},{3,7},{4,0},{5,1},{6,2},{7,3},{8,12},{9,13},{10,... | collective-permute-start | bytes 405512 | tf_op jit(solution)/shard_map/ppermute | solution.py:454
  119.3 12.1 %collective-permute-start.22 = (f32[264,128]{1,0:T(8,128)S(1)}, f32[264,128]{1,0:T(8,128)S(1)}, u32[]{:S(2)}, u32[]{:S(2)}) collective-permute-start(f32[264,128]{1,0:T(8,128)S(1)} %get-tuple-element.116), channel_id=1, source_target_pairs={{0,2},{1,3},{2,4},{3,5},{4,6},{5,7},{6,0},{7,1},{8,10},{9,11},{10,... | collective-permute-start | bytes 405512 | tf_op jit(solution)/shard_map/ppermute | solution.py:454
  133.6 38.0 %collective-permute-start.33 = (f32[1,1,512,128]{3,2,1,0:T(8,128)S(1)}, f32[1,1,512,128]{3,2,1,0:T(8,128)S(1)}, u32[]{:S(2)}, u32[]{:S(2)}) collective-permute-start(f32[1,1,512,128]{3,2,1,0:T(8,128)S(1)} %get-tuple-element.143), channel_id=1, source_target_pairs={{0,225},{1,224},{2,227},{3,226},{4,229},{5,228},{6,231},{7,230},{8... | collective-permute-start | bytes 786440 | tf_op jit(solution)/shard_map/ppermute | solution.py:454
  140.6 31.0 %collective-permute-start.32 = (f32[1,1,512,128]{3,2,1,0:T(8,128)S(1)}, f32[1,1,512,128]{3,2,1,0:T(8,128)S(1)}, u32[]{:S(2)}, u32[]{:S(2)}) collective-permute-start(f32[1,1,512,128]{3,2,1,0:T(8,128)S(1)} %get-tuple-element.144), channel_id=1, source_target_pairs={{0,224},{1,225},{2,226},{3,227},{4,228},{5,229},{6,230},{7,231},{8... | collective-permute-start | bytes 786440 | tf_op jit(solution)/shard_map/ppermute | solution.py:454
  143.7 1.6 collective-permute-start.31
  143.9 15.8 %collective-permute-start.29 = (f32[1,2,512,128]{3,2,1,0:T(8,128)S(1)}, f32[1,2,512,128]{3,2,1,0:T(8,128)S(1)}, u32[]{:S(2)}, u32[]{:S(2)}) collective-permute-start(f32[1,2,512,128]{3,2,1,0:T(8,128)S(1)} %get-tuple-element.141), channel_id=1, source_target_pairs={{0,65},{1,64},{2,67},{3,66},{4,69},{5,68},{6,71},{7,70},{8,73},{9,... | collective-permute-start | bytes 1572872 | tf_op jit(solution)/shard_map/ppermute | solution.py:454
  145.2 25.3 %collective-permute-start.28 = (f32[1,2,512,128]{3,2,1,0:T(8,128)S(1)}, f32[1,2,512,128]{3,2,1,0:T(8,128)S(1)}, u32[]{:S(2)}, u32[]{:S(2)}) collective-permute-start(f32[1,2,512,128]{3,2,1,0:T(8,128)S(1)} %get-tuple-element.142), channel_id=1, source_target_pairs={{0,64},{1,65},{2,66},{3,67},{4,68},{5,69},{6,70},{7,71},{8,72},{9,... | collective-permute-start | bytes 1572872 | tf_op jit(solution)/shard_map/ppermute | solution.py:454
  145.3 25.2 %collective-permute-start.27 = (f32[8,512,128]{2,1,0:T(8,128)S(1)}, f32[8,512,128]{2,1,0:T(8,128)S(1)}, u32[]{:S(2)}, u32[]{:S(2)}) collective-permute-start(f32[8,512,128]{2,1,0:T(8,128)S(1)} %get-tuple-element.133), channel_id=1, source_target_pairs={{0,1},{1,0},{2,3},{3,2},{4,5},{5,4},{6,7},{7,6},{8,9},{9,8},{10,11... | collective-permute-start | bytes 6291464 | tf_op jit(solution)/shard_map/ppermute | solution.py:454

commit v6 on v5

--- a/solution.py
+++ b/solution.py
@@ -524,10 +524,10 @@
     run(last)
     edges(first)
     two(last)
+    edges(second)
     terms_a, sums_a = finish(first, after=[chains[last]["far"]])
     back_a = shift(terms_a, -1)
     edges(last)
-    edges(second)
     terms_b, sums_b = finish(second)
     terms_a, sums_a = finish(last, sums_a, sums_b[1:])
     final = there_and_across((terms_a[:1], terms_a[1:]), -1)

time: 174 us -> 207 us (1.19)
  the two profiles are of different devices: /device:TPU:1 before, /device:TPU:97 now
where the time goes in v6:
time: 207 us
  starting transfers between devices  93.8 us (45%)
  waiting for transfers between devices  87.1 us (42%)
  Pallas kernels  23.3 us (11%)
  local copies, waits for them, and re-layouts  2.51 us (1%)
    ppermute x34, starting transfers between devices, move(): return lax.ppermute(value, ('band', 'grid'), pairs)  93.8 us
    ppermute x34, waiting for transfers between devices, move(): return lax.ppermute(value, ('band', 'grid'), pairs)  87.1 us
    pallas_call x20, Pallas kernels, launch(): pl.pallas_call(ordered, grid=grid, in_specs=[*in_specs, *[unread] * waits...  23.3 us
  transfers between devices with their start and end apart: 34, of which 16 were waited for; matrix products, arithmetic and copies ran while one was open for 0% of the time, Pallas kernels for 10%

profile of v6, /device:TPU:97, one launch (start us, length us, event | category | flops | bytes accessed | tf_op | source)
XLA Modules:
  0.0 207.2 jit_solution(5029024727548728966)
XLA Ops:
  0.0 0.7 collective-permute-start
  0.7 0.8 copy.11.refs_0_
  1.4 3.2 %collective-permute-done.refs_2_ = f32[8,512,128]{2,1,0:T(8,128)S(1)} collective-permute-done((f32[8,512,128]{2,1,0:T(8,128)}, f32[8,512,128]{2,1,0:T(8,128)S(1)}, u32[]{:S(2)}, u32[]{:S(2)}) %collective-permute-start) | collective-permute-done | bytes 2097184 | tf_op jit(solution)/shard_map/ppermute | solution.py:454
  4.7 1.6 copy-done.1
  6.3 1.5 pick.1
  7.7 2.6 %collective-permute-start.2 = (f32[2,2,512,128]{3,2,1,0:T(8,128)S(1)}, f32[2,2,512,128]{3,2,1,0:T(8,128)S(1)}, u32[]{:S(2)}, u32[]{:S(2)}) collective-permute-start(f32[2,2,512,128]{3,2,1,0:T(8,128)S(1)} %get-tuple-element.77), channel_id=1, source_target_pairs={{0,192},{1,193},{2,194},{3,195},{4,196},{5,197},{6,198},{7,199},{8... | collective-permute-start | bytes 3145736 | tf_op jit(solution)/shard_map/ppermute | solution.py:454
  10.3 4.2 %collective-permute-start.1 = (f32[2,2,512,128]{3,2,1,0:T(8,128)S(1)}, f32[2,2,512,128]{3,2,1,0:T(8,128)S(1)}, u32[]{:S(2)}, u32[]{:S(2)}) collective-permute-start(f32[2,2,512,128]{3,2,1,0:T(8,128)S(1)} %get-tuple-element.76), channel_id=1, source_target_pairs={{0,32},{1,33},{2,34},{3,35},{4,36},{5,37},{6,38},{7,39},{8,40},{9,... | collective-permute-start | bytes 3145736 | tf_op jit(solution)/shard_map/ppermute | solution.py:454
  14.5 0.9 pick_own.1
  15.4 17.1 %collective-permute-done.2.refs_1_.refs_6_ = f32[2,2,512,128]{3,2,1,0:T(8,128)S(1)} collective-permute-done((f32[2,2,512,128]{3,2,1,0:T(8,128)S(1)}, f32[2,2,512,128]{3,2,1,0:T(8,128)S(1)}, u32[]{:S(2)}, u32[]{:S(2)}) %collective-permute-start.2) | collective-permute-done | bytes 1048608 | tf_op jit(solution)/shard_map/ppermute | solution.py:454
  32.5 4.0 %forward.3 = (f32[8,8,128,128]{3,2,1,0:T(8,128)S(1)}, f32[520,128]{1,0:T(8,128)S(1)}, f32[520,128]{1,0:T(8,128)S(1)}, f32[520,128]{1,0:T(8,128)S(1)}, f32[520,128]{1,0:T(8,128)S(1)}, /*index=5*/f32[8,128]{1,0:T(8,128)S(1)}) custom-call(f32[2,2,4,512,128]{4,3,2,1,0:T(8,128)S(1)} %get-tuple-element.75.refs_0_.refs_5_, ...), custom_call_target="tpu_custom_call" | custom-call | tf_op jit(solution)/shard_map/forward/pallas_call | solution.py:96
  36.5 1.4 collective-permute-start.3
  37.9 2.6 %collective-permute-start.4 = (f32[520,128]{1,0:T(8,128)S(1)}, f32[520,128]{1,0:T(8,128)S(1)}, u32[]{:S(2)}, u32[]{:S(2)}) collective-permute-start(f32[520,128]{1,0:T(8,128)S(1)} %get-tuple-element.81), channel_id=1, source_target_pairs={{0,4},{1,5},{2,6},{3,7},{4,0},{5,1},{6,2},{7,3},{8,12},{9,13},{10,... | collective-permute-start | bytes 798728 | tf_op jit(solution)/shard_map/ppermute | solution.py:454
  40.5 1.1 collective-permute-start.5
  41.6 3.0 %collective-permute-done.3.refs_1_ = f32[520,128]{1,0:T(8,128)S(1)} collective-permute-done((f32[520,128]{1,0:T(8,128)S(1)}, f32[520,128]{1,0:T(8,128)S(1)}, u32[]{:S(2)}, u32[]{:S(2)}) %collective-permute-start.3) | collective-permute-done | bytes 266272 | tf_op jit(solution)/shard_map/ppermute | solution.py:454
  44.6 6.8 %collective-permute-done.4.refs_2_ = f32[520,128]{1,0:T(8,128)S(1)} collective-permute-done((f32[520,128]{1,0:T(8,128)S(1)}, f32[520,128]{1,0:T(8,128)S(1)}, u32[]{:S(2)}, u32[]{:S(2)}) %collective-permute-start.4) | collective-permute-done | bytes 266272 | tf_op jit(solution)/shard_map/ppermute | solution.py:454
  51.5 0.1 run.3
  51.6 0.1 collective-permute-start.9
  51.7 11.3 %collective-permute-done.1.refs_1_.refs_6_ = f32[2,2,512,128]{3,2,1,0:T(8,128)S(1)} collective-permute-done((f32[2,2,512,128]{3,2,1,0:T(8,128)S(1)}, f32[2,2,512,128]{3,2,1,0:T(8,128)S(1)}, u32[]{:S(2)}, u32[]{:S(2)}) %collective-permute-start.1) | collective-permute-done | bytes 1048608 | tf_op jit(solution)/shard_map/ppermute | solution.py:454
  63.0 2.0 forward.4
  65.0 1.3 collective-permute-start.10
  66.3 2.6 %collective-permute-start.11 = (f32[264,128]{1,0:T(8,128)S(1)}, f32[264,128]{1,0:T(8,128)S(1)}, u32[]{:S(2)}, u32[]{:S(2)}) collective-permute-start(f32[264,128]{1,0:T(8,128)S(1)} %get-tuple-element.94), channel_id=1, source_target_pairs={{0,4},{1,5},{2,6},{3,7},{4,0},{5,1},{6,2},{7,3},{8,12},{9,13},{10,... | collective-permute-start | bytes 405512 | tf_op jit(solution)/shard_map/ppermute | solution.py:454
  69.0 1.1 collective-permute-start.12
  70.1 2.0 forward.5
  72.1 0.8 collective-permute-done.11.refs_2_
  72.9 0.3 collective-permute-done.12.refs_3_
  73.3 1.6 collective-permute-start.13
  74.9 1.1 collective-permute-start.6
  76.0 2.2 %collective-permute-start.7 = (f32[264,128]{1,0:T(8,128)S(1)}, f32[264,128]{1,0:T(8,128)S(1)}, u32[]{:S(2)}, u32[]{:S(2)}) collective-permute-start(f32[264,128]{1,0:T(8,128)S(1)} %get-tuple-element.89), channel_id=1, source_target_pairs={{0,4},{1,5},{2,6},{3,7},{4,0},{5,1},{6,2},{7,3},{8,12},{9,13},{10,... | collective-permute-start | bytes 405512 | tf_op jit(solution)/shard_map/ppermute | solution.py:454
  78.2 0.8 collective-permute-start.8
  79.0 0.1 collective-permute-start.15
  79.2 2.4 %collective-permute-start.20 = (f32[520,128]{1,0:T(8,128)S(1)}, f32[520,128]{1,0:T(8,128)S(1)}, u32[]{:S(2)}, u32[]{:S(2)}) collective-permute-start(f32[520,128]{1,0:T(8,128)S(1)} %get-tuple-element.111.refs_5_), channel_id=1, source_target_pairs={{0,16},{1,17},{2,18},{3,19},{4,20},{5,21},{6,22},{7,23},{8,24},{9,... | collective-permute-start | bytes 798728 | tf_op jit(solution)/shard_map/ppermute | solution.py:454
  81.6 0.5 collective-permute-done.7.refs_2_
  82.1 0.3 collective-permute-done.8.refs_3_
  82.4 0.1 collective-permute-start.14
  82.5 11.5 %collective-permute-done.15.refs_6_ = f32[264,128]{1,0:T(8,128)S(1)} collective-permute-done((f32[264,128]{1,0:T(8,128)S(1)}, f32[264,128]{1,0:T(8,128)S(1)}, u32[]{:S(2)}, u32[]{:S(2)}) %collective-permute-start.15) | collective-permute-done | bytes 135200 | tf_op jit(solution)/shard_map/ppermute | solution.py:454
  94.0 0.2 edges.3
  94.2 0.1 collective-permute-start.17
  94.3 2.6 %collective-permute-start.18 = (f32[264,128]{1,0:T(8,128)S(1)}, f32[264,128]{1,0:T(8,128)S(1)}, u32[]{:S(2)}, u32[]{:S(2)}) collective-permute-start(f32[264,128]{1,0:T(8,128)S(1)} %get-tuple-element.109), channel_id=1, source_target_pairs={{0,4},{1,5},{2,6},{3,7},{4,0},{5,1},{6,2},{7,3},{8,12},{9,13},{10,... | collective-permute-start | bytes 405512 | tf_op jit(solution)/shard_map/ppermute | solution.py:454
  96.9 0.1 collective-permute-start.16
  97.0 4.2 %collective-permute-done.20.refs_6_ = f32[520,128]{1,0:T(8,128)S(1)} collective-permute-done((f32[520,128]{1,0:T(8,128)S(1)}, f32[520,128]{1,0:T(8,128)S(1)}, u32[]{:S(2)}, u32[]{:S(2)}) %collective-permute-start.20) | collective-permute-done | bytes 266272 | tf_op jit(solution)/shard_map/ppermute | solution.py:454
  101.2 0.3 edges.4
  101.4 0.1 collective-permute-start.24
  101.5 2.5 %collective-permute-start.25 = (f32[520,128]{1,0:T(8,128)S(1)}, f32[520,128]{1,0:T(8,128)S(1)}, u32[]{:S(2)}, u32[]{:S(2)}) collective-permute-start(f32[520,128]{1,0:T(8,128)S(1)} %get-tuple-element.124), channel_id=1, source_target_pairs={{0,4},{1,5},{2,6},{3,7},{4,0},{5,1},{6,2},{7,3},{8,12},{9,13},{10,... | collective-permute-start | bytes 798728 | tf_op jit(solution)/shard_map/ppermute | solution.py:454
  104.1 2.0 backward.3
  106.1 3.8 %collective-permute-start.30 = (f32[2,1,512,128]{3,2,1,0:T(8,128)S(1)}, f32[2,1,512,128]{3,2,1,0:T(8,128)S(1)}, u32[]{:S(2)}, u32[]{:S(2)}) collective-permute-start(f32[2,1,512,128]{3,2,1,0:T(8,128)S(1)} %get-tuple-element.135), channel_id=1, source_target_pairs={{0,224},{1,225},{2,226},{3,227},{4,228},{5,229},{6,230},{7,231},{8... | collective-permute-start | bytes 1572872 | tf_op jit(solution)/shard_map/ppermute | solution.py:454
  110.0 1.5 collective-permute-start.26
  111.5 0.2 edges.5
  111.6 1.3 collective-permute-start.21
  112.9 0.7 collective-permute-start.22
  113.6 0.5 collective-permute-start.23
  114.1 2.4 %collective-permute-done.26.refs_4_ = f32[520,128]{1,0:T(8,128)S(1)} collective-permute-done((f32[520,128]{1,0:T(8,128)S(1)}, f32[520,128]{1,0:T(8,128)S(1)}, u32[]{:S(2)}, u32[]{:S(2)}) %collective-permute-start.26) | collective-permute-done | bytes 266272 | tf_op jit(solution)/shard_map/ppermute | solution.py:454
  116.5 4.2 %backward.4 = (f32[2,2,512,128]{3,2,1,0:T(8,128)S(1)}, f32[4,512,128]{2,1,0:T(8,128)S(1)}, f32[4,512,128]{2,1,0:T(8,128)S(1)}, f32[8,128]{1,0:T(8,128)S(1)}) custom-call(f32[8,8,128,128]{3,2,1,0:T(8,128)S(1)} %get-tuple-element.121.refs_0_, f32[520,128]{1,0:T(8,128)S(1)} %get-tuple-element.122.refs_1_, f32[520,128]{1,0:T(8,128)S(1)} %collective-permute-done.24.refs_2_, ...), custom_call_target="tpu_custom_call" | custom-call | tf_op jit(solution)/shard_map/backward/pallas_call | solution.py:96
  120.7 2.1 %backward.5 = (f32[2,1,512,128]{3,2,1,0:T(8,128)S(1)}, f32[4,512,128]{2,1,0:T(8,128)S(1)}, f32[8,512,128]{2,1,0:T(8,128)S(1)}, f32[8,128]{1,0:T(8,128)S(1)}) custom-call(f32[4,8,128,128]{3,2,1,0:T(8,128)S(1)} %get-tuple-element.86.refs_0_, f32[264,128]{1,0:T(8,128)S(1)} %get-tuple-element.115.refs_1_, f32[264,128]{1,0:T(8,128)S(1)} %collective-permute-done.21.refs_2_, ...), custom_call_target="tpu_custom_call" | custom-call | tf_op jit(solution)/shard_map/backward/pallas_call | solution.py:96
  122.8 47.0 %collective-permute-start.33 = (f32[1,1,512,128]{3,2,1,0:T(8,128)S(1)}, f32[1,1,512,128]{3,2,1,0:T(8,128)S(1)}, u32[]{:S(2)}, u32[]{:S(2)}) collective-permute-start(f32[1,1,512,128]{3,2,1,0:T(8,128)S(1)} %get-tuple-element.143), channel_id=1, source_target_pairs={{0,225},{1,224},{2,227},{3,226},{4,229},{5,228},{6,231},{7,230},{8... | collective-permute-start | bytes 786440 | tf_op jit(solution)/shard_map/ppermute | solution.py:454
  169.9 7.3 %collective-permute-start.32 = (f32[1,1,512,128]{3,2,1,0:T(8,128)S(1)}, f32[1,1,512,128]{3,2,1,0:T(8,128)S(1)}, u32[]{:S(2)}, u32[]{:S(2)}) collective-permute-start(f32[1,1,512,128]{3,2,1,0:T(8,128)S(1)} %get-tuple-element.144), channel_id=1, source_target_pairs={{0,224},{1,225},{2,226},{3,227},{4,228},{5,229},{6,230},{7,231},{8... | collective-permute-start | bytes 786440 | tf_op jit(solution)/shard_map/ppermute | solution.py:454
  177.2 0.1 collective-permute-start.31
  177.3 0.1 collective-permute-start.29
  177.5 1.3 collective-permute-done.31.refs_6_
  178.8 0.1 collective-permute-start.27
  178.9 0.8 add_early.1
  179.7 13.1 %collective-permute-done.29.refs_4_ = f32[1,2,512,128]{3,2,1,0:T(8,128)S(1)} collective-permute-done((f32[1,2,512,128]{3,2,1,0:T(8,128)S(1)}, f32[1,2,512,128]{3,2,1,0:T(8,128)S(1)}, u32[]{:S(2)}, u32[]{:S(2)}) %collective-permute-start.29) | collective-permute-done | bytes 524320 | tf_op jit(solution)/shard_map/ppermute | solution.py:454
  192.9 11.1 %collective-permute-done.28.refs_3_ = f32[1,2,512,128]{3,2,1,0:T(8,128)S(1)} collective-permute-done((f32[1,2,512,128]{3,2,1,0:T(8,128)S(1)}, f32[1,2,512,128]{3,2,1,0:T(8,128)S(1)}, u32[]{:S(2)}, u32[]{:S(2)}) %collective-permute-start.28) | collective-permute-done | bytes 524320 | tf_op jit(solution)/shard_map/ppermute | solution.py:454
  204.0 1.1 add_middle.1
  205.1 1.9 add_late.1
  (46 shorter events, 0.7 us)
Async XLA Ops:
  0.0 4.7 %collective-permute-start = (f32[8,512,128]{2,1,0:T(8,128)}, f32[8,512,128]{2,1,0:T(8,128)S(1)}, u32[]{:S(2)}, u32[]{:S(2)}) collective-permute-start(f32[8,512,128]{2,1,0:T(8,128)} %bitcast.10), channel_id=1, source_target_pairs={{0,1},{1,0},{2,3},{3,2},{4,5},{5,4},{6,7},{7,6},{8,9},{9,8},{10,11... | collective-permute-start | bytes 6291464 | tf_op jit(solution)/shard_map/ppermute | solution.py:454
  4.7 1.6 copy-start.1
  6.3 8.3 %copy-start.2 = (f32[8,4,16384]{2,1,0:T(4,128)S(1)}, f32[8,4,16384]{2,1,0:T(4,128)}, u32[]{:S(2)}) copy-start(f32[8,4,16384]{2,1,0:T(4,128)} %param.9) | copy-start | bytes 6291460
  7.7 24.7 %collective-permute-start.2 = (f32[2,2,512,128]{3,2,1,0:T(8,128)S(1)}, f32[2,2,512,128]{3,2,1,0:T(8,128)S(1)}, u32[]{:S(2)}, u32[]{:S(2)}) collective-permute-start(f32[2,2,512,128]{3,2,1,0:T(8,128)S(1)} %get-tuple-element.77), channel_id=1, source_target_pairs={{0,192},{1,193},{2,194},{3,195},{4,196},{5,197},{6,198},{7,199},{8... | collective-permute-start | bytes 3145736 | tf_op jit(solution)/shard_map/ppermute | solution.py:454
  10.3 52.7 %collective-permute-start.1 = (f32[2,2,512,128]{3,2,1,0:T(8,128)S(1)}, f32[2,2,512,128]{3,2,1,0:T(8,128)S(1)}, u32[]{:S(2)}, u32[]{:S(2)}) collective-permute-start(f32[2,2,512,128]{3,2,1,0:T(8,128)S(1)} %get-tuple-element.76), channel_id=1, source_target_pairs={{0,32},{1,33},{2,34},{3,35},{4,36},{5,37},{6,38},{7,39},{8,40},{9,... | collective-permute-start | bytes 3145736 | tf_op jit(solution)/shard_map/ppermute | solution.py:454
  14.5 18.0 %copy-start.4 = (bf16[256,256]{1,0:T(8,128)(2,1)S(1)}, bf16[256,256]{1,0:T(8,128)(2,1)}, u32[]{:S(2)}) copy-start(bf16[256,256]{1,0:T(8,128)(2,1)} %constant.15.clone.refs_3_.refs_8_) | copy-start | bytes 393220
  14.5 18.0 %copy-start.5 = (bf16[256,256]{1,0:T(8,128)(2,1)S(1)}, bf16[256,256]{1,0:T(8,128)(2,1)}, u32[]{:S(2)}) copy-start(bf16[256,256]{1,0:T(8,128)(2,1)} %constant.14.clone.refs_2_.refs_7_) | copy-start | bytes 393220
  14.5 18.0 %copy-start.6 = (f32[128,128]{1,0:T(8,128)S(1)}, f32[128,128]{1,0:T(8,128)}, u32[]{:S(2)}) copy-start(f32[128,128]{1,0:T(8,128)} %constant.16.clone.refs_4_.refs_9_) | copy-start | bytes 196612
  14.5 18.0 %copy-start.7 = (f32[128,128]{1,0:T(8,128)S(1)}, f32[128,128]{1,0:T(8,128)}, u32[]{:S(2)}) copy-start(f32[128,128]{1,0:T(8,128)} %constant.17.clone.refs_5_) | copy-start | bytes 196612
  32.5 19.0 %copy-start = (f32[4,128,128]{2,1,0:T(8,128)S(1)}, f32[4,128,128]{2,1,0:T(8,128)}, u32[]{:S(2)}) copy-start(f32[4,128,128]{2,1,0:T(8,128)} %constant.18.clone.refs_4_.refs_7_) | copy-start | bytes 786436
  36.5 8.1 %collective-permute-start.3 = (f32[520,128]{1,0:T(8,128)S(1)}, f32[520,128]{1,0:T(8,128)S(1)}, u32[]{:S(2)}, u32[]{:S(2)}) collective-permute-start(f32[520,128]{1,0:T(8,128)S(1)} %get-tuple-element.80), channel_id=1, source_target_pairs={{0,2},{1,3},{2,4},{3,5},{4,6},{5,7},{6,0},{7,1},{8,10},{9,11},{10,... | collective-permute-start | bytes 798728 | tf_op jit(solution)/shard_map/ppermute | solution.py:454
  37.9 13.5 %collective-permute-start.4 = (f32[520,128]{1,0:T(8,128)S(1)}, f32[520,128]{1,0:T(8,128)S(1)}, u32[]{:S(2)}, u32[]{:S(2)}) collective-permute-start(f32[520,128]{1,0:T(8,128)S(1)} %get-tuple-element.81), channel_id=1, source_target_pairs={{0,4},{1,5},{2,6},{3,7},{4,0},{5,1},{6,2},{7,3},{8,12},{9,13},{10,... | collective-permute-start | bytes 798728 | tf_op jit(solution)/shard_map/ppermute | solution.py:454
  40.5 11.0 %collective-permute-start.5 = (f32[520,128]{1,0:T(8,128)S(1)}, f32[520,128]{1,0:T(8,128)S(1)}, u32[]{:S(2)}, u32[]{:S(2)}) collective-permute-start(f32[520,128]{1,0:T(8,128)S(1)} %get-tuple-element.82), channel_id=1, source_target_pairs={{0,6},{1,7},{2,0},{3,1},{4,2},{5,3},{6,4},{7,5},{8,14},{9,15},{10,... | collective-permute-start | bytes 798728 | tf_op jit(solution)/shard_map/ppermute | solution.py:454
  51.6 21.6 %collective-permute-start.9 = (f32[520,128]{1,0:T(8,128)S(1)}, f32[520,128]{1,0:T(8,128)S(1)}, u32[]{:S(2)}, u32[]{:S(2)}) collective-permute-start(f32[520,128]{1,0:T(8,128)S(1)} %get-tuple-element.91.refs_0_), channel_id=1, source_target_pairs={{0,8},{1,9},{2,10},{3,11},{4,12},{5,13},{6,14},{7,15},{8,0},{9,1},... | collective-permute-start | bytes 798728 | tf_op jit(solution)/shard_map/ppermute | solution.py:454
  65.0 7.1 %collective-permute-start.10 = (f32[264,128]{1,0:T(8,128)S(1)}, f32[264,128]{1,0:T(8,128)S(1)}, u32[]{:S(2)}, u32[]{:S(2)}) collective-permute-start(f32[264,128]{1,0:T(8,128)S(1)} %get-tuple-element.93), channel_id=1, source_target_pairs={{0,2},{1,3},{2,4},{3,5},{4,6},{5,7},{6,0},{7,1},{8,10},{9,11},{10,... | collective-permute-start | bytes 405512 | tf_op jit(solution)/shard_map/ppermute | solution.py:454
  66.3 6.6 %collective-permute-start.11 = (f32[264,128]{1,0:T(8,128)S(1)}, f32[264,128]{1,0:T(8,128)S(1)}, u32[]{:S(2)}, u32[]{:S(2)}) collective-permute-start(f32[264,128]{1,0:T(8,128)S(1)} %get-tuple-element.94), channel_id=1, source_target_pairs={{0,4},{1,5},{2,6},{3,7},{4,0},{5,1},{6,2},{7,3},{8,12},{9,13},{10,... | collective-permute-start | bytes 405512 | tf_op jit(solution)/shard_map/ppermute | solution.py:454
  69.0 4.3 %collective-permute-start.12 = (f32[264,128]{1,0:T(8,128)S(1)}, f32[264,128]{1,0:T(8,128)S(1)}, u32[]{:S(2)}, u32[]{:S(2)}) collective-permute-start(f32[264,128]{1,0:T(8,128)S(1)} %get-tuple-element.95), channel_id=1, source_target_pairs={{0,6},{1,7},{2,0},{3,1},{4,2},{5,3},{6,4},{7,5},{8,14},{9,15},{10,... | collective-permute-start | bytes 405512 | tf_op jit(solution)/shard_map/ppermute | solution.py:454
  70.1 8.9 %copy-start.3 = (f32[3,128,128]{2,1,0:T(8,128)S(1)}, f32[3,128,128]{2,1,0:T(8,128)}, u32[]{:S(2)}) copy-start(f32[3,128,128]{2,1,0:T(8,128)} %constant.19.clone.refs_2_.refs_8_) | copy-start | bytes 589828
  73.3 5.7 %collective-permute-start.13 = (f32[264,128]{1,0:T(8,128)S(1)}, f32[264,128]{1,0:T(8,128)S(1)}, u32[]{:S(2)}, u32[]{:S(2)}) collective-permute-start(f32[264,128]{1,0:T(8,128)S(1)} %get-tuple-element.97.refs_0_), channel_id=1, source_target_pairs={{0,8},{1,9},{2,10},{3,11},{4,12},{5,13},{6,14},{7,15},{8,0},{9,1},... | collective-permute-start | bytes 405512 | tf_op jit(solution)/shard_map/ppermute | solution.py:454
  74.9 6.7 %collective-permute-start.6 = (f32[264,128]{1,0:T(8,128)S(1)}, f32[264,128]{1,0:T(8,128)S(1)}, u32[]{:S(2)}, u32[]{:S(2)}) collective-permute-start(f32[264,128]{1,0:T(8,128)S(1)} %get-tuple-element.88), channel_id=1, source_target_pairs={{0,2},{1,3},{2,4},{3,5},{4,6},{5,7},{6,0},{7,1},{8,10},{9,11},{10,... | collective-permute-start | bytes 405512 | tf_op jit(solution)/shard_map/ppermute | solution.py:454
  76.0 6.1 %collective-permute-start.7 = (f32[264,128]{1,0:T(8,128)S(1)}, f32[264,128]{1,0:T(8,128)S(1)}, u32[]{:S(2)}, u32[]{:S(2)}) collective-permute-start(f32[264,128]{1,0:T(8,128)S(1)} %get-tuple-element.89), channel_id=1, source_target_pairs={{0,4},{1,5},{2,6},{3,7},{4,0},{5,1},{6,2},{7,3},{8,12},{9,13},{10,... | collective-permute-start | bytes 405512 | tf_op jit(solution)/shard_map/ppermute | solution.py:454
  78.2 4.2 %collective-permute-start.8 = (f32[264,128]{1,0:T(8,128)S(1)}, f32[264,128]{1,0:T(8,128)S(1)}, u32[]{:S(2)}, u32[]{:S(2)}) collective-permute-start(f32[264,128]{1,0:T(8,128)S(1)} %get-tuple-element.90), channel_id=1, source_target_pairs={{0,6},{1,7},{2,0},{3,1},{4,2},{5,3},{6,4},{7,5},{8,14},{9,15},{10,... | collective-permute-start | bytes 405512 | tf_op jit(solution)/shard_map/ppermute | solution.py:454
  79.0 15.0 %collective-permute-start.15 = (f32[264,128]{1,0:T(8,128)S(1)}, f32[264,128]{1,0:T(8,128)S(1)}, u32[]{:S(2)}, u32[]{:S(2)}) collective-permute-start(f32[264,128]{1,0:T(8,128)S(1)} %get-tuple-element.102.refs_5_), channel_id=1, source_target_pairs={{0,16},{1,17},{2,18},{3,19},{4,20},{5,21},{6,22},{7,23},{8,24},{9,... | collective-permute-start | bytes 405512 | tf_op jit(solution)/shard_map/ppermute | solution.py:454
  79.2 22.0 %collective-permute-start.20 = (f32[520,128]{1,0:T(8,128)S(1)}, f32[520,128]{1,0:T(8,128)S(1)}, u32[]{:S(2)}, u32[]{:S(2)}) collective-permute-start(f32[520,128]{1,0:T(8,128)S(1)} %get-tuple-element.111.refs_5_), channel_id=1, source_target_pairs={{0,16},{1,17},{2,18},{3,19},{4,20},{5,21},{6,22},{7,23},{8,24},{9,... | collective-permute-start | bytes 798728 | tf_op jit(solution)/shard_map/ppermute | solution.py:454
  82.4 14.4 %collective-permute-start.14 = (f32[264,128]{1,0:T(8,128)S(1)}, f32[264,128]{1,0:T(8,128)S(1)}, u32[]{:S(2)}, u32[]{:S(2)}) collective-permute-start(f32[264,128]{1,0:T(8,128)S(1)} %get-tuple-element.101.refs_0_), channel_id=1, source_target_pairs={{0,8},{1,9},{2,10},{3,11},{4,12},{5,13},{6,14},{7,15},{8,0},{9,1},... | collective-permute-start | bytes 405512 | tf_op jit(solution)/shard_map/ppermute | solution.py:454
  94.0 10.2 %copy-start.8 = (f32[1,128]{1,0:T(1,128)S(1)}, f32[1,128]{1,0:T(1,128)}, u32[]{:S(2)}) copy-start(f32[1,128]{1,0:T(1,128)} %constant.20.clone.refs_10_) | copy-start | bytes 1540
  94.2 7.4 %collective-permute-start.17 = (f32[264,128]{1,0:T(8,128)S(1)}, f32[264,128]{1,0:T(8,128)S(1)}, u32[]{:S(2)}, u32[]{:S(2)}) collective-permute-start(f32[264,128]{1,0:T(8,128)S(1)} %get-tuple-element.108), channel_id=1, source_target_pairs={{0,6},{1,7},{2,0},{3,1},{4,2},{5,3},{6,4},{7,5},{8,14},{9,15},{10,... | collective-permute-start | bytes 405512 | tf_op jit(solution)/shard_map/ppermute | solution.py:454
  94.3 9.8 %collective-permute-start.18 = (f32[264,128]{1,0:T(8,128)S(1)}, f32[264,128]{1,0:T(8,128)S(1)}, u32[]{:S(2)}, u32[]{:S(2)}) collective-permute-start(f32[264,128]{1,0:T(8,128)S(1)} %get-tuple-element.109), channel_id=1, source_target_pairs={{0,4},{1,5},{2,6},{3,7},{4,0},{5,1},{6,2},{7,3},{8,12},{9,13},{10,... | collective-permute-start | bytes 405512 | tf_op jit(solution)/shard_map/ppermute | solution.py:454
  96.8 7.3 %collective-permute-start.19 = (f32[264,128]{1,0:T(8,128)S(1)}, f32[264,128]{1,0:T(8,128)S(1)}, u32[]{:S(2)}, u32[]{:S(2)}) collective-permute-start(f32[264,128]{1,0:T(8,128)S(1)} %get-tuple-element.110), channel_id=1, source_target_pairs={{0,2},{1,3},{2,4},{3,5},{4,6},{5,7},{6,0},{7,1},{8,10},{9,11},{10,... | collective-permute-start | bytes 405512 | tf_op jit(solution)/shard_map/ppermute | solution.py:454
  96.9 7.3 %collective-permute-start.16 = (f32[264,128]{1,0:T(8,128)S(1)}, f32[264,128]{1,0:T(8,128)S(1)}, u32[]{:S(2)}, u32[]{:S(2)}) collective-permute-start(f32[264,128]{1,0:T(8,128)S(1)} %get-tuple-element.105.refs_5_), channel_id=1, source_target_pairs={{0,16},{1,17},{2,18},{3,19},{4,20},{5,21},{6,22},{7,23},{8,24},{9,... | collective-permute-start | bytes 405512 | tf_op jit(solution)/shard_map/ppermute | solution.py:454
  101.4 11.5 %collective-permute-start.24 = (f32[520,128]{1,0:T(8,128)S(1)}, f32[520,128]{1,0:T(8,128)S(1)}, u32[]{:S(2)}, u32[]{:S(2)}) collective-permute-start(f32[520,128]{1,0:T(8,128)S(1)} %get-tuple-element.123), channel_id=1, source_target_pairs={{0,6},{1,7},{2,0},{3,1},{4,2},{5,3},{6,4},{7,5},{8,14},{9,15},{10,... | collective-permute-start | bytes 798728 | tf_op jit(solution)/shard_map/ppermute | solution.py:454
  101.5 12.1 %collective-permute-start.25 = (f32[520,128]{1,0:T(8,128)S(1)}, f32[520,128]{1,0:T(8,128)S(1)}, u32[]{:S(2)}, u32[]{:S(2)}) collective-permute-start(f32[520,128]{1,0:T(8,128)S(1)} %get-tuple-element.124), channel_id=1, source_target_pairs={{0,4},{1,5},{2,6},{3,7},{4,0},{5,1},{6,2},{7,3},{8,12},{9,13},{10,... | collective-permute-start | bytes 798728 | tf_op jit(solution)/shard_map/ppermute | solution.py:454
  106.1 71.0 %collective-permute-start.30 = (f32[2,1,512,128]{3,2,1,0:T(8,128)S(1)}, f32[2,1,512,128]{3,2,1,0:T(8,128)S(1)}, u32[]{:S(2)}, u32[]{:S(2)}) collective-permute-start(f32[2,1,512,128]{3,2,1,0:T(8,128)S(1)} %get-tuple-element.135), channel_id=1, source_target_pairs={{0,224},{1,225},{2,226},{3,227},{4,228},{5,229},{6,230},{7,231},{8... | collective-permute-start | bytes 1572872 | tf_op jit(solution)/shard_map/ppermute | solution.py:454
  110.0 6.5 %collective-permute-start.26 = (f32[520,128]{1,0:T(8,128)S(1)}, f32[520,128]{1,0:T(8,128)S(1)}, u32[]{:S(2)}, u32[]{:S(2)}) collective-permute-start(f32[520,128]{1,0:T(8,128)S(1)} %get-tuple-element.125), channel_id=1, source_target_pairs={{0,2},{1,3},{2,4},{3,5},{4,6},{5,7},{6,0},{7,1},{8,10},{9,11},{10,... | collective-permute-start | bytes 798728 | tf_op jit(solution)/shard_map/ppermute | solution.py:454
  111.6 9.0 %collective-permute-start.21 = (f32[264,128]{1,0:T(8,128)S(1)}, f32[264,128]{1,0:T(8,128)S(1)}, u32[]{:S(2)}, u32[]{:S(2)}) collective-permute-start(f32[264,128]{1,0:T(8,128)S(1)} %get-tuple-element.116), channel_id=1, source_target_pairs={{0,6},{1,7},{2,0},{3,1},{4,2},{5,3},{6,4},{7,5},{8,14},{9,15},{10,... | collective-permute-start | bytes 405512 | tf_op jit(solution)/shard_map/ppermute | solution.py:454
  112.9 7.8 %collective-permute-start.22 = (f32[264,128]{1,0:T(8,128)S(1)}, f32[264,128]{1,0:T(8,128)S(1)}, u32[]{:S(2)}, u32[]{:S(2)}) collective-permute-start(f32[264,128]{1,0:T(8,128)S(1)} %get-tuple-element.117), channel_id=1, source_target_pairs={{0,4},{1,5},{2,6},{3,7},{4,0},{5,1},{6,2},{7,3},{8,12},{9,13},{10,... | collective-permute-start | bytes 405512 | tf_op jit(solution)/shard_map/ppermute | solution.py:454
  113.6 7.1 %collective-permute-start.23 = (f32[264,128]{1,0:T(8,128)S(1)}, f32[264,128]{1,0:T(8,128)S(1)}, u32[]{:S(2)}, u32[]{:S(2)}) collective-permute-start(f32[264,128]{1,0:T(8,128)S(1)} %get-tuple-element.118), channel_id=1, source_target_pairs={{0,2},{1,3},{2,4},{3,5},{4,6},{5,7},{6,0},{7,1},{8,10},{9,11},{10,... | collective-permute-start | bytes 405512 | tf_op jit(solution)/shard_map/ppermute | solution.py:454
  122.8 82.3 %collective-permute-start.33 = (f32[1,1,512,128]{3,2,1,0:T(8,128)S(1)}, f32[1,1,512,128]{3,2,1,0:T(8,128)S(1)}, u32[]{:S(2)}, u32[]{:S(2)}) collective-permute-start(f32[1,1,512,128]{3,2,1,0:T(8,128)S(1)} %get-tuple-element.143), channel_id=1, source_target_pairs={{0,225},{1,224},{2,227},{3,226},{4,229},{5,228},{6,231},{7,230},{8... | collective-permute-start | bytes 786440 | tf_op jit(solution)/shard_map/ppermute | solution.py:454
  169.9 35.3 %collective-permute-start.32 = (f32[1,1,512,128]{3,2,1,0:T(8,128)S(1)}, f32[1,1,512,128]{3,2,1,0:T(8,128)S(1)}, u32[]{:S(2)}, u32[]{:S(2)}) collective-permute-start(f32[1,1,512,128]{3,2,1,0:T(8,128)S(1)} %get-tuple-element.144), channel_id=1, source_target_pairs={{0,224},{1,225},{2,226},{3,227},{4,228},{5,229},{6,230},{7,231},{8... | collective-permute-start | bytes 786440 | tf_op jit(solution)/shard_map/ppermute | solution.py:454
  177.2 1.6 collective-permute-start.31
  177.3 15.5 %collective-permute-start.29 = (f32[1,2,512,128]{3,2,1,0:T(8,128)S(1)}, f32[1,2,512,128]{3,2,1,0:T(8,128)S(1)}, u32[]{:S(2)}, u32[]{:S(2)}) collective-permute-start(f32[1,2,512,128]{3,2,1,0:T(8,128)S(1)} %get-tuple-element.141), channel_id=1, source_target_pairs={{0,65},{1,64},{2,67},{3,66},{4,69},{5,68},{6,71},{7,70},{8,73},{9,... | collective-permute-start | bytes 1572872 | tf_op jit(solution)/shard_map/ppermute | solution.py:454
  177.4 26.5 %collective-permute-start.28 = (f32[1,2,512,128]{3,2,1,0:T(8,128)S(1)}, f32[1,2,512,128]{3,2,1,0:T(8,128)S(1)}, u32[]{:S(2)}, u32[]{:S(2)}) collective-permute-start(f32[1,2,512,128]{3,2,1,0:T(8,128)S(1)} %get-tuple-element.142), channel_id=1, source_target_pairs={{0,64},{1,65},{2,66},{3,67},{4,68},{5,69},{6,70},{7,71},{8,72},{9,... | collective-permute-start | bytes 1572872 | tf_op jit(solution)/shard_map/ppermute | solution.py:454
  178.8 25.2 %collective-permute-start.27 = (f32[8,512,128]{2,1,0:T(8,128)S(1)}, f32[8,512,128]{2,1,0:T(8,128)S(1)}, u32[]{:S(2)}, u32[]{:S(2)}) collective-permute-start(f32[8,512,128]{2,1,0:T(8,128)S(1)} %get-tuple-element.133), channel_id=1, source_target_pairs={{0,1},{1,0},{2,3},{3,2},{4,5},{5,4},{6,7},{7,6},{8,9},{9,8},{10,11... | collective-permute-start | bytes 6291464 | tf_op jit(solution)/shard_map/ppermute | solution.py:454

commit v7 on v4

--- a/solution.py
+++ b/solution.py
@@ -529,7 +529,8 @@
     terms_a, sums_a = finish(first)
     back_a = shift(terms_a, -1)
     terms_a, sums_a = finish(last, sums_a, sums_b[1:])
-    final = there_and_across((terms_a[:1], terms_a[1:]), -1)
+    back_last = shift(terms_a, -1)
+    final = [back_last, swap_cores(back_last[1:])]
     back_b = there_and_across((terms_b[:1], terms_b[1:]), 2)
     total, token = add_early(token, index, [sums_a[0], sums_b[0]])
     total, token = add_middle(

time: 166 us -> 171 us (1.030)
  starting transfers between devices: 86.5 us -> 92.6 us
  waiting for transfers between devices: 53.1 us -> 50.8 us
    ppermute x34, starting transfers between devices: 86.5 us -> 92.6 us  [move(): return lax.ppermute(value, ('band', 'grid'), pairs)]
    ppermute x34, waiting for transfers between devices: 53.1 us -> 50.8 us  [move(): return lax.ppermute(value, ('band', 'grid'), pairs)]
  transfers between devices with their start and end apart: 34 -> 34, of which waited for: 16 -> 12; matrix products, arithmetic and copies ran while one was open for 1% -> 1% of each run, Pallas kernels for 11% -> 12%
where the time goes in v7:
time: 171 us; the launch traced here: 170 us
  starting transfers between devices  92.6 us (54%)
  waiting for transfers between devices  50.8 us (30%)
  Pallas kernels  23.5 us (14%)
  local copies, waits for them, and re-layouts  2.49 us (1%)
    ppermute x34, starting transfers between devices, move(): return lax.ppermute(value, ('band', 'grid'), pairs)  92.6 us
    ppermute x34, waiting for transfers between devices, move(): return lax.ppermute(value, ('band', 'grid'), pairs)  50.8 us
    pallas_call x20, Pallas kernels, launch(): pl.pallas_call(ordered, grid=grid, in_specs=[*in_specs, *[unread] * waits...  23.5 us
  transfers between devices with their start and end apart: 34, of which 12 were waited for; matrix products, arithmetic and copies ran while one was open for 1% of the time, Pallas kernels for 12%

profile of v7, /device:TPU:1, one launch (start us, length us, event | category | flops | bytes accessed | tf_op | source)
XLA Modules:
  0.0 169.9 jit_solution(5637246572480997641)
XLA Ops:
  0.0 3.2 %collective-permute-start = (f32[8,512,128]{2,1,0:T(8,128)}, f32[8,512,128]{2,1,0:T(8,128)S(1)}, u32[]{:S(2)}, u32[]{:S(2)}) collective-permute-start(f32[8,512,128]{2,1,0:T(8,128)} %bitcast.10), channel_id=1, source_target_pairs={{0,1},{1,0},{2,3},{3,2},{4,5},{5,4},{6,7},{7,6},{8,9},{9,8},{10,11... | collective-permute-start | bytes 6291464 | tf_op jit(solution)/shard_map/ppermute | solution.py:453
  3.2 0.8 copy.11.refs_0_
  4.0 3.2 %collective-permute-done.refs_2_ = f32[8,512,128]{2,1,0:T(8,128)S(1)} collective-permute-done((f32[8,512,128]{2,1,0:T(8,128)}, f32[8,512,128]{2,1,0:T(8,128)S(1)}, u32[]{:S(2)}, u32[]{:S(2)}) %collective-permute-start) | collective-permute-done | bytes 2097184 | tf_op jit(solution)/shard_map/ppermute | solution.py:453
  7.2 1.6 copy-done.1
  8.8 1.5 pick.1
  10.3 0.8 collective-permute-start.2
  11.1 6.9 %collective-permute-start.1 = (f32[2,2,512,128]{3,2,1,0:T(8,128)S(1)}, f32[2,2,512,128]{3,2,1,0:T(8,128)S(1)}, u32[]{:S(2)}, u32[]{:S(2)}) collective-permute-start(f32[2,2,512,128]{3,2,1,0:T(8,128)S(1)} %get-tuple-element.76), channel_id=1, source_target_pairs={{0,32},{1,33},{2,34},{3,35},{4,36},{5,37},{6,38},{7,39},{8,40},{9,... | collective-permute-start | bytes 3145736 | tf_op jit(solution)/shard_map/ppermute | solution.py:453
  18.1 0.9 pick_own.1
  18.9 15.8 %collective-permute-done.2.refs_1_.refs_6_ = f32[2,2,512,128]{3,2,1,0:T(8,128)S(1)} collective-permute-done((f32[2,2,512,128]{3,2,1,0:T(8,128)S(1)}, f32[2,2,512,128]{3,2,1,0:T(8,128)S(1)}, u32[]{:S(2)}, u32[]{:S(2)}) %collective-permute-start.2) | collective-permute-done | bytes 1048608 | tf_op jit(solution)/shard_map/ppermute | solution.py:453
  34.8 4.0 %forward.3 = (f32[8,8,128,128]{3,2,1,0:T(8,128)S(1)}, f32[520,128]{1,0:T(8,128)S(1)}, f32[520,128]{1,0:T(8,128)S(1)}, f32[520,128]{1,0:T(8,128)S(1)}, f32[520,128]{1,0:T(8,128)S(1)}, /*index=5*/f32[8,128]{1,0:T(8,128)S(1)}) custom-call(f32[2,2,4,512,128]{4,3,2,1,0:T(8,128)S(1)} %get-tuple-element.75.refs_0_.refs_5_, ...), custom_call_target="tpu_custom_call" | custom-call | tf_op jit(solution)/shard_map/forward/pallas_call | solution.py:96
  38.8 0.1 collective-permute-start.3
  38.9 2.4 %collective-permute-start.4 = (f32[520,128]{1,0:T(8,128)S(1)}, f32[520,128]{1,0:T(8,128)S(1)}, u32[]{:S(2)}, u32[]{:S(2)}) collective-permute-start(f32[520,128]{1,0:T(8,128)S(1)} %get-tuple-element.81), channel_id=1, source_target_pairs={{0,4},{1,5},{2,6},{3,7},{4,0},{5,1},{6,2},{7,3},{8,12},{9,13},{10,... | collective-permute-start | bytes 798728 | tf_op jit(solution)/shard_map/ppermute | solution.py:453
  41.4 1.1 collective-permute-start.5
  42.4 4.6 %collective-permute-done.3.refs_1_ = f32[520,128]{1,0:T(8,128)S(1)} collective-permute-done((f32[520,128]{1,0:T(8,128)S(1)}, f32[520,128]{1,0:T(8,128)S(1)}, u32[]{:S(2)}, u32[]{:S(2)}) %collective-permute-start.3) | collective-permute-done | bytes 266272 | tf_op jit(solution)/shard_map/ppermute | solution.py:453
  47.0 5.3 %collective-permute-done.4.refs_2_ = f32[520,128]{1,0:T(8,128)S(1)} collective-permute-done((f32[520,128]{1,0:T(8,128)S(1)}, f32[520,128]{1,0:T(8,128)S(1)}, u32[]{:S(2)}, u32[]{:S(2)}) %collective-permute-start.4) | collective-permute-done | bytes 266272 | tf_op jit(solution)/shard_map/ppermute | solution.py:453
  52.4 1.4 collective-permute-done.5.refs_3_
  53.7 0.1 run.3
  53.8 0.4 collective-permute-start.6
  54.2 2.0 %forward.4 = (f32[4,8,128,128]{3,2,1,0:T(8,128)S(1)}, f32[264,128]{1,0:T(8,128)S(1)}, f32[264,128]{1,0:T(8,128)S(1)}, f32[264,128]{1,0:T(8,128)S(1)}, f32[264,128]{1,0:T(8,128)S(1)}, /*index=5*/f32[8,128]{1,0:T(8,128)S(1)}) custom-call(f32[2,2,4,512,128]{4,3,2,1,0:T(8,128)S(1)} %get-tuple-element.75.refs_0_.refs_5_, ...), custom_call_target="tpu_custom_call" | custom-call | tf_op jit(solution)/shard_map/forward/pallas_call | solution.py:96
  56.2 1.8 %collective-permute-start.10 = (f32[264,128]{1,0:T(8,128)S(1)}, f32[264,128]{1,0:T(8,128)S(1)}, u32[]{:S(2)}, u32[]{:S(2)}) collective-permute-start(f32[264,128]{1,0:T(8,128)S(1)} %get-tuple-element.94), channel_id=1, source_target_pairs={{0,2},{1,3},{2,4},{3,5},{4,6},{5,7},{6,0},{7,1},{8,10},{9,11},{10,... | collective-permute-start | bytes 405512 | tf_op jit(solution)/shard_map/ppermute | solution.py:453
  58.1 2.8 %collective-permute-start.11 = (f32[264,128]{1,0:T(8,128)S(1)}, f32[264,128]{1,0:T(8,128)S(1)}, u32[]{:S(2)}, u32[]{:S(2)}) collective-permute-start(f32[264,128]{1,0:T(8,128)S(1)} %get-tuple-element.95), channel_id=1, source_target_pairs={{0,4},{1,5},{2,6},{3,7},{4,0},{5,1},{6,2},{7,3},{8,12},{9,13},{10,... | collective-permute-start | bytes 405512 | tf_op jit(solution)/shard_map/ppermute | solution.py:453
  60.9 8.7 %collective-permute-done.6.refs_1_.refs_4_ = f32[520,128]{1,0:T(8,128)S(1)} collective-permute-done((f32[520,128]{1,0:T(8,128)S(1)}, f32[520,128]{1,0:T(8,128)S(1)}, u32[]{:S(2)}, u32[]{:S(2)}) %collective-permute-start.6) | collective-permute-done | bytes 266272 | tf_op jit(solution)/shard_map/ppermute | solution.py:453
  69.7 0.1 two.3
  69.7 4.5 %collective-permute-start.15 = (f32[520,128]{1,0:T(8,128)S(1)}, f32[520,128]{1,0:T(8,128)S(1)}, u32[]{:S(2)}, u32[]{:S(2)}) collective-permute-start(f32[520,128]{1,0:T(8,128)S(1)} %get-tuple-element.101.refs_5_), channel_id=1, source_target_pairs={{0,16},{1,17},{2,18},{3,19},{4,20},{5,21},{6,22},{7,23},{8,24},{9,... | collective-permute-start | bytes 798728 | tf_op jit(solution)/shard_map/ppermute | solution.py:453
  74.2 2.0 %forward.5 = (f32[4,8,128,128]{3,2,1,0:T(8,128)S(1)}, f32[264,128]{1,0:T(8,128)S(1)}, f32[264,128]{1,0:T(8,128)S(1)}, f32[264,128]{1,0:T(8,128)S(1)}, f32[264,128]{1,0:T(8,128)S(1)}, /*index=5*/f32[8,128]{1,0:T(8,128)S(1)}) custom-call(f32[2,2,4,512,128]{4,3,2,1,0:T(8,128)S(1)} %get-tuple-element.75.refs_0_.refs_5_, ...), custom_call_target="tpu_custom_call" | custom-call | tf_op jit(solution)/shard_map/forward/pallas_call | solution.py:96
  76.2 0.5 collective-permute-start.7
  76.7 0.8 collective-permute-start.8
  77.5 1.7 %collective-permute-start.9 = (f32[264,128]{1,0:T(8,128)S(1)}, f32[264,128]{1,0:T(8,128)S(1)}, u32[]{:S(2)}, u32[]{:S(2)}) collective-permute-start(f32[264,128]{1,0:T(8,128)S(1)} %get-tuple-element.92), channel_id=1, source_target_pairs={{0,6},{1,7},{2,0},{3,1},{4,2},{5,3},{6,4},{7,5},{8,14},{9,15},{10,... | collective-permute-start | bytes 405512 | tf_op jit(solution)/shard_map/ppermute | solution.py:453
  79.2 1.7 %collective-permute-start.14 = (f32[264,128]{1,0:T(8,128)S(1)}, f32[264,128]{1,0:T(8,128)S(1)}, u32[]{:S(2)}, u32[]{:S(2)}) collective-permute-start(f32[264,128]{1,0:T(8,128)S(1)} %get-tuple-element.100.refs_0_), channel_id=1, source_target_pairs={{0,8},{1,9},{2,10},{3,11},{4,12},{5,13},{6,14},{7,15},{8,0},{9,1},... | collective-permute-start | bytes 405512 | tf_op jit(solution)/shard_map/ppermute | solution.py:453
  81.0 1.3 collective-permute-done.7.refs_1_
  82.2 1.4 collective-permute-done.8.refs_2_
  83.6 0.4 collective-permute-done.9.refs_3_
  84.1 1.1 collective-permute-start.13
  85.3 0.3 edges.3
  85.6 1.5 collective-permute-done.14.refs_1_.refs_4_
  87.1 1.6 collective-permute-start.20
  88.7 1.8 %collective-permute-start.17 = (f32[520,128]{1,0:T(8,128)S(1)}, f32[520,128]{1,0:T(8,128)S(1)}, u32[]{:S(2)}, u32[]{:S(2)}) collective-permute-start(f32[520,128]{1,0:T(8,128)S(1)} %get-tuple-element.108), channel_id=1, source_target_pairs={{0,6},{1,7},{2,0},{3,1},{4,2},{5,3},{6,4},{7,5},{8,14},{9,15},{10,... | collective-permute-start | bytes 798728 | tf_op jit(solution)/shard_map/ppermute | solution.py:453
  90.5 0.8 collective-permute-start.18
  91.3 0.9 collective-permute-start.19
  92.2 1.3 collective-permute-start.16
  93.5 0.2 edges.4
  93.7 3.0 %collective-permute-start.24 = (f32[264,128]{1,0:T(8,128)S(1)}, f32[264,128]{1,0:T(8,128)S(1)}, u32[]{:S(2)}, u32[]{:S(2)}) collective-permute-start(f32[264,128]{1,0:T(8,128)S(1)} %get-tuple-element.121), channel_id=1, source_target_pairs={{0,6},{1,7},{2,0},{3,1},{4,2},{5,3},{6,4},{7,5},{8,14},{9,15},{10,... | collective-permute-start | bytes 405512 | tf_op jit(solution)/shard_map/ppermute | solution.py:453
  96.7 0.9 collective-permute-start.25
  97.6 5.1 %collective-permute-start.26 = (f32[264,128]{1,0:T(8,128)S(1)}, f32[264,128]{1,0:T(8,128)S(1)}, u32[]{:S(2)}, u32[]{:S(2)}) collective-permute-start(f32[264,128]{1,0:T(8,128)S(1)} %get-tuple-element.123), channel_id=1, source_target_pairs={{0,2},{1,3},{2,4},{3,5},{4,6},{5,7},{6,0},{7,1},{8,10},{9,11},{10,... | collective-permute-start | bytes 405512 | tf_op jit(solution)/shard_map/ppermute | solution.py:453
  102.7 3.5 %collective-permute-done.19.refs_4_ = f32[520,128]{1,0:T(8,128)S(1)} collective-permute-done((f32[520,128]{1,0:T(8,128)S(1)}, f32[520,128]{1,0:T(8,128)S(1)}, u32[]{:S(2)}, u32[]{:S(2)}) %collective-permute-start.19) | collective-permute-done | bytes 266272 | tf_op jit(solution)/shard_map/ppermute | solution.py:453
  106.2 4.2 %backward.3 = (f32[2,2,512,128]{3,2,1,0:T(8,128)S(1)}, f32[4,512,128]{2,1,0:T(8,128)S(1)}, f32[4,512,128]{2,1,0:T(8,128)S(1)}, f32[8,128]{1,0:T(8,128)S(1)}) custom-call(f32[8,8,128,128]{3,2,1,0:T(8,128)S(1)} %get-tuple-element.106.refs_0_, f32[520,128]{1,0:T(8,128)S(1)} %get-tuple-element.107.refs_1_, f32[520,128]{1,0:T(8,128)S(1)} %collective-permute-done.17.refs_2_, ...), custom_call_target="tpu_custom_call" | custom-call | tf_op jit(solution)/shard_map/backward/pallas_call | solution.py:96
  110.5 0.2 edges.5
  110.7 0.1 collective-permute-start.21
  110.8 0.8 collective-permute-start.22
  111.6 0.8 collective-permute-start.23
  112.4 2.0 %backward.4 = (f32[2,1,512,128]{3,2,1,0:T(8,128)S(1)}, f32[4,512,128]{2,1,0:T(8,128)S(1)}, f32[4,512,128]{2,1,0:T(8,128)S(1)}, f32[8,128]{1,0:T(8,128)S(1)}) custom-call(f32[4,8,128,128]{3,2,1,0:T(8,128)S(1)} %get-tuple-element.119.refs_0_, f32[264,128]{1,0:T(8,128)S(1)} %get-tuple-element.120.refs_1_, f32[264,128]{1,0:T(8,128)S(1)} %collective-permute-done.24.refs_2_, ...), custom_call_target="tpu_custom_call" | custom-call | tf_op jit(solution)/shard_map/backward/pallas_call | solution.py:96
  114.4 5.6 %collective-permute-start.30 = (f32[2,1,512,128]{3,2,1,0:T(8,128)S(1)}, f32[2,1,512,128]{3,2,1,0:T(8,128)S(1)}, u32[]{:S(2)}, u32[]{:S(2)}) collective-permute-start(f32[2,1,512,128]{3,2,1,0:T(8,128)S(1)} %get-tuple-element.135), channel_id=1, source_target_pairs={{0,224},{1,225},{2,226},{3,227},{4,228},{5,229},{6,230},{7,231},{8... | collective-permute-start | bytes 1572872 | tf_op jit(solution)/shard_map/ppermute | solution.py:453
  120.0 2.1 %backward.5 = (f32[2,1,512,128]{3,2,1,0:T(8,128)S(1)}, f32[4,512,128]{2,1,0:T(8,128)S(1)}, f32[8,512,128]{2,1,0:T(8,128)S(1)}, f32[8,128]{1,0:T(8,128)S(1)}) custom-call(f32[4,8,128,128]{3,2,1,0:T(8,128)S(1)} %get-tuple-element.88.refs_0_, f32[264,128]{1,0:T(8,128)S(1)} %get-tuple-element.115.refs_1_, f32[264,128]{1,0:T(8,128)S(1)} %collective-permute-done.21.refs_2_, ...), custom_call_target="tpu_custom_call" | custom-call | tf_op jit(solution)/shard_map/backward/pallas_call | solution.py:96
  122.1 3.9 %collective-permute-start.32 = (f32[2,1,512,128]{3,2,1,0:T(8,128)S(1)}, f32[2,1,512,128]{3,2,1,0:T(8,128)S(1)}, u32[]{:S(2)}, u32[]{:S(2)}) collective-permute-start(f32[2,1,512,128]{3,2,1,0:T(8,128)S(1)} %get-tuple-element.138), channel_id=1, source_target_pairs={{0,224},{1,225},{2,226},{3,227},{4,228},{5,229},{6,230},{7,231},{8... | collective-permute-start | bytes 1572872 | tf_op jit(solution)/shard_map/ppermute | solution.py:453
  126.0 0.1 fusion
  126.1 0.1 collective-permute-start.28
  126.2 3.4 %collective-permute-start.29 = (f32[1,2,512,128]{3,2,1,0:T(8,128)S(1)}, f32[1,2,512,128]{3,2,1,0:T(8,128)S(1)}, u32[]{:S(2)}, u32[]{:S(2)}) collective-permute-start(f32[1,2,512,128]{3,2,1,0:T(8,128)S(1)} %get-tuple-element.141), channel_id=1, source_target_pairs={{0,65},{1,64},{2,67},{3,66},{4,69},{5,68},{6,71},{7,70},{8,73},{9,... | collective-permute-start | bytes 1572872 | tf_op jit(solution)/shard_map/ppermute | solution.py:453
  129.6 0.6 collective-permute-start.27
  130.2 9.7 %collective-permute-start.31 = (f32[1,1,512,128]{3,2,1,0:T(8,128)S(1)}, f32[1,1,512,128]{3,2,1,0:T(8,128)S(1)}, u32[]{:S(2)}, u32[]{:S(2)}) collective-permute-start(f32[1,1,512,128]{3,2,1,0:T(8,128)S(1)} %slice.16), channel_id=1, source_target_pairs={{0,1},{1,0},{2,3},{3,2},{4,5},{5,4},{6,7},{7,6},{8,9},{9,8},{10,11... | collective-permute-start | bytes 786440 | tf_op jit(solution)/shard_map/ppermute | solution.py:453
  139.9 3.6 %collective-permute-done.32.refs_2_ = f32[2,1,512,128]{3,2,1,0:T(8,128)S(1)} collective-permute-done((f32[2,1,512,128]{3,2,1,0:T(8,128)S(1)}, f32[2,1,512,128]{3,2,1,0:T(8,128)S(1)}, u32[]{:S(2)}, u32[]{:S(2)}) %collective-permute-start.32) | collective-permute-done | bytes 524320 | tf_op jit(solution)/shard_map/ppermute | solution.py:453
  143.5 22.3 %collective-permute-start.33 = (f32[1,1,512,128]{3,2,1,0:T(8,128)S(1)}, f32[1,1,512,128]{3,2,1,0:T(8,128)S(1)}, u32[]{:S(2)}, u32[]{:S(2)}) collective-permute-start(f32[1,1,512,128]{3,2,1,0:T(8,128)S(1)} %slice.17), channel_id=1, source_target_pairs={{0,1},{1,0},{2,3},{3,2},{4,5},{5,4},{6,7},{7,6},{8,9},{9,8},{10,11... | collective-permute-start | bytes 786440 | tf_op jit(solution)/shard_map/ppermute | solution.py:453
  165.8 0.8 add_early.1
  166.6 1.1 add_middle.1
  167.8 1.9 %add_late.1 = (f32[8,512,128]{2,1,0:T(8,128)}, f32[8,128]{1,0:T(8,128)}) custom-call(s32[4]{0:T(128)S(1)} %get-tuple-element.73.refs_0_, f32[8,512,128]{2,1,0:T(8,128)S(1)} %get-tuple-element.137.refs_1_, f32[2,1,512,128]{3,2,1,0:T(8,128)S(1)} %collective-permute-done.32.refs_2_, f32[1,1,512,128]{3,2,1,0:T(8,128)S(1)} %collective-permute-done.33.refs_3_, ...), custom_call_target="tpu_custom_call" | custom-call | tf_op jit(solution)/shard_map/add_late/pallas_call | solution.py:96
  (46 shorter events, 0.3 us)
Async XLA Ops:
  0.0 7.2 %collective-permute-start = (f32[8,512,128]{2,1,0:T(8,128)}, f32[8,512,128]{2,1,0:T(8,128)S(1)}, u32[]{:S(2)}, u32[]{:S(2)}) collective-permute-start(f32[8,512,128]{2,1,0:T(8,128)} %bitcast.10), channel_id=1, source_target_pairs={{0,1},{1,0},{2,3},{3,2},{4,5},{5,4},{6,7},{7,6},{8,9},{9,8},{10,11... | collective-permute-start | bytes 6291464 | tf_op jit(solution)/shard_map/ppermute | solution.py:453
  7.2 1.6 copy-start.1
  8.8 9.2 %copy-start.2 = (f32[8,4,16384]{2,1,0:T(4,128)S(1)}, f32[8,4,16384]{2,1,0:T(4,128)}, u32[]{:S(2)}) copy-start(f32[8,4,16384]{2,1,0:T(4,128)} %param.9) | copy-start | bytes 6291460
  10.3 24.5 %collective-permute-start.2 = (f32[2,2,512,128]{3,2,1,0:T(8,128)S(1)}, f32[2,2,512,128]{3,2,1,0:T(8,128)S(1)}, u32[]{:S(2)}, u32[]{:S(2)}) collective-permute-start(f32[2,2,512,128]{3,2,1,0:T(8,128)S(1)} %get-tuple-element.77), channel_id=1, source_target_pairs={{0,192},{1,193},{2,194},{3,195},{4,196},{5,197},{6,198},{7,199},{8... | collective-permute-start | bytes 3145736 | tf_op jit(solution)/shard_map/ppermute | solution.py:453
  11.1 43.1 %collective-permute-start.1 = (f32[2,2,512,128]{3,2,1,0:T(8,128)S(1)}, f32[2,2,512,128]{3,2,1,0:T(8,128)S(1)}, u32[]{:S(2)}, u32[]{:S(2)}) collective-permute-start(f32[2,2,512,128]{3,2,1,0:T(8,128)S(1)} %get-tuple-element.76), channel_id=1, source_target_pairs={{0,32},{1,33},{2,34},{3,35},{4,36},{5,37},{6,38},{7,39},{8,40},{9,... | collective-permute-start | bytes 3145736 | tf_op jit(solution)/shard_map/ppermute | solution.py:453
  18.0 16.7 %copy-start.4 = (bf16[256,256]{1,0:T(8,128)(2,1)S(1)}, bf16[256,256]{1,0:T(8,128)(2,1)}, u32[]{:S(2)}) copy-start(bf16[256,256]{1,0:T(8,128)(2,1)} %constant.14.clone.refs_2_.refs_7_) | copy-start | bytes 393220
  18.0 16.7 %copy-start.5 = (bf16[256,256]{1,0:T(8,128)(2,1)S(1)}, bf16[256,256]{1,0:T(8,128)(2,1)}, u32[]{:S(2)}) copy-start(bf16[256,256]{1,0:T(8,128)(2,1)} %constant.15.clone.refs_3_.refs_8_) | copy-start | bytes 393220
  18.0 16.7 %copy-start.6 = (f32[128,128]{1,0:T(8,128)S(1)}, f32[128,128]{1,0:T(8,128)}, u32[]{:S(2)}) copy-start(f32[128,128]{1,0:T(8,128)} %constant.16.clone.refs_4_.refs_9_) | copy-start | bytes 196612
  18.1 16.7 %copy-start.7 = (f32[128,128]{1,0:T(8,128)S(1)}, f32[128,128]{1,0:T(8,128)}, u32[]{:S(2)}) copy-start(f32[128,128]{1,0:T(8,128)} %constant.17.clone.refs_5_) | copy-start | bytes 196612
  34.8 18.9 %copy-start = (f32[4,128,128]{2,1,0:T(8,128)S(1)}, f32[4,128,128]{2,1,0:T(8,128)}, u32[]{:S(2)}) copy-start(f32[4,128,128]{2,1,0:T(8,128)} %constant.18.clone.refs_4_.refs_7_) | copy-start | bytes 786436
  38.8 8.2 %collective-permute-start.3 = (f32[520,128]{1,0:T(8,128)S(1)}, f32[520,128]{1,0:T(8,128)S(1)}, u32[]{:S(2)}, u32[]{:S(2)}) collective-permute-start(f32[520,128]{1,0:T(8,128)S(1)} %get-tuple-element.80), channel_id=1, source_target_pairs={{0,2},{1,3},{2,4},{3,5},{4,6},{5,7},{6,0},{7,1},{8,10},{9,11},{10,... | collective-permute-start | bytes 798728 | tf_op jit(solution)/shard_map/ppermute | solution.py:453
  38.9 13.4 %collective-permute-start.4 = (f32[520,128]{1,0:T(8,128)S(1)}, f32[520,128]{1,0:T(8,128)S(1)}, u32[]{:S(2)}, u32[]{:S(2)}) collective-permute-start(f32[520,128]{1,0:T(8,128)S(1)} %get-tuple-element.81), channel_id=1, source_target_pairs={{0,4},{1,5},{2,6},{3,7},{4,0},{5,1},{6,2},{7,3},{8,12},{9,13},{10,... | collective-permute-start | bytes 798728 | tf_op jit(solution)/shard_map/ppermute | solution.py:453
  41.4 12.3 %collective-permute-start.5 = (f32[520,128]{1,0:T(8,128)S(1)}, f32[520,128]{1,0:T(8,128)S(1)}, u32[]{:S(2)}, u32[]{:S(2)}) collective-permute-start(f32[520,128]{1,0:T(8,128)S(1)} %get-tuple-element.82), channel_id=1, source_target_pairs={{0,6},{1,7},{2,0},{3,1},{4,2},{5,3},{6,4},{7,5},{8,14},{9,15},{10,... | collective-permute-start | bytes 798728 | tf_op jit(solution)/shard_map/ppermute | solution.py:453
  53.8 15.8 %collective-permute-start.6 = (f32[520,128]{1,0:T(8,128)S(1)}, f32[520,128]{1,0:T(8,128)S(1)}, u32[]{:S(2)}, u32[]{:S(2)}) collective-permute-start(f32[520,128]{1,0:T(8,128)S(1)} %get-tuple-element.84.refs_0_), channel_id=1, source_target_pairs={{0,8},{1,9},{2,10},{3,11},{4,12},{5,13},{6,14},{7,15},{8,0},{9,1},... | collective-permute-start | bytes 798728 | tf_op jit(solution)/shard_map/ppermute | solution.py:453
  54.2 15.4 %copy-start.3 = (f32[3,128,128]{2,1,0:T(8,128)S(1)}, f32[3,128,128]{2,1,0:T(8,128)}, u32[]{:S(2)}) copy-start(f32[3,128,128]{2,1,0:T(8,128)} %constant.19.clone.refs_2_.refs_8_) | copy-start | bytes 589828
  56.2 20.4 %collective-permute-start.10 = (f32[264,128]{1,0:T(8,128)S(1)}, f32[264,128]{1,0:T(8,128)S(1)}, u32[]{:S(2)}, u32[]{:S(2)}) collective-permute-start(f32[264,128]{1,0:T(8,128)S(1)} %get-tuple-element.94), channel_id=1, source_target_pairs={{0,2},{1,3},{2,4},{3,5},{4,6},{5,7},{6,0},{7,1},{8,10},{9,11},{10,... | collective-permute-start | bytes 405512 | tf_op jit(solution)/shard_map/ppermute | solution.py:453
  58.1 19.4 %collective-permute-start.11 = (f32[264,128]{1,0:T(8,128)S(1)}, f32[264,128]{1,0:T(8,128)S(1)}, u32[]{:S(2)}, u32[]{:S(2)}) collective-permute-start(f32[264,128]{1,0:T(8,128)S(1)} %get-tuple-element.95), channel_id=1, source_target_pairs={{0,4},{1,5},{2,6},{3,7},{4,0},{5,1},{6,2},{7,3},{8,12},{9,13},{10,... | collective-permute-start | bytes 405512 | tf_op jit(solution)/shard_map/ppermute | solution.py:453
  60.9 18.3 %collective-permute-start.12 = (f32[264,128]{1,0:T(8,128)S(1)}, f32[264,128]{1,0:T(8,128)S(1)}, u32[]{:S(2)}, u32[]{:S(2)}) collective-permute-start(f32[264,128]{1,0:T(8,128)S(1)} %get-tuple-element.96), channel_id=1, source_target_pairs={{0,6},{1,7},{2,0},{3,1},{4,2},{5,3},{6,4},{7,5},{8,14},{9,15},{10,... | collective-permute-start | bytes 405512 | tf_op jit(solution)/shard_map/ppermute | solution.py:453
  69.7 15.6 %collective-permute-start.15 = (f32[520,128]{1,0:T(8,128)S(1)}, f32[520,128]{1,0:T(8,128)S(1)}, u32[]{:S(2)}, u32[]{:S(2)}) collective-permute-start(f32[520,128]{1,0:T(8,128)S(1)} %get-tuple-element.101.refs_5_), channel_id=1, source_target_pairs={{0,16},{1,17},{2,18},{3,19},{4,20},{5,21},{6,22},{7,23},{8,24},{9,... | collective-permute-start | bytes 798728 | tf_op jit(solution)/shard_map/ppermute | solution.py:453
  76.2 6.0 %collective-permute-start.7 = (f32[264,128]{1,0:T(8,128)S(1)}, f32[264,128]{1,0:T(8,128)S(1)}, u32[]{:S(2)}, u32[]{:S(2)}) collective-permute-start(f32[264,128]{1,0:T(8,128)S(1)} %get-tuple-element.90), channel_id=1, source_target_pairs={{0,2},{1,3},{2,4},{3,5},{4,6},{5,7},{6,0},{7,1},{8,10},{9,11},{10,... | collective-permute-start | bytes 405512 | tf_op jit(solution)/shard_map/ppermute | solution.py:453
  76.7 7.0 %collective-permute-start.8 = (f32[264,128]{1,0:T(8,128)S(1)}, f32[264,128]{1,0:T(8,128)S(1)}, u32[]{:S(2)}, u32[]{:S(2)}) collective-permute-start(f32[264,128]{1,0:T(8,128)S(1)} %get-tuple-element.91), channel_id=1, source_target_pairs={{0,4},{1,5},{2,6},{3,7},{4,0},{5,1},{6,2},{7,3},{8,12},{9,13},{10,... | collective-permute-start | bytes 405512 | tf_op jit(solution)/shard_map/ppermute | solution.py:453
  77.5 6.6 %collective-permute-start.9 = (f32[264,128]{1,0:T(8,128)S(1)}, f32[264,128]{1,0:T(8,128)S(1)}, u32[]{:S(2)}, u32[]{:S(2)}) collective-permute-start(f32[264,128]{1,0:T(8,128)S(1)} %get-tuple-element.92), channel_id=1, source_target_pairs={{0,6},{1,7},{2,0},{3,1},{4,2},{5,3},{6,4},{7,5},{8,14},{9,15},{10,... | collective-permute-start | bytes 405512 | tf_op jit(solution)/shard_map/ppermute | solution.py:453
  79.2 7.8 %collective-permute-start.14 = (f32[264,128]{1,0:T(8,128)S(1)}, f32[264,128]{1,0:T(8,128)S(1)}, u32[]{:S(2)}, u32[]{:S(2)}) collective-permute-start(f32[264,128]{1,0:T(8,128)S(1)} %get-tuple-element.100.refs_0_), channel_id=1, source_target_pairs={{0,8},{1,9},{2,10},{3,11},{4,12},{5,13},{6,14},{7,15},{8,0},{9,1},... | collective-permute-start | bytes 405512 | tf_op jit(solution)/shard_map/ppermute | solution.py:453
  84.1 8.1 %collective-permute-start.13 = (f32[264,128]{1,0:T(8,128)S(1)}, f32[264,128]{1,0:T(8,128)S(1)}, u32[]{:S(2)}, u32[]{:S(2)}) collective-permute-start(f32[264,128]{1,0:T(8,128)S(1)} %get-tuple-element.99.refs_0_), channel_id=1, source_target_pairs={{0,8},{1,9},{2,10},{3,11},{4,12},{5,13},{6,14},{7,15},{8,0},{9,1},... | collective-permute-start | bytes 405512 | tf_op jit(solution)/shard_map/ppermute | solution.py:453
  85.3 21.0 %copy-start.8 = (f32[1,128]{1,0:T(1,128)S(1)}, f32[1,128]{1,0:T(1,128)}, u32[]{:S(2)}) copy-start(f32[1,128]{1,0:T(1,128)} %constant.20.clone.refs_10_) | copy-start | bytes 1540
  87.1 6.4 %collective-permute-start.20 = (f32[264,128]{1,0:T(8,128)S(1)}, f32[264,128]{1,0:T(8,128)S(1)}, u32[]{:S(2)}, u32[]{:S(2)}) collective-permute-start(f32[264,128]{1,0:T(8,128)S(1)} %get-tuple-element.111.refs_5_), channel_id=1, source_target_pairs={{0,16},{1,17},{2,18},{3,19},{4,20},{5,21},{6,22},{7,23},{8,24},{9,... | collective-permute-start | bytes 405512 | tf_op jit(solution)/shard_map/ppermute | solution.py:453
  88.7 8.0 %collective-permute-start.17 = (f32[520,128]{1,0:T(8,128)S(1)}, f32[520,128]{1,0:T(8,128)S(1)}, u32[]{:S(2)}, u32[]{:S(2)}) collective-permute-start(f32[520,128]{1,0:T(8,128)S(1)} %get-tuple-element.108), channel_id=1, source_target_pairs={{0,6},{1,7},{2,0},{3,1},{4,2},{5,3},{6,4},{7,5},{8,14},{9,15},{10,... | collective-permute-start | bytes 798728 | tf_op jit(solution)/shard_map/ppermute | solution.py:453
  90.5 7.1 %collective-permute-start.18 = (f32[520,128]{1,0:T(8,128)S(1)}, f32[520,128]{1,0:T(8,128)S(1)}, u32[]{:S(2)}, u32[]{:S(2)}) collective-permute-start(f32[520,128]{1,0:T(8,128)S(1)} %get-tuple-element.109), channel_id=1, source_target_pairs={{0,4},{1,5},{2,6},{3,7},{4,0},{5,1},{6,2},{7,3},{8,12},{9,13},{10,... | collective-permute-start | bytes 798728 | tf_op jit(solution)/shard_map/ppermute | solution.py:453
  91.3 14.9 %collective-permute-start.19 = (f32[520,128]{1,0:T(8,128)S(1)}, f32[520,128]{1,0:T(8,128)S(1)}, u32[]{:S(2)}, u32[]{:S(2)}) collective-permute-start(f32[520,128]{1,0:T(8,128)S(1)} %get-tuple-element.110), channel_id=1, source_target_pairs={{0,2},{1,3},{2,4},{3,5},{4,6},{5,7},{6,0},{7,1},{8,10},{9,11},{10,... | collective-permute-start | bytes 798728 | tf_op jit(solution)/shard_map/ppermute | solution.py:453
  92.2 18.3 %collective-permute-start.16 = (f32[264,128]{1,0:T(8,128)S(1)}, f32[264,128]{1,0:T(8,128)S(1)}, u32[]{:S(2)}, u32[]{:S(2)}) collective-permute-start(f32[264,128]{1,0:T(8,128)S(1)} %get-tuple-element.105.refs_5_), channel_id=1, source_target_pairs={{0,16},{1,17},{2,18},{3,19},{4,20},{5,21},{6,22},{7,23},{8,24},{9,... | collective-permute-start | bytes 405512 | tf_op jit(solution)/shard_map/ppermute | solution.py:453
  93.7 17.9 %collective-permute-start.24 = (f32[264,128]{1,0:T(8,128)S(1)}, f32[264,128]{1,0:T(8,128)S(1)}, u32[]{:S(2)}, u32[]{:S(2)}) collective-permute-start(f32[264,128]{1,0:T(8,128)S(1)} %get-tuple-element.121), channel_id=1, source_target_pairs={{0,6},{1,7},{2,0},{3,1},{4,2},{5,3},{6,4},{7,5},{8,14},{9,15},{10,... | collective-permute-start | bytes 405512 | tf_op jit(solution)/shard_map/ppermute | solution.py:453
  96.7 15.6 %collective-permute-start.25 = (f32[264,128]{1,0:T(8,128)S(1)}, f32[264,128]{1,0:T(8,128)S(1)}, u32[]{:S(2)}, u32[]{:S(2)}) collective-permute-start(f32[264,128]{1,0:T(8,128)S(1)} %get-tuple-element.122), channel_id=1, source_target_pairs={{0,4},{1,5},{2,6},{3,7},{4,0},{5,1},{6,2},{7,3},{8,12},{9,13},{10,... | collective-permute-start | bytes 405512 | tf_op jit(solution)/shard_map/ppermute | solution.py:453
  97.6 14.8 %collective-permute-start.26 = (f32[264,128]{1,0:T(8,128)S(1)}, f32[264,128]{1,0:T(8,128)S(1)}, u32[]{:S(2)}, u32[]{:S(2)}) collective-permute-start(f32[264,128]{1,0:T(8,128)S(1)} %get-tuple-element.123), channel_id=1, source_target_pairs={{0,2},{1,3},{2,4},{3,5},{4,6},{5,7},{6,0},{7,1},{8,10},{9,11},{10,... | collective-permute-start | bytes 405512 | tf_op jit(solution)/shard_map/ppermute | solution.py:453
  110.7 9.3 %collective-permute-start.21 = (f32[264,128]{1,0:T(8,128)S(1)}, f32[264,128]{1,0:T(8,128)S(1)}, u32[]{:S(2)}, u32[]{:S(2)}) collective-permute-start(f32[264,128]{1,0:T(8,128)S(1)} %get-tuple-element.116), channel_id=1, source_target_pairs={{0,6},{1,7},{2,0},{3,1},{4,2},{5,3},{6,4},{7,5},{8,14},{9,15},{10,... | collective-permute-start | bytes 405512 | tf_op jit(solution)/shard_map/ppermute | solution.py:453
  110.8 9.2 %collective-permute-start.22 = (f32[264,128]{1,0:T(8,128)S(1)}, f32[264,128]{1,0:T(8,128)S(1)}, u32[]{:S(2)}, u32[]{:S(2)}) collective-permute-start(f32[264,128]{1,0:T(8,128)S(1)} %get-tuple-element.117), channel_id=1, source_target_pairs={{0,4},{1,5},{2,6},{3,7},{4,0},{5,1},{6,2},{7,3},{8,12},{9,13},{10,... | collective-permute-start | bytes 405512 | tf_op jit(solution)/shard_map/ppermute | solution.py:453
  111.6 8.4 %collective-permute-start.23 = (f32[264,128]{1,0:T(8,128)S(1)}, f32[264,128]{1,0:T(8,128)S(1)}, u32[]{:S(2)}, u32[]{:S(2)}) collective-permute-start(f32[264,128]{1,0:T(8,128)S(1)} %get-tuple-element.118), channel_id=1, source_target_pairs={{0,2},{1,3},{2,4},{3,5},{4,6},{5,7},{6,0},{7,1},{8,10},{9,11},{10,... | collective-permute-start | bytes 405512 | tf_op jit(solution)/shard_map/ppermute | solution.py:453
  114.4 15.8 %collective-permute-start.30 = (f32[2,1,512,128]{3,2,1,0:T(8,128)S(1)}, f32[2,1,512,128]{3,2,1,0:T(8,128)S(1)}, u32[]{:S(2)}, u32[]{:S(2)}) collective-permute-start(f32[2,1,512,128]{3,2,1,0:T(8,128)S(1)} %get-tuple-element.135), channel_id=1, source_target_pairs={{0,224},{1,225},{2,226},{3,227},{4,228},{5,229},{6,230},{7,231},{8... | collective-permute-start | bytes 1572872 | tf_op jit(solution)/shard_map/ppermute | solution.py:453
  122.1 21.4 %collective-permute-start.32 = (f32[2,1,512,128]{3,2,1,0:T(8,128)S(1)}, f32[2,1,512,128]{3,2,1,0:T(8,128)S(1)}, u32[]{:S(2)}, u32[]{:S(2)}) collective-permute-start(f32[2,1,512,128]{3,2,1,0:T(8,128)S(1)} %get-tuple-element.138), channel_id=1, source_target_pairs={{0,224},{1,225},{2,226},{3,227},{4,228},{5,229},{6,230},{7,231},{8... | collective-permute-start | bytes 1572872 | tf_op jit(solution)/shard_map/ppermute | solution.py:453
  126.1 40.5 %collective-permute-start.28 = (f32[1,2,512,128]{3,2,1,0:T(8,128)S(1)}, f32[1,2,512,128]{3,2,1,0:T(8,128)S(1)}, u32[]{:S(2)}, u32[]{:S(2)}) collective-permute-start(f32[1,2,512,128]{3,2,1,0:T(8,128)S(1)} %get-tuple-element.142), channel_id=1, source_target_pairs={{0,64},{1,65},{2,66},{3,67},{4,68},{5,69},{6,70},{7,71},{8,72},{9,... | collective-permute-start | bytes 1572872 | tf_op jit(solution)/shard_map/ppermute | solution.py:453
  126.2 40.4 %collective-permute-start.29 = (f32[1,2,512,128]{3,2,1,0:T(8,128)S(1)}, f32[1,2,512,128]{3,2,1,0:T(8,128)S(1)}, u32[]{:S(2)}, u32[]{:S(2)}) collective-permute-start(f32[1,2,512,128]{3,2,1,0:T(8,128)S(1)} %get-tuple-element.141), channel_id=1, source_target_pairs={{0,65},{1,64},{2,67},{3,66},{4,69},{5,68},{6,71},{7,70},{8,73},{9,... | collective-permute-start | bytes 1572872 | tf_op jit(solution)/shard_map/ppermute | solution.py:453
  129.6 37.0 %collective-permute-start.27 = (f32[8,512,128]{2,1,0:T(8,128)S(1)}, f32[8,512,128]{2,1,0:T(8,128)S(1)}, u32[]{:S(2)}, u32[]{:S(2)}) collective-permute-start(f32[8,512,128]{2,1,0:T(8,128)S(1)} %get-tuple-element.133), channel_id=1, source_target_pairs={{0,1},{1,0},{2,3},{3,2},{4,5},{5,4},{6,7},{7,6},{8,9},{9,8},{10,11... | collective-permute-start | bytes 6291464 | tf_op jit(solution)/shard_map/ppermute | solution.py:453
  130.2 36.4 %collective-permute-start.31 = (f32[1,1,512,128]{3,2,1,0:T(8,128)S(1)}, f32[1,1,512,128]{3,2,1,0:T(8,128)S(1)}, u32[]{:S(2)}, u32[]{:S(2)}) collective-permute-start(f32[1,1,512,128]{3,2,1,0:T(8,128)S(1)} %slice.16), channel_id=1, source_target_pairs={{0,1},{1,0},{2,3},{3,2},{4,5},{5,4},{6,7},{7,6},{8,9},{9,8},{10,11... | collective-permute-start | bytes 786440 | tf_op jit(solution)/shard_map/ppermute | solution.py:453
  143.5 24.3 %collective-permute-start.33 = (f32[1,1,512,128]{3,2,1,0:T(8,128)S(1)}, f32[1,1,512,128]{3,2,1,0:T(8,128)S(1)}, u32[]{:S(2)}, u32[]{:S(2)}) collective-permute-start(f32[1,1,512,128]{3,2,1,0:T(8,128)S(1)} %slice.17), channel_id=1, source_target_pairs={{0,1},{1,0},{2,3},{3,2},{4,5},{5,4},{6,7},{7,6},{8,9},{9,8},{10,11... | collective-permute-start | bytes 786440 | tf_op jit(solution)/shard_map/ppermute | solution.py:453
